TPU v7x, 256 devices: a whole 4x4x8 slice. The times are simulated.
256 devices in a mesh: grp: 8 (over z), shard: 32 (over x, y, core).
Axes of the slice: x: 4, y: 4, z: 8, core: 2. Of those that a mesh axis runs over, the one named last changes fastest.
Arguments:
- values: bfloat16 [32768, 2048], P(('grp', 'shard')), may hold values from -6 to 6
- state_input: float32 [32768, 64], P(('grp', 'shard')), may hold values from -0.0625 to 0.0625
- state_output: float32 [32768, 64], P(('grp', 'shard')), may hold values from -6 to 6
- log_decay: float32 [32768, 32], P(('grp', 'shard')), may hold values from -1 to 0, as said below
- level_lam: float32 [32768, 256], P(('grp', 'shard')), may hold values from 0.2 to 2
- level_ids: int32 [256, 8], P(('grp', 'shard')), may hold values from 0 to 7
- upstream: bfloat16 [32768, 2048], P(('grp', 'shard')), may hold values from -6 to 6
- final_upstream: float32 [32, 64, 64], replicated, may hold values from -6 to 6
Outputs:
- values_grad: bfloat16 [32768, 2048], P(('grp', 'shard'))
- input_grad: float32 [32768, 64], P(('grp', 'shard'))
- output_grad: float32 [32768, 64], P(('grp', 'shard'))
- decay_grad: float32 [32768, 32], P(('grp', 'shard'))
- lambda_grad: float32 [32768, 256], P(('grp', 'shard'))
Inputs may be any that keep to these rules, and one draw needn't show every extreme that they name: `log_decay`: every log decay is negative.
All inputs are finite; a program needn't handle non-finite values.
Results may differ from a plain program's by a relative error of at most 0.018.
Values sent between devices are 32-bit elements; how exact they have to be, the bound alone decides.
A program may use at most 128 MiB of HBM per device.

v0:
```python
from functools import partial

import jax
import jax.numpy as jnp
from jax import lax
from jax.sharding import PartitionSpec as P

highest = lax.Precision.HIGHEST


def swapped(x, axis, apart):
    return lax.ppermute(x, axis, [(i, i ^ 1 << apart) for i in range(lax.axis_size(axis))])


def stretch_state(values, state_input, log_decay):
    cumlog = jnp.cumsum(log_decay, axis=0)
    tail_decay = jnp.exp(cumlog[-1][None, :] - cumlog)
    decayed = (values * tail_decay[:, :, None]).astype(jnp.bfloat16)
    stretch_sum = jnp.einsum(
        "tn,thp->hnp", state_input.astype(jnp.bfloat16), decayed, preferred_element_type=jnp.float32
    )
    return (stretch_sum, jnp.exp(cumlog[-1]))


def intra_output(values, state_input, state_output, log_decay):
    tok_count, head_count, head_dim = values.shape
    head_block = min(16, head_count)
    group_count = head_count // head_block
    cumlog = jnp.cumsum(log_decay, axis=0)
    scores = jnp.dot(state_output, state_input.T, precision=highest)
    causal = jnp.arange(tok_count)[:, None] >= jnp.arange(tok_count)[None, :]
    value_groups = values.reshape(tok_count, group_count, head_block, head_dim).transpose(
        1, 0, 2, 3
    )
    cum_groups = cumlog.reshape(tok_count, group_count, head_block).transpose(1, 2, 0)

    def head_group(pair):
        group_values, group_cum = pair
        log_gap = group_cum[:, :, None] - group_cum[:, None, :]
        weighted = (jnp.exp(jnp.where(causal[None], log_gap, -jnp.inf)) * scores[None]).astype(
            jnp.bfloat16
        )
        return jnp.einsum(
            "hts,shp->thp",
            weighted,
            group_values.astype(jnp.bfloat16),
            preferred_element_type=jnp.float32,
        )

    mixed = lax.map(head_group, (value_groups, cum_groups))
    return mixed.transpose(1, 0, 2, 3).reshape(tok_count, head_count, head_dim)


def inter_output(state_output, log_decay, weights, level_states):
    growth = jnp.exp(jnp.cumsum(log_decay, axis=0))
    out_low = state_output.astype(jnp.bfloat16)
    inter_total = jnp.zeros(
        (state_output.shape[0], level_states.shape[1], level_states.shape[3]), jnp.float32
    )
    for bit_no in range(level_states.shape[0]):
        read_out = jnp.einsum(
            "tn,hnp->thp",
            out_low,
            level_states[bit_no].astype(jnp.bfloat16),
            preferred_element_type=jnp.float32,
        )
        inter_total = inter_total + (growth * weights[:, bit_no])[:, :, None] * read_out
    return inter_total


def level_weights(level_lam, id_row, bit_count):
    head_count = level_lam.shape[1] // id_row.shape[0]
    table = level_lam.reshape(level_lam.shape[0], id_row.shape[0], head_count)
    onehot = (
        id_row[:bit_count, None] == jnp.arange(id_row.shape[0], dtype=jnp.int32)[None, :]
    ).astype(jnp.float32)
    return jnp.einsum("tlh,bl->tbh", table, onehot, precision=highest)


def level_merge(own_agg, own_decay, own_prefix, far_agg, far_decay, upper_half):
    upper_state = upper_half[..., None, None]
    held_state = upper_state * own_prefix[..., None, None] * far_agg
    merged = upper_state * (own_decay[..., None, None] * far_agg + own_agg) + (
        1.0 - upper_state
    ) * (far_decay[..., None, None] * own_agg + far_agg)
    return (
        held_state,
        merged,
        own_decay * far_decay,
        own_prefix * (upper_half * far_decay + 1.0 - upper_half),
    )


def merge_pull(stored, cotangents):
    own_agg, own_decay, own_prefix, far_agg, far_decay, upper_half = stored
    primal, pull = jax.vjp(
        partial(level_merge, upper_half=upper_half),
        own_agg,
        own_decay,
        own_prefix,
        far_agg,
        far_decay,
    )
    return pull(cotangents)


def body(
    values, state_input, state_output, log_decay, level_lam, level_ids, upstream, final_upstream
):
    low_bits = lax.axis_size("shard").bit_length() - 1
    high_bits = lax.axis_size("grp").bit_length() - 1
    bit_count = low_bits + high_bits
    stretch_count = lax.axis_size("shard") * lax.axis_size("grp")
    final_share = final_upstream / float(stretch_count)
    shard_pos = lax.axis_index("shard")
    group_pos = lax.axis_index("grp")
    tok_count = values.shape[0]
    head_count = log_decay.shape[1]
    head_dim = values.shape[1] // head_count
    values32 = values.astype(jnp.float32).reshape(tok_count, head_count, head_dim)
    state_result, state_pull = jax.vjp(stretch_state, values32, state_input, log_decay)
    block_agg, block_decay = state_result
    prefix = jnp.ones((head_count,), jnp.float32)
    held_list = []
    stored_low = []
    for bit_no in range(low_bits):
        far_agg, far_decay = swapped((block_agg, block_decay), "shard", bit_no)
        upper_half = (shard_pos >> bit_no & 1).astype(jnp.float32)
        stored_low.append((block_agg, block_decay, prefix, far_agg, far_decay, upper_half))
        held_state, block_agg, block_decay, prefix = level_merge(
            block_agg, block_decay, prefix, far_agg, far_decay, upper_half
        )
        held_list.append(held_state)
    stored_high = []
    for bit_no in range(high_bits):
        far_agg, far_decay = swapped((block_agg, block_decay), "grp", bit_no)
        upper_half = (group_pos >> bit_no & 1).astype(jnp.float32)
        stored_high.append((block_agg, block_decay, prefix, far_agg, far_decay, upper_half))
        held_state, block_agg, block_decay, prefix = level_merge(
            block_agg, block_decay, prefix, far_agg, far_decay, upper_half
        )
        held_list.append(held_state)
    level_states = jnp.stack(held_list, axis=0)

    def output_fn(values32, state_input, state_output, log_decay, level_lam, level_states):
        weights = level_weights(level_lam, level_ids[0], bit_count)
        return intra_output(values32, state_input, state_output, log_decay) + inter_output(
            state_output, log_decay, weights, level_states
        )

    primal, out_pull = jax.vjp(
        output_fn, values32, state_input, state_output, log_decay, level_lam, level_states
    )
    grad_vals, grad_in, grad_outmap, grad_decay, grad_lam, grad_states = out_pull(
        upstream.astype(jnp.float32).reshape(tok_count, head_count, head_dim)
    )
    agg_grad = final_share
    dec_grad = jnp.zeros_like(block_decay)
    pre_grad = jnp.zeros_like(prefix)
    for bit_no in reversed(range(high_bits)):
        own_agg_g, own_dec_g, own_pre_g, far_agg_g, far_dec_g = merge_pull(
            stored_high[bit_no], (grad_states[low_bits + bit_no], agg_grad, dec_grad, pre_grad)
        )
        back_agg, back_decay = swapped((far_agg_g, far_dec_g), "grp", bit_no)
        agg_grad = own_agg_g + back_agg
        dec_grad = own_dec_g + back_decay
        pre_grad = own_pre_g
    for bit_no in reversed(range(low_bits)):
        own_agg_g, own_dec_g, own_pre_g, far_agg_g, far_dec_g = merge_pull(
            stored_low[bit_no], (grad_states[bit_no], agg_grad, dec_grad, pre_grad)
        )
        back_agg, back_decay = swapped((far_agg_g, far_dec_g), "shard", bit_no)
        agg_grad = own_agg_g + back_agg
        dec_grad = own_dec_g + back_decay
        pre_grad = own_pre_g
    state_vals, state_in, state_decay = state_pull((agg_grad, dec_grad))
    values_grad = (
        (grad_vals + state_vals).astype(jnp.bfloat16).reshape(tok_count, head_count * head_dim)
    )
    return (values_grad, grad_in + state_in, grad_outmap, grad_decay + state_decay, grad_lam)


def solution(mesh):
    return jax.shard_map(
        body,
        mesh=mesh,
        in_specs=(
            P(("grp", "shard"), None),
            P(("grp", "shard"), None),
            P(("grp", "shard"), None),
            P(("grp", "shard"), None),
            P(("grp", "shard"), None),
            P(("grp", "shard"), None),
            P(("grp", "shard"), None),
            P(),
        ),
        out_specs=(
            P(("grp", "shard"), None),
            P(("grp", "shard"), None),
            P(("grp", "shard"), None),
            P(("grp", "shard"), None),
            P(("grp", "shard"), None),
        ),
        check_vma=False,
    )
```

profile of v0, /device:TPU:1, one launch (start us, length us, event | category | flops | bytes accessed | tf_op | source)
XLA Modules:
  0.0 503.9 jit_solution(1657592018342457322)
XLA Ops:
  4.3 3.3 collective-permute-start.16
  13.8 23.0 %collective-permute-done.1 = f32[32]{0:T(128)S(1)} collective-permute-done((f32[32]{0:T(128)S(1)}, f32[32]{0:T(128)S(1)}, u32[]{:S(2)}, u32[]{:S(2)}) %collective-permute-start.1) | collective-permute-done | bytes 160 | tf_op jit(solution)/shard_map/ppermute | solution.py:12
  43.8 20.7 %collective-permute-done.2 = f32[32]{0:T(128)S(1)} collective-permute-done((f32[32]{0:T(128)S(1)}, f32[32]{0:T(128)S(1)}, u32[]{:S(2)}, u32[]{:S(2)}) %collective-permute-start.2) | collective-permute-done | bytes 160 | tf_op jit(solution)/shard_map/ppermute | solution.py:12
  67.0 10.3 %while.35 = (s32[]{:T(128)}, f32[2,16,128,128]{3,2,1,0:T(8,128)}, bf16[2,16,128,128]{3,2,1,0:T(8,128)(2,1)}, bf16[2,128,16,64]{1,3,2,0:T(8,128)(2,1)}, f32[2,16,...) while((s32[]{:T(128)}, f32[2,16,128,128]{3,2,1,0:T(8,128)}, ...), condition=%wide.region_2.3_spmd.clone, body=%wide.region_1.2_spmd.clone.sunk | while | flops 1572866 | bytes 3817593 | solution.py:50
  79.9 9.8 %collective-permute-done.3 = f32[32]{0:T(128)S(1)} collective-permute-done((f32[32]{0:T(128)S(1)}, f32[32]{0:T(128)S(1)}, u32[]{:S(2)}, u32[]{:S(2)}) %collective-permute-start.3) | collective-permute-done | bytes 160 | tf_op jit(solution)/shard_map/ppermute | solution.py:12
  89.7 2.9 multiply_add_fusion.3
  101.9 14.0 %collective-permute-done.4 = f32[32]{0:T(128)} collective-permute-done((f32[32]{0:T(128)}, f32[32]{0:T(128)}, u32[]{:S(2)}, u32[]{:S(2)}) %collective-permute-start.4) | collective-permute-done | bytes 160 | tf_op jit(solution)/shard_map/ppermute | solution.py:12
  115.9 2.9 multiply_add_fusion.2
  126.2 13.4 %collective-permute-done.5 = f32[32]{0:T(128)} collective-permute-done((f32[32]{0:T(128)}, f32[32]{0:T(128)}, u32[]{:S(2)}, u32[]{:S(2)}) %collective-permute-start.5) | collective-permute-done | bytes 160 | tf_op jit(solution)/shard_map/ppermute | solution.py:12
  139.6 2.9 multiply_add_fusion.1
  154.1 37.0 %collective-permute-done.6 = f32[32]{0:T(128)S(1)} collective-permute-done((f32[32]{0:T(128)S(1)}, f32[32]{0:T(128)S(1)}, u32[]{:S(2)}, u32[]{:S(2)}) %collective-permute-start.6) | collective-permute-done | bytes 160 | tf_op jit(solution)/shard_map/ppermute | solution.py:12
  192.9 5.0 collective-permute-start.23
  197.9 3.5 convert_add_fusion
  201.5 42.0 %collective-permute-done.23 = f32[32,64,64]{1,2,0:T(8,128)S(1)} collective-permute-done((f32[32,64,64]{1,2,0:T(8,128)S(1)}, f32[32,64,64]{1,2,0:T(8,128)S(1)}, u32[]{:S(2)}, u32[]{:S(2)}) %collective-permute-start.23) | collective-permute-done | bytes 524320 | tf_op jit(solution)/shard_map/ppermute | solution.py:12
  243.5 4.8 multiply_reduce_fusion.2
  254.8 9.7 %while.36 = (s32[]{:T(128)}, f32[128,128]{1,0:T(8,128)S(1)}, f32[2,128,16,64]{1,3,2,0:T(8,128)}, f32[2,16,128]{2,1,0:T(8,128)}, f32[2,16,128,128]{3,2,1,0:T(8,12...) while((s32[]{:T(128)}, f32[128,128]{1,0:T(8,128)S(1)}, ...), condition=%wide.region_7.8_spmd.clone, body=%wide.region_3.7_spmd.clone.sunk | while | flops 69353472 | bytes 3271831 | solution.py:50
  264.6 3.2 collective-permute-start.7
  270.0 23.6 %collective-permute-done.7 = f32[32]{0:T(128)S(1)} collective-permute-done((f32[32]{0:T(128)}, f32[32]{0:T(128)S(1)}, u32[]{:S(2)}, u32[]{:S(2)}) %collective-permute-start.7) | collective-permute-done | bytes 160 | tf_op jit(solution)/shard_map/ppermute | solution.py:12
  293.7 2.9 multiply_reduce_fusion.21
  297.6 2.6 multiply_add_fusion.12
  306.0 2.6 collective-permute-start.25
  308.6 38.7 %collective-permute-done.9 = f32[32,64,64]{1,2,0:T(8,128)} collective-permute-done((f32[32,64,64]{1,2,0:T(8,128)}, f32[32,64,64]{1,2,0:T(8,128)}, u32[]{:S(2)}, u32[]{:S(2)}) %collective-permute-start.9) | collective-permute-done | bytes 524320 | tf_op jit(solution)/shard_map/ppermute | solution.py:12
  347.3 3.0 multiply_reduce_fusion.18
  357.9 19.0 %collective-permute-done.10 = f32[32,64,64]{1,2,0:T(8,128)S(1)} collective-permute-done((f32[32,64,64]{1,2,0:T(8,128)S(1)}, f32[32,64,64]{1,2,0:T(8,128)S(1)}, u32[]{:S(2)}, u32[]{:S(2)}) %collective-permute-start.10) | collective-permute-done | bytes 524320 | tf_op jit(solution)/shard_map/ppermute | solution.py:12
  380.8 2.8 collective-permute-start.11
  388.9 16.8 %collective-permute-done.11 = f32[32,64,64]{1,2,0:T(8,128)S(1)} collective-permute-done((f32[32,64,64]{1,2,0:T(8,128)S(1)}, f32[32,64,64]{1,2,0:T(8,128)S(1)}, u32[]{:S(2)}, u32[]{:S(2)}) %collective-permute-start.11) | collective-permute-done | bytes 524320 | tf_op jit(solution)/shard_map/ppermute | solution.py:12
  414.1 17.4 %collective-permute-done.12 = f32[32,64,64]{1,2,0:T(8,128)S(1)} collective-permute-done((f32[32,64,64]{1,2,0:T(8,128)S(1)}, f32[32,64,64]{1,2,0:T(8,128)S(1)}, u32[]{:S(2)}, u32[]{:S(2)}) %collective-permute-start.12) | collective-permute-done | bytes 524320 | tf_op jit(solution)/shard_map/ppermute | solution.py:12
  433.9 3.0 collective-permute-start.13
  439.8 17.2 %collective-permute-done.13 = f32[32,64,64]{1,2,0:T(8,128)S(1)} collective-permute-done((f32[32,64,64]{1,2,0:T(8,128)S(1)}, f32[32,64,64]{1,2,0:T(8,128)S(1)}, u32[]{:S(2)}, u32[]{:S(2)}) %collective-permute-start.13) | collective-permute-done | bytes 524320 | tf_op jit(solution)/shard_map/ppermute | solution.py:12
  464.4 16.6 %collective-permute-done.14 = f32[32,64,64]{1,2,0:T(8,128)S(1)} collective-permute-done((f32[32,64,64]{1,2,0:T(8,128)S(1)}, f32[32,64,64]{1,2,0:T(8,128)S(1)}, u32[]{:S(2)}, u32[]{:S(2)}) %collective-permute-start.14) | collective-permute-done | bytes 524320 | tf_op jit(solution)/shard_map/ppermute | solution.py:12
  483.1 5.1 %collective-permute-start.15 = (f32[32,64,64]{1,2,0:T(8,128)}, f32[32,64,64]{1,2,0:T(8,128)S(1)}, u32[]{:S(2)}, u32[]{:S(2)}) collective-permute-start(f32[32,64,64]{1,2,0:T(8,128)} %fusion.70), channel_id=1, source_target_pairs={{0,1},{1,0},{2,3},{3,2},{4,5},{5,4},{6,7},{7,6},{8,9},{9,8},{10,11... | collective-permute-start | bytes 1572872 | tf_op jit(solution)/shard_map/ppermute | solution.py:12
  494.4 2.7 multiply_reduce_fusion
  (356 shorter events, 139.3 us)
Async XLA Ops:
  4.3 5.6 %collective-permute-start.16 = (f32[32,64,64]{1,2,0:T(8,128)S(1)}, f32[32,64,64]{1,2,0:T(8,128)S(1)}, u32[]{:S(2)}, u32[]{:S(2)}) collective-permute-start(f32[32,64,64]{1,2,0:T(8,128)S(1)} %convolution_bitcast_fusion.8), channel_id=1, source_target_pairs={{0,1},{1,0},{2,3},{3,2},{4,5},{5,4},{6,7},{7,6},{8,9},{9,8},{10,11... | collective-permute-start | bytes 1572872 | tf_op jit(solution)/shard_map/ppermute | solution.py:12
  7.7 2.3 collective-permute-start
  12.2 24.6 %collective-permute-start.17 = (f32[32,64,64]{1,2,0:T(8,128)}, f32[32,64,64]{1,2,0:T(8,128)S(1)}, u32[]{:S(2)}, u32[]{:S(2)}) collective-permute-start(f32[32,64,64]{1,2,0:T(8,128)} %multiply_add_fusion.6), channel_id=1, source_target_pairs={{0,2},{1,3},{2,0},{3,1},{4,6},{5,7},{6,4},{7,5},{8,10},{9,11},{10,... | collective-permute-start | bytes 1572872 | tf_op jit(solution)/shard_map/ppermute | solution.py:12
  12.3 24.6 %collective-permute-start.1 = (f32[32]{0:T(128)S(1)}, f32[32]{0:T(128)S(1)}, u32[]{:S(2)}, u32[]{:S(2)}) collective-permute-start(f32[32]{0:T(128)S(1)} %fusion.139), channel_id=1, source_target_pairs={{0,2},{1,3},{2,0},{3,1},{4,6},{5,7},{6,4},{7,5},{8,10},{9,11},{10,... | collective-permute-start | bytes 392 | tf_op jit(solution)/shard_map/ppermute | solution.py:12
  39.4 25.1 %collective-permute-start.18 = (f32[32,64,64]{1,2,0:T(8,128)}, f32[32,64,64]{1,2,0:T(8,128)S(1)}, u32[]{:S(2)}, u32[]{:S(2)}) collective-permute-start(f32[32,64,64]{1,2,0:T(8,128)} %multiply_add_fusion.5), channel_id=1, source_target_pairs={{0,4},{1,5},{2,6},{3,7},{4,0},{5,1},{6,2},{7,3},{8,12},{9,13},{10,... | collective-permute-start | bytes 1572872 | tf_op jit(solution)/shard_map/ppermute | solution.py:12
  41.9 22.6 %collective-permute-start.2 = (f32[32]{0:T(128)S(1)}, f32[32]{0:T(128)S(1)}, u32[]{:S(2)}, u32[]{:S(2)}) collective-permute-start(f32[32]{0:T(128)S(1)} %mul.1336), channel_id=1, source_target_pairs={{0,4},{1,5},{2,6},{3,7},{4,0},{5,1},{6,2},{7,3},{8,12},{9,13},{10,... | collective-permute-start | bytes 392 | tf_op jit(solution)/shard_map/ppermute | solution.py:12
  67.0 22.7 %collective-permute-start.19 = (f32[32,64,64]{1,2,0:T(8,128)}, f32[32,64,64]{1,2,0:T(8,128)}, u32[]{:S(2)}, u32[]{:S(2)}) collective-permute-start(f32[32,64,64]{1,2,0:T(8,128)} %multiply_add_fusion.4), channel_id=1, source_target_pairs={{0,8},{1,9},{2,10},{3,11},{4,12},{5,13},{6,14},{7,15},{8,0},{9,1},... | collective-permute-start | bytes 1572872 | tf_op jit(solution)/shard_map/ppermute | solution.py:12
  78.4 11.3 %collective-permute-start.3 = (f32[32]{0:T(128)S(1)}, f32[32]{0:T(128)S(1)}, u32[]{:S(2)}, u32[]{:S(2)}) collective-permute-start(f32[32]{0:T(128)S(1)} %mul.1339), channel_id=1, source_target_pairs={{0,8},{1,9},{2,10},{3,11},{4,12},{5,13},{6,14},{7,15},{8,0},{9,1},... | collective-permute-start | bytes 392 | tf_op jit(solution)/shard_map/ppermute | solution.py:12
  92.6 23.3 %collective-permute-start.20 = (f32[32,64,64]{1,2,0:T(8,128)}, f32[32,64,64]{1,2,0:T(8,128)}, u32[]{:S(2)}, u32[]{:S(2)}) collective-permute-start(f32[32,64,64]{1,2,0:T(8,128)} %multiply_add_fusion.3), channel_id=1, source_target_pairs={{0,16},{1,17},{2,18},{3,19},{4,20},{5,21},{6,22},{7,23},{8,24},{9,... | collective-permute-start | bytes 1572872 | tf_op jit(solution)/shard_map/ppermute | solution.py:12
  99.9 16.0 %collective-permute-start.4 = (f32[32]{0:T(128)}, f32[32]{0:T(128)}, u32[]{:S(2)}, u32[]{:S(2)}) collective-permute-start(f32[32]{0:T(128)} %mul.1342), channel_id=1, source_target_pairs={{0,16},{1,17},{2,18},{3,19},{4,20},{5,21},{6,22},{7,23},{8,24},{9,... | collective-permute-start | bytes 392 | tf_op jit(solution)/shard_map/ppermute | solution.py:12
  118.8 20.8 %collective-permute-start.21 = (f32[32,64,64]{1,2,0:T(8,128)}, f32[32,64,64]{1,2,0:T(8,128)}, u32[]{:S(2)}, u32[]{:S(2)}) collective-permute-start(f32[32,64,64]{1,2,0:T(8,128)} %multiply_add_fusion.2), channel_id=1, source_target_pairs={{0,32},{32,0},{64,96},{96,64},{128,160},{160,128},{192,224},{224,1... | collective-permute-start | bytes 1572872 | tf_op jit(solution)/shard_map/ppermute | solution.py:12
  124.3 15.3 %collective-permute-start.5 = (f32[32]{0:T(128)}, f32[32]{0:T(128)}, u32[]{:S(2)}, u32[]{:S(2)}) collective-permute-start(f32[32]{0:T(128)} %mul.1345), channel_id=1, source_target_pairs={{0,32},{32,0},{64,96},{96,64},{128,160},{160,128},{192,224},{224,1... | collective-permute-start | bytes 392 | tf_op jit(solution)/shard_map/ppermute | solution.py:12
  142.5 48.5 %collective-permute-start.22 = (f32[32,64,64]{1,2,0:T(8,128)}, f32[32,64,64]{1,2,0:T(8,128)}, u32[]{:S(2)}, u32[]{:S(2)}) collective-permute-start(f32[32,64,64]{1,2,0:T(8,128)} %multiply_add_fusion.1), channel_id=1, source_target_pairs={{0,64},{32,96},{64,0},{96,32},{128,192},{160,224},{192,128},{224,1... | collective-permute-start | bytes 1572872 | tf_op jit(solution)/shard_map/ppermute | solution.py:12
  153.3 37.7 %collective-permute-start.6 = (f32[32]{0:T(128)S(1)}, f32[32]{0:T(128)S(1)}, u32[]{:S(2)}, u32[]{:S(2)}) collective-permute-start(f32[32]{0:T(128)S(1)} %mul.1348), channel_id=1, source_target_pairs={{0,64},{32,96},{64,0},{96,32},{128,192},{160,224},{192,128},{224,1... | collective-permute-start | bytes 392 | tf_op jit(solution)/shard_map/ppermute | solution.py:12
  192.9 50.6 %collective-permute-start.23 = (f32[32,64,64]{1,2,0:T(8,128)S(1)}, f32[32,64,64]{1,2,0:T(8,128)S(1)}, u32[]{:S(2)}, u32[]{:S(2)}) collective-permute-start(f32[32,64,64]{1,2,0:T(8,128)S(1)} %multiply_add_fusion), channel_id=1, source_target_pairs={{0,128},{32,160},{64,192},{96,224},{128,0},{160,32},{192,64},{224,... | collective-permute-start | bytes 1572872 | tf_op jit(solution)/shard_map/ppermute | solution.py:12
  250.9 42.8 %collective-permute-start.8 = (f32[32,64,64]{1,2,0:T(8,128)}, f32[32,64,64]{1,2,0:T(8,128)}, u32[]{:S(2)}, u32[]{:S(2)}) collective-permute-start(f32[32,64,64]{1,2,0:T(8,128)} %multiply_add_fusion.13), channel_id=1, source_target_pairs={{0,128},{32,160},{64,192},{96,224},{128,0},{160,32},{192,64},{224,... | collective-permute-start | bytes 1572872 | tf_op jit(solution)/shard_map/ppermute | solution.py:12
  264.6 29.1 %collective-permute-start.7 = (f32[32]{0:T(128)}, f32[32]{0:T(128)S(1)}, u32[]{:S(2)}, u32[]{:S(2)}) collective-permute-start(f32[32]{0:T(128)} %copy-done.89), channel_id=1, source_target_pairs={{0,128},{32,160},{64,192},{96,224},{128,0},{160,32},{192,64},{224,... | collective-permute-start | bytes 392 | tf_op jit(solution)/shard_map/ppermute | solution.py:12
  267.8 28.8 %collective-permute-start.24 = (f32[32]{0:T(128)}, f32[32]{0:T(128)S(1)}, u32[]{:S(2)}, u32[]{:S(2)}) collective-permute-start(f32[32]{0:T(128)} %get-tuple-element.478), channel_id=1, source_target_pairs={{0,128},{32,160},{64,192},{96,224},{128,0},{160,32},{192,64},{224,... | collective-permute-start | bytes 392 | tf_op jit(solution)/shard_map/ppermute | solution.py:12
  300.2 47.1 %collective-permute-start.9 = (f32[32,64,64]{1,2,0:T(8,128)}, f32[32,64,64]{1,2,0:T(8,128)}, u32[]{:S(2)}, u32[]{:S(2)}) collective-permute-start(f32[32,64,64]{1,2,0:T(8,128)} %multiply_add_fusion.12), channel_id=1, source_target_pairs={{0,64},{32,96},{64,0},{96,32},{128,192},{160,224},{192,128},{224,1... | collective-permute-start | bytes 1572872 | tf_op jit(solution)/shard_map/ppermute | solution.py:12
  306.0 44.3 %collective-permute-start.25 = (f32[32]{0:T(128)S(1)}, f32[32]{0:T(128)S(1)}, u32[]{:S(2)}, u32[]{:S(2)}) collective-permute-start(f32[32]{0:T(128)S(1)} %get-tuple-element.524), channel_id=1, source_target_pairs={{0,64},{32,96},{64,0},{96,32},{128,192},{160,224},{192,128},{224,1... | collective-permute-start | bytes 392 | tf_op jit(solution)/shard_map/ppermute | solution.py:12
  352.6 24.3 %collective-permute-start.10 = (f32[32,64,64]{1,2,0:T(8,128)S(1)}, f32[32,64,64]{1,2,0:T(8,128)S(1)}, u32[]{:S(2)}, u32[]{:S(2)}) collective-permute-start(f32[32,64,64]{1,2,0:T(8,128)S(1)} %multiply_add_fusion.11), channel_id=1, source_target_pairs={{0,32},{32,0},{64,96},{96,64},{128,160},{160,128},{192,224},{224,1... | collective-permute-start | bytes 1572872 | tf_op jit(solution)/shard_map/ppermute | solution.py:12
  356.6 22.5 %collective-permute-start.26 = (f32[32]{0:T(128)S(1)}, f32[32]{0:T(128)S(1)}, u32[]{:S(2)}, u32[]{:S(2)}) collective-permute-start(f32[32]{0:T(128)S(1)} %get-tuple-element.475), channel_id=1, source_target_pairs={{0,32},{32,0},{64,96},{96,64},{128,160},{160,128},{192,224},{224,1... | collective-permute-start | bytes 392 | tf_op jit(solution)/shard_map/ppermute | solution.py:12
  380.8 24.9 %collective-permute-start.11 = (f32[32,64,64]{1,2,0:T(8,128)S(1)}, f32[32,64,64]{1,2,0:T(8,128)S(1)}, u32[]{:S(2)}, u32[]{:S(2)}) collective-permute-start(f32[32,64,64]{1,2,0:T(8,128)S(1)} %multiply_add_fusion.10), channel_id=1, source_target_pairs={{0,16},{1,17},{2,18},{3,19},{4,20},{5,21},{6,22},{7,23},{8,24},{9,... | collective-permute-start | bytes 1572872 | tf_op jit(solution)/shard_map/ppermute | solution.py:12
  387.0 21.0 %collective-permute-start.27 = (f32[32]{0:T(128)S(1)}, f32[32]{0:T(128)S(1)}, u32[]{:S(2)}, u32[]{:S(2)}) collective-permute-start(f32[32]{0:T(128)S(1)} %get-tuple-element.472), channel_id=1, source_target_pairs={{0,16},{1,17},{2,18},{3,19},{4,20},{5,21},{6,22},{7,23},{8,24},{9,... | collective-permute-start | bytes 392 | tf_op jit(solution)/shard_map/ppermute | solution.py:12
  409.0 22.5 %collective-permute-start.12 = (f32[32,64,64]{1,2,0:T(8,128)S(1)}, f32[32,64,64]{1,2,0:T(8,128)S(1)}, u32[]{:S(2)}, u32[]{:S(2)}) collective-permute-start(f32[32,64,64]{1,2,0:T(8,128)S(1)} %multiply_add_fusion.9), channel_id=1, source_target_pairs={{0,8},{1,9},{2,10},{3,11},{4,12},{5,13},{6,14},{7,15},{8,0},{9,1},... | collective-permute-start | bytes 1572872 | tf_op jit(solution)/shard_map/ppermute | solution.py:12
  412.0 21.4 %collective-permute-start.28 = (f32[32]{0:T(128)S(1)}, f32[32]{0:T(128)S(1)}, u32[]{:S(2)}, u32[]{:S(2)}) collective-permute-start(f32[32]{0:T(128)S(1)} %get-tuple-element.469), channel_id=1, source_target_pairs={{0,8},{1,9},{2,10},{3,11},{4,12},{5,13},{6,14},{7,15},{8,0},{9,1},... | collective-permute-start | bytes 392 | tf_op jit(solution)/shard_map/ppermute | solution.py:12
  433.9 23.0 %collective-permute-start.13 = (f32[32,64,64]{1,2,0:T(8,128)S(1)}, f32[32,64,64]{1,2,0:T(8,128)S(1)}, u32[]{:S(2)}, u32[]{:S(2)}) collective-permute-start(f32[32,64,64]{1,2,0:T(8,128)S(1)} %multiply_add_fusion.8), channel_id=1, source_target_pairs={{0,4},{1,5},{2,6},{3,7},{4,0},{5,1},{6,2},{7,3},{8,12},{9,13},{10,... | collective-permute-start | bytes 1572872 | tf_op jit(solution)/shard_map/ppermute | solution.py:12
  438.5 20.9 %collective-permute-start.29 = (f32[32]{0:T(128)S(1)}, f32[32]{0:T(128)S(1)}, u32[]{:S(2)}, u32[]{:S(2)}) collective-permute-start(f32[32]{0:T(128)S(1)} %get-tuple-element.466), channel_id=1, source_target_pairs={{0,4},{1,5},{2,6},{3,7},{4,0},{5,1},{6,2},{7,3},{8,12},{9,13},{10,... | collective-permute-start | bytes 392 | tf_op jit(solution)/shard_map/ppermute | solution.py:12
  460.4 20.6 %collective-permute-start.14 = (f32[32,64,64]{1,2,0:T(8,128)S(1)}, f32[32,64,64]{1,2,0:T(8,128)S(1)}, u32[]{:S(2)}, u32[]{:S(2)}) collective-permute-start(f32[32,64,64]{1,2,0:T(8,128)S(1)} %multiply_add_fusion.7), channel_id=1, source_target_pairs={{0,2},{1,3},{2,0},{3,1},{4,6},{5,7},{6,4},{7,5},{8,10},{9,11},{10,... | collective-permute-start | bytes 1572872 | tf_op jit(solution)/shard_map/ppermute | solution.py:12
  461.8 30.0 %collective-permute-start.30 = (f32[32]{0:T(128)}, f32[32]{0:T(128)}, u32[]{:S(2)}, u32[]{:S(2)}) collective-permute-start(f32[32]{0:T(128)} %get-tuple-element.464), channel_id=1, source_target_pairs={{0,2},{1,3},{2,0},{3,1},{4,6},{5,7},{6,4},{7,5},{8,10},{9,11},{10,... | collective-permute-start | bytes 392 | tf_op jit(solution)/shard_map/ppermute | solution.py:12
  483.1 11.3 %collective-permute-start.15 = (f32[32,64,64]{1,2,0:T(8,128)}, f32[32,64,64]{1,2,0:T(8,128)S(1)}, u32[]{:S(2)}, u32[]{:S(2)}) collective-permute-start(f32[32,64,64]{1,2,0:T(8,128)} %fusion.70), channel_id=1, source_target_pairs={{0,1},{1,0},{2,3},{3,2},{4,5},{5,4},{6,7},{7,6},{8,9},{9,8},{10,11... | collective-permute-start | bytes 1572872 | tf_op jit(solution)/shard_map/ppermute | solution.py:12
  492.5 1.2 collective-permute-start.31
  (94 other events, 3293.4 us)
where the time goes:
time: 514 us; the launch traced here: 504 us
  waiting for transfers between devices  312 us (61%)
  other arithmetic  72.8 us (14%)
  starting transfers between devices  48.4 us (9%)
  matrix products  46.3 us (9%)
  local copies, waits for them, and re-layouts  22.5 us (4%)
    ppermute x32, waiting for transfers between devices, swapped(): lax.ppermute(x, axis, [(i, i ^ 1 << apart) for i in range(lax.axis_size(a...  312 us
    ppermute x32, starting transfers between devices, swapped(): lax.ppermute(x, axis, [(i, i ^ 1 << apart) for i in range(lax.axis_size(a...  48.4 us
    dot_general x24, matrix products, inter_output(): jnp.einsum('tn,hnp->thp', out_low, level_states[bit_no].astype(jnp.bfloat...  28.6 us
    add x7, other arithmetic, level_merge(): upper_state * (own_decay[..., None, None] * far_agg + own_agg)  16.9 us
    reduce_sum x7, other arithmetic, level_merge(): own_decay[..., None, None] * far_agg + own_agg  15.6 us
    unnamed x195, local copies, waits for them, and re-layouts  11.3 us
  transfers between devices with their start and end apart: 32, of which 16 were waited for; matrix products, arithmetic and copies ran while one was open for 18% of the time, Pallas kernels for 0%

commit v1 on v0

v1 whole, which is shorter than its diff:
```python
from functools import partial

import jax
import jax.numpy as jnp
from jax import lax
from jax.experimental import pallas as pl
from jax.experimental.pallas import tpu as pltpu
from jax.sharding import PartitionSpec as P

highest = lax.Precision.HIGHEST
MESH = pl.DeviceIdType.MESH
F32 = jnp.float32
BF16 = jnp.bfloat16
TOK = 128
VMEM_CAP = 48 * 1024 * 1024


def log2(n):
    return n.bit_length() - 1


def vmem():
    return pl.BlockSpec(memory_space=pltpu.VMEM)


def f32(*shape):
    return jax.ShapeDtypeStruct(shape, F32)


def iota(shape, dim):
    return lax.broadcasted_iota(jnp.int32, shape, dim)


def dot(a, b, **kw):
    return jnp.dot(a, b, preferred_element_type=F32, **kw)


def place():
    group = lax.axis_index("grp")
    me = lax.axis_index("shard")
    return group, me, me // 2, me % 2


def remote(src, dst, send, recv, device):
    return pltpu.make_async_remote_copy(
        src_ref=src, dst_ref=dst, send_sem=send, recv_sem=recv, device_id=device, device_id_type=MESH
    )


def loop(start, stop, fn):
    def step(i, carry):
        fn(i)
        return carry

    lax.fori_loop(start, stop, step, 0)


def enter(group, me, shards, groups):
    barrier = pltpu.get_barrier_semaphore()

    def greet_shard(d):
        pl.semaphore_signal(
            barrier, inc=1, device_id=(group, (me + d) % shards), device_id_type=MESH
        )

    def greet_group(d):
        pl.semaphore_signal(
            barrier, inc=1, device_id=((group + d) % groups, me), device_id_type=MESH
        )

    loop(1, shards, greet_shard)
    loop(1, groups, greet_group)
    pl.semaphore_wait(barrier, shards + groups - 2)


def offsets(chips):
    offs, at, n = [], 0, chips
    while n >= 1:
        offs.append(at)
        at += n
        n //= 2
    return offs


def high_level(group, far, bits):
    level = jnp.int32(0)
    for b in range(1, bits):
        level = jnp.where(group // 2**b != far // 2**b, jnp.int32(b), level)
    return level


def bit_of(x, b):
    return (x // 2**b) % 2 == 1


def state_kernel(v_ref, k_ref, ld_ref, blk_ref, crow_ref, ccol_ref):
    heads = ld_ref.shape[1]
    pairs = heads // 2
    ld = ld_ref[...]
    row = iota((TOK, TOK), 0)
    col = iota((TOK, TOK), 1)
    ccol = dot((row >= col).astype(F32), ld, precision=highest)
    ccol_ref[...] = ccol
    crow = ccol.T
    crow_ref[...] = crow
    last = jnp.broadcast_to(crow[:, TOK - 1 : TOK], (heads, TOK))
    tail = jnp.exp(last - crow)
    whole = jnp.exp(last)
    kt = k_ref[...].T
    half = (col < 64).astype(F32)
    m0 = half.astype(BF16)
    m1 = (1.0 - half).astype(BF16)
    for p in range(pairs):
        k2 = jnp.concatenate(
            [kt * tail[2 * p : 2 * p + 1], kt * tail[2 * p + 1 : 2 * p + 2]], axis=1
        ).astype(BF16)
        vp = v_ref[:, p * 128 : (p + 1) * 128]
        s = dot(k2, jnp.concatenate([vp * m0, vp * m1], axis=0))
        blk_ref[2 * p, 0:4] = s[0:32].reshape(4, 8, 128)
        blk_ref[2 * p + 1, 0:4] = s[32:64].reshape(4, 8, 128)
        dec = half[0:8] * whole[2 * p : 2 * p + 1] + (1.0 - half[0:8]) * whole[2 * p + 1 : 2 * p + 2]
        blk_ref[2 * p, 4] = dec
        blk_ref[2 * p + 1, 4] = dec


def forward_kernel(
    shards,
    groups,
    blk,
    h,
    sib,
    r1,
    nd,
    zb,
    hz,
    stage,
    pin,
    coef,
    sib_sem,
    a_sem,
    z_send,
    z_recv,
    h_send,
    h_recv,
    f_send,
    f_recv,
):
    chips = shards // 2
    nb, nz = log2(chips), log2(groups)
    group, me, chip, core = place()
    mate = me + 1 - 2 * core
    offs = offsets(chips)
    top = offs[nb]
    enter(group, me, shards, groups)

    sib_copy = remote(blk, sib, sib_sem.at[0], sib_sem.at[1], (group, mate))

    @pl.when(core == 0)
    def _():
        sib_copy.start()

    def scatter(d):
        to = (me + d) % shards
        remote(blk.at[to], r1.at[me], a_sem.at[0], a_sem.at[1], (group, to)).start()

    loop(1, shards, scatter)
    r1[me] = blk[me]
    part = r1.at[pl.ds(0, shards - 1)]
    whole = remote(part, part, a_sem.at[0], a_sem.at[1], (group, mate))
    whole.wait_recv()

    for c in range(chips):
        right = r1[2 * c + 1, 4]
        nd[c, 0:4] = right[None] * r1[2 * c, 0:4] + r1[2 * c + 1, 0:4]
        nd[c, 4] = right * r1[2 * c, 4]
    for b in range(1, nb + 1):
        for i in range(chips >> b):
            lo = offs[b - 1] + 2 * i
            right = nd[lo + 1, 4]
            nd[offs[b] + i, 0:4] = right[None] * nd[lo, 0:4] + nd[lo + 1, 0:4]
            nd[offs[b] + i, 4] = right * nd[lo, 4]

    def spread(d):
        to = (group + d) % groups
        remote(nd.at[top], zb.at[group], z_send.at[0], z_recv.at[group], (to, me)).start()

    loop(1, groups, spread)

    for c in range(chips):
        pre = None
        for b in range(nb):
            if (c >> b) & 1:
                left = offs[b] + (c >> b) - 1
                far = nd[left, 0:4]
                stage[c, b] = far if pre is None else pre[None] * far
                pre = nd[left, 4] if pre is None else pre * nd[left, 4]
        pin[c] = jnp.ones((8, 128), F32) if pre is None else pre

    def send_level(lev, to):
        remote(
            stage.at[to, lev],
            h.at[lev, chip, core],
            h_send.at[lev],
            h_recv.at[lev],
            (group, 2 * to + core),
        ).start()

    def send_low(d):
        to = (chip + d) % chips
        for b in range(nb):

            @pl.when(bit_of(to, b))
            def _():
                send_level(b, to)

    loop(1, chips, send_low)
    for b in range(nb):

        @pl.when(bit_of(chip, b))
        def _():
            h[b, chip, core] = stage[chip, b]

    coef[...] = jnp.ones((8, 128), F32)
    hz[...] = jnp.zeros(hz.shape, F32)
    for d in range(1, groups):
        far = group - d

        @pl.when(far >= 0)
        def _():
            slot = zb.at[far]
            remote(slot, slot, z_send.at[0], z_recv.at[far], (group, mate)).wait_recv()
            level = high_level(group, far, nz)
            hz[level] = hz[level] + coef[...][None] * zb[far, 0:4]
            coef[...] = coef[...] * zb[far, 4]

    def stage_high(c):
        for l in range(nz):

            @pl.when(bit_of(group, l))
            def _():
                stage[c, nb + l] = pin[c][None] * hz[l]

    loop(0, chips, stage_high)

    def send_high(d):
        to = (chip + d) % chips
        for l in range(nz):

            @pl.when(bit_of(group, l))
            def _():
                send_level(nb + l, to)

    loop(1, chips, send_high)

    for lev in range(nb + nz):
        mine = bit_of(chip, lev) if lev < nb else bit_of(group, lev - nb)

        @pl.when(mine)
        def _():
            if lev >= nb:
                h[lev, chip, core] = stage[chip, lev]
            arrive = h.at[lev, pl.ds(0, chips - 1), core]
            remote(arrive, arrive, h_send.at[lev], h_recv.at[lev], (group, mate)).wait_recv()
            ours = h.at[lev, :, core]
            remote(ours, ours, f_send.at[lev], f_recv.at[lev], (group, mate)).start()

    for lev in range(nb + nz):
        mine = bit_of(chip, lev) if lev < nb else bit_of(group, lev - nb)

        @pl.when(mine)
        def _():
            theirs = h.at[lev, :, 1 - core]
            ours = remote(theirs, theirs, f_send.at[lev], f_recv.at[lev], (group, mate))
            ours.wait_recv()
            ours.wait_send()

    def sent(lev, count):
        out = stage.at[pl.ds(0, count), lev]
        remote(out, out, h_send.at[lev], h_recv.at[lev], (group, mate)).wait_send()

    for b in range(nb):

        @pl.when(bit_of(chip, b))
        def _():
            if chips // 2 > 1:
                sent(b, chips // 2 - 1)

        @pl.when(jnp.logical_not(bit_of(chip, b)))
        def _():
            sent(b, chips // 2)

    for l in range(nz):

        @pl.when(bit_of(group, l))
        def _():
            sent(nb + l, chips - 1)

    for d in range(1, groups):
        far = group + d

        @pl.when(far < groups)
        def _():
            slot = zb.at[far]
            remote(slot, slot, z_send.at[0], z_recv.at[far], (group, mate)).wait_recv()

    zpart = zb.at[pl.ds(0, groups - 1)]
    remote(zpart, zpart, z_send.at[0], z_recv.at[0], (group, mate)).wait_send()
    whole.wait_send()

    @pl.when(core == 0)
    def _():
        sib_copy.wait_send()

    @pl.when(core == 1)
    def _():
        sib_copy.wait_recv()


def backward_kernel(
    shards,
    groups,
    g,
    r1,
    nd,
    zb,
    hz,
    fu,
    ds,
    g0,
    x,
    st,
    rb,
    u,
    zu,
    ct,
    cown,
    coef,
    dn,
    rt,
    out,
    g0_sem,
    x_send,
    x_recv,
    b_send,
    b_recv,
    z_send,
    z_recv,
    c_send,
    c_recv,
    o_sem,
):
    chips = shards // 2
    nb, nz = log2(chips), log2(groups)
    group, me, chip, core = place()
    mate = me + 1 - 2 * core
    offs = offsets(chips)
    top = offs[nb]
    enter(group, me, shards, groups)

    order = [nb + l for l in range(nz)] + list(range(nb))

    def mine(lev):
        return bit_of(chip, lev) if lev < nb else bit_of(group, lev - nb)

    def swap(lev):
        return remote(
            g.at[lev + 1, :, 1 - core], x.at[lev], x_send.at[lev], x_recv.at[lev], (group, mate)
        )

    for lev in order:

        @pl.when(mine(lev))
        def _():
            swap(lev).start()

    g0_copy = remote(g.at[0], g0, g0_sem.at[0], g0_sem.at[1], (group, mate))

    @pl.when(core == 1)
    def _():
        g0_copy.start()

    for lev in order:

        @pl.when(mine(lev))
        def _():
            swap(lev).wait_recv()

            def add(c):
                st[lev, c] = g[lev + 1, c, core] + x[lev, c]

            loop(0, chips, add)

            def send(d):
                to = (chip + d) % chips
                remote(
                    st.at[lev, to],
                    rb.at[lev, chip],
                    b_send.at[lev],
                    b_recv.at[lev],
                    (group, 2 * to + core),
                ).start()

            loop(1, chips, send)
            rb[lev, chip] = st[lev, chip]

    def arrived(lev, count):
        part = rb.at[lev, pl.ds(0, count)]
        remote(part, part, b_send.at[lev], b_recv.at[lev], (group, mate)).wait_recv()

    pres = []
    pin = []
    for c in range(chips):
        pre = None
        mid = []
        for b in range(nb):
            if (c >> b) & 1:
                mid.append((b, offs[b] + (c >> b) - 1))
        pres.append(mid)

    def pin_of(c):
        pre = None
        for _, left in pres[c]:
            pre = nd[left, 4] if pre is None else pre * nd[left, 4]
        return jnp.ones((8, 128), F32) if pre is None else pre

    rt[...] = jnp.zeros(rt.shape, F32)
    for l in range(nz):

        @pl.when(bit_of(group, l))
        def _():
            arrived(nb + l, chips - 1)
            total = jnp.zeros((4, 8, 128), F32)
            for c in range(chips):
                w = pin_of(c)[None] * rb[nb + l, c]
                total = total + w
                rt[c] = rt[c] + jnp.sum(w * hz[l], axis=0)
            u[l] = total

    for d in range(1, groups):

        @pl.when(group - d >= 0)
        def _():
            level = high_level(group, group - d, nz)
            remote(u.at[level], zu.at[group], z_send.at[d], z_recv.at[group], (group - d, me)).start()

    coef[...] = jnp.ones((8, 128), F32)
    dn[top] = jnp.zeros((4, 8, 128), F32)
    for d in range(1, groups):

        @pl.when(group + d < groups)
        def _():
            slot = zu.at[group + d]
            remote(slot, slot, z_send.at[d], z_recv.at[group + d], (group, mate)).wait_recv()
            dn[top] = dn[top] + coef[...][None] * zu[group + d]
            coef[...] = coef[...] * zb[group + d, 4]

    dn[top] = dn[top] + coef[...][None] * fu[...]
    cown[...] = jnp.sum(nd[top, 0:4] * dn[top], axis=0)
    for l in range(nz):

        @pl.when(bit_of(group, l))
        def _():
            cown[...] = cown[...] - jnp.sum(u[l] * hz[l], axis=0)

    for d in range(1, groups):

        @pl.when(group + d < groups)
        def _():
            remote(cown, ct.at[group], c_send.at[d], c_recv.at[group], (group + d, me)).start()

    for b in range(nb):

        @pl.when(bit_of(chip, b))
        def _():
            if chips // 2 > 1:
                arrived(b, chips // 2 - 1)

        @pl.when(jnp.logical_not(bit_of(chip, b)))
        def _():
            arrived(b, chips // 2)

    for b in range(nb):
        for i in range(0, chips >> b, 2):
            left = offs[b] + i
            total = None
            for c in range((i + 1) << b, (i + 2) << b):
                w = rb[b, c]
                for bb, node in pres[c]:
                    if bb < b:
                        w = nd[node, 4][None] * w
                rt[c] = rt[c] + jnp.sum(w * nd[left, 0:4], axis=0)
                total = w if total is None else total + w
            dn[left] = total
    for b in reversed(range(nb)):
        for i in range(0, chips >> b, 2):
            left = offs[b] + i
            parent = dn[offs[b + 1] + i // 2]
            dn[left] = dn[left] + nd[left + 1, 4][None] * parent
            dn[left + 1] = parent

    carry = jnp.zeros((8, 128), F32)
    for c in range(chips):
        right = dn[c]
        left = r1[2 * c + 1, 4][None] * right
        out[2 * c, 0:4] = left
        out[2 * c + 1, 0:4] = right
        l0 = jnp.sum(r1[2 * c, 0:4] * left, axis=0)
        l1 = jnp.sum(r1[2 * c + 1, 0:4] * right, axis=0)
        out[2 * c, 4] = carry
        odd = carry + l0 - rt[c]
        out[2 * c + 1, 4] = odd
        carry = odd + l1

    coef[...] = jnp.zeros((8, 128), F32)
    for d in range(1, groups):

        @pl.when(group - d >= 0)
        def _():
            slot = ct.at[group - d]
            remote(slot, slot, c_send.at[d], c_recv.at[group - d], (group, mate)).wait_recv()
            coef[...] = coef[...] + ct[group - d]

    def carry_in(s):
        out[s, 4] = out[s, 4] + coef[...]

    loop(0, shards, carry_in)

    def give(d):
        to = (me + d) % shards
        remote(out.at[to], ds.at[me], o_sem.at[0], o_sem.at[1], (group, to)).start()

    loop(1, shards, give)
    ds[me] = out[me]

    for lev in range(nb + nz):

        @pl.when(mine(lev))
        def _():
            swap(lev).wait_send()
            part = st.at[lev, pl.ds(0, chips - 1)]
            remote(part, part, b_send.at[lev], b_recv.at[lev], (group, mate)).wait_send()

    for d in range(1, groups):

        @pl.when(group - d >= 0)
        def _():
            remote(u.at[0], u.at[0], z_send.at[d], z_recv.at[0], (group, mate)).wait_send()

        @pl.when(group + d < groups)
        def _():
            remote(cown, cown, c_send.at[d], c_recv.at[0], (group, mate)).wait_send()

    @pl.when(core == 1)
    def _():
        g0_copy.wait_send()

    @pl.when(core == 0)
    def _():
        g0_copy.wait_recv()

    part = out.at[pl.ds(0, shards - 1)]
    rest = remote(part, part, o_sem.at[0], o_sem.at[1], (group, mate))
    rest.wait_send()
    rest.wait_recv()


def middle_kernel(
    nb,
    nz,
    ids_ref,
    v_ref,
    do_ref,
    k_ref,
    q_ref,
    lam_ref,
    crow_ref,
    ccol_ref,
    sib_ref,
    h_ref,
    dv_ref,
    dq_ref,
    dk_ref,
    dlam_ref,
    dlog_ref,
    g_ref,
    bd_t,
    bd,
    lam_t,
    dlam_t,
    rint,
    dq_acc,
    dsc,
):
    heads = ccol_ref.shape[1]
    pairs = heads // 2
    columns = lam_t.shape[0]
    group, me, chip, core = place()
    row = iota((TOK, TOK), 0)
    col = iota((TOK, TOK), 1)
    half = (col < 64).astype(F32)
    m0 = half.astype(BF16)
    m1 = (1.0 - half).astype(BF16)
    t0 = (row < 64).astype(F32).astype(BF16)
    t1 = (row >= 64).astype(F32).astype(BF16)
    crow = crow_ref[...]
    ccol = ccol_ref[...]
    growth = jnp.exp(crow)
    q = q_ref[...]
    k = k_ref[...]
    qt = q.T
    kt = k.T
    causal = row <= col
    scores = jnp.where(causal, dot(k, qt, precision=highest), 0.0)
    mid = ccol[TOK // 2 - 1 : TOK // 2, :]
    b_col = jnp.exp(mid - ccol)
    a_row = jnp.exp(crow - crow[:, TOK // 2 - 1 : TOK // 2])
    suffix = (row >= col).astype(F32).astype(BF16)
    before = row < col
    wide = min(128, columns * heads)
    n = wide // heads
    for j in range(columns // n):
        lam_t[pl.ds(j * n, n)] = lam_ref[:, j * wide : (j + 1) * wide].T.reshape(n, heads, TOK)
    dlam_t[...] = jnp.zeros(dlam_t.shape, F32)
    rint[...] = jnp.zeros(rint.shape, F32)
    dq_acc[...] = jnp.zeros(dq_acc.shape, F32)
    dsc[...] = jnp.zeros(dsc.shape, F32)

    for p in range(pairs):
        sl = slice(p * 128, (p + 1) * 128)
        dop = do_ref[:, sl]
        dot_t = dop.astype(F32).T.astype(BF16)
        bdt = jnp.concatenate([dot_t * t0, dot_t * t1], axis=1)
        bdo = jnp.concatenate([dop * m0, dop * m1], axis=0)
        bd_t[p] = bdt
        bd[p] = bdo
        dmix = dot(v_ref[:, sl], bdt)
        xs = []
        for j in range(2):
            head = 2 * p + j
            dm = dmix[:, j * 128 : (j + 1) * 128]
            e = jnp.where(causal, b_col[:, head : head + 1] * a_row[head : head + 1, :], 0.0)
            x = e * scores
            dsc[...] += e * dm
            y = dot((x * dm).astype(BF16), suffix)
            dlog_ref[head : head + 1, :] = jnp.sum(
                jnp.where(before, y, 0.0), axis=0, keepdims=True
            )
            xs.append(x.astype(BF16))
        dv_ref[:, sl] = dot(jnp.concatenate(xs, axis=1), bdo)

    q_low = q.astype(BF16).astype(F32).T
    q2 = jnp.concatenate([q_low, q_low], axis=1)

    for b in range(1 + nb + nz):
        if b == 0:
            mine = core == 1
        elif b <= nb:
            mine = bit_of(chip, b - 1)
        else:
            mine = bit_of(group, b - 1 - nb)

        @pl.when(mine)
        def _():
            lev = ids_ref[0, b]

            def pair_step(p):
                if b == 0:
                    held = sib_ref[pl.ds(2 * p, 2), 0:4].reshape(64, 128)
                    scale = None
                else:
                    scale = jnp.where(core == 1, sib_ref[2 * p, 4, 0:1], jnp.ones((1, 128), F32))
                    held = h_ref[b - 1, p].reshape(64, 128) * scale
                m = dot(held.astype(BF16), bd_t[p])
                lam2 = lam_t[lev, pl.ds(2 * p, 2), :]
                gr2 = jnp.exp(crow_ref[pl.ds(2 * p, 2), :])
                w2 = lam2 * gr2
                w = jnp.concatenate([w2[0:1], w2[1:2]], axis=1)
                gsum = jnp.sum(q2 * m, axis=0, keepdims=True)
                dq_acc[...] += w * m
                grad = dot((w * q2).astype(BF16), bd[p])
                if scale is not None:
                    grad = grad * scale
                g_ref[b, p] = grad.reshape(2, 4, 8, 128)
                g2 = jnp.concatenate([gsum[:, 0:128], gsum[:, 128:256]], axis=0)
                dlam_t[lev, pl.ds(2 * p, 2), :] += gr2 * g2
                rint[pl.ds(2 * p, 2), :] += w2 * g2

            loop(0, pairs, pair_step)

    r = rint[...]
    tri = (row >= col).astype(F32)
    own = jnp.where(core == 0, 1.0, 0.0)
    dlog_ref[...] += dot(r, tri, precision=highest) - own * jnp.sum(r, axis=1, keepdims=True)
    dqi = (dq_acc[:, 0:128] + dq_acc[:, 128:256]).astype(BF16).astype(F32)
    dst = dsc[...]
    dq_ref[...] = (dqi + dot(kt, dst, precision=highest)).T
    dk_ref[...] = dot(dst, q, precision=highest)
    for j in range(columns // n):
        dlam_ref[:, j * wide : (j + 1) * wide] = dlam_t[pl.ds(j * n, n)].reshape(wide, TOK).T


def end_kernel(
    v_ref, k_ref, ccol_ref, ds_ref, g0_ref, dvp_ref, dkp_ref, dlogp_ref, dv_ref, dk_ref, dlog_ref
):
    heads = ccol_ref.shape[1]
    pairs = heads // 2
    group, me, chip, core = place()
    row = iota((TOK, TOK), 0)
    col = iota((TOK, TOK), 1)
    left = col < 64
    ccol = ccol_ref[...]
    tail = jnp.exp(ccol[TOK - 1 : TOK, :] - ccol)
    k_low = k_ref[...].astype(BF16)
    even = core == 0
    dk = jnp.zeros((TOK, 64), F32)
    ls = jnp.zeros((TOK, heads), F32)
    dd = jnp.zeros((8, heads), F32)
    lane_row = iota((TOK, heads), 0)
    lane_col = iota((TOK, heads), 1)
    for p in range(pairs):
        sl = slice(p * 128, (p + 1) * 128)
        pick = (lane_col == 2 * p + lane_row // 64).astype(F32)
        grad = ds_ref[2 * p : 2 * p + 2, 0:4].reshape(64, 128)
        grad = grad + jnp.where(even, g0_ref[p].reshape(64, 128), 0.0)
        low = grad.astype(BF16)
        scale = jnp.where(left, tail[:, 2 * p : 2 * p + 1], tail[:, 2 * p + 1 : 2 * p + 2])
        vp = v_ref[:, sl].astype(F32)
        dvs = scale * dot(k_low, low)
        decayed = (scale * vp).astype(BF16)
        dk += lax.dot_general(
            decayed, low, (((1,), (1,)), ((), ())), preferred_element_type=F32
        )
        dv_ref[:, sl] = (dvp_ref[:, sl] + dvs).astype(BF16)
        ls += dot((vp * dvs).astype(BF16), pick.astype(BF16))
        dd += dot(ds_ref[2 * p, 4] + ds_ref[2 * p + 1, 4], pick, precision=highest)
    dk_ref[...] = dkp_ref[...] + dk
    strict = (row > col).astype(F32)
    dlog_ref[...] = (
        dlogp_ref[...].T
        + dot(strict, ls, precision=highest)
        + jnp.sum(dd, axis=0, keepdims=True)
    )


def body(
    values, state_input, state_output, log_decay, level_lam, level_ids, upstream, final_upstream
):
    shards, groups = lax.axis_size("shard"), lax.axis_size("grp")
    chips = shards // 2
    nb, nz = log2(chips), log2(groups)
    heads = log_decay.shape[1]
    columns = level_lam.shape[1] // heads
    me = lax.axis_index("shard")
    params = partial(pltpu.CompilerParams, vmem_limit_bytes=VMEM_CAP)

    blk, crow, ccol = pl.pallas_call(
        state_kernel,
        out_shape=(f32(shards, 5, 8, 128), f32(heads, TOK), f32(TOK, heads)),
        in_specs=[vmem()] * 3,
        out_specs=(vmem(),) * 3,
        compiler_params=params(),
        name="state",
    )(values, state_input, log_decay)

    dma = pltpu.SemaphoreType.DMA
    h, sib, r1, nd, zb, hz = pl.pallas_call(
        partial(forward_kernel, shards, groups),
        out_shape=(
            f32(nb + nz, chips, 2, 4, 8, 128),
            f32(shards, 5, 8, 128),
            f32(shards, 5, 8, 128),
            f32(2 * chips, 5, 8, 128),
            f32(groups, 5, 8, 128),
            f32(nz, 4, 8, 128),
        ),
        in_specs=[vmem()],
        out_specs=(vmem(),) * 6,
        scratch_shapes=[
            pltpu.VMEM((chips, nb + nz, 4, 8, 128), F32),
            pltpu.VMEM((chips, 8, 128), F32),
            pltpu.VMEM((8, 128), F32),
            dma((2,)),
            dma((2,)),
            dma((1,)),
            dma((groups,)),
            dma((nb + nz,)),
            dma((nb + nz,)),
            dma((nb + nz,)),
            dma((nb + nz,)),
        ],
        compiler_params=params(collective_id=0, has_side_effects=True),
        name="forward",
    )(blk)

    dv, dq, dk, dlam, dlog, g = pl.pallas_call(
        partial(middle_kernel, nb, nz),
        out_shape=(
            f32(TOK, heads * 64),
            f32(TOK, 64),
            f32(TOK, 64),
            f32(TOK, columns * heads),
            f32(heads, TOK),
            f32(1 + nb + nz, chips, 2, 4, 8, 128),
        ),
        in_specs=[pl.BlockSpec(memory_space=pltpu.SMEM)] + [vmem()] * 9,
        out_specs=(vmem(),) * 6,
        scratch_shapes=[
            pltpu.VMEM((chips, 128, 256), BF16),
            pltpu.VMEM((chips, 256, 128), BF16),
            pltpu.VMEM((columns, heads, TOK), F32),
            pltpu.VMEM((columns, heads, TOK), F32),
            pltpu.VMEM((heads, TOK), F32),
            pltpu.VMEM((64, 256), F32),
            pltpu.VMEM((TOK, TOK), F32),
        ],
        compiler_params=params(),
        name="middle",
    )(
        level_ids,
        values,
        upstream,
        state_input,
        state_output,
        level_lam,
        crow,
        ccol,
        sib,
        h,
    )

    final = final_upstream.reshape(chips, 2, 2, 32, 64)[me // 2, :, me % 2]
    final = final.transpose(1, 0, 2).reshape(4, 8, 128)
    ds, g0 = pl.pallas_call(
        partial(backward_kernel, shards, groups),
        out_shape=(f32(shards, 5, 8, 128), f32(chips, 2, 4, 8, 128)),
        in_specs=[vmem()] * 6,
        out_specs=(vmem(),) * 2,
        scratch_shapes=[
            pltpu.VMEM((nb + nz, chips, 4, 8, 128), F32),
            pltpu.VMEM((nb + nz, chips, 4, 8, 128), F32),
            pltpu.VMEM((nb + nz, chips, 4, 8, 128), F32),
            pltpu.VMEM((nz, 4, 8, 128), F32),
            pltpu.VMEM((groups, 4, 8, 128), F32),
            pltpu.VMEM((groups, 8, 128), F32),
            pltpu.VMEM((8, 128), F32),
            pltpu.VMEM((8, 128), F32),
            pltpu.VMEM((2 * chips, 4, 8, 128), F32),
            pltpu.VMEM((chips, 8, 128), F32),
            pltpu.VMEM((shards, 5, 8, 128), F32),
            dma((2,)),
            dma((nb + nz,)),
            dma((nb + nz,)),
            dma((nb + nz,)),
            dma((nb + nz,)),
            dma((groups,)),
            dma((groups,)),
            dma((groups,)),
            dma((groups,)),
            dma((2,)),
        ],
        compiler_params=params(collective_id=1, has_side_effects=True),
        name="backward",
    )(g, r1, nd, zb, hz, final)

    dv, dk, dlog = pl.pallas_call(
        end_kernel,
        out_shape=(
            jax.ShapeDtypeStruct((TOK, heads * 64), BF16),
            f32(TOK, 64),
            f32(TOK, heads),
        ),
        in_specs=[vmem()] * 8,
        out_specs=(vmem(),) * 3,
        compiler_params=params(),
        name="end",
    )(values, state_input, ccol, ds, g0, dv, dk, dlog)
    return (dv, dk, dq, dlog, dlam)


def solution(mesh):
    spec = P(("grp", "shard"), None)
    return jax.shard_map(
        body,
        mesh=mesh,
        in_specs=(spec,) * 7 + (P(),),
        out_specs=(spec,) * 5,
        check_vma=False,
    )
```

time: 514 us -> 128 us (0.25); the launches traced: 504 us -> 128 us
  waiting for transfers between devices: 312 us -> 0 us
  Pallas kernels: 0 us -> 111 us
  other arithmetic: 72.8 us -> 0 us
  starting transfers between devices: 48.4 us -> 0 us
  matrix products: 46.3 us -> 0 us
  local copies, waits for them, and re-layouts: 22.5 us -> 15.8 us
    ppermute x32 -> x0, waiting for transfers between devices: 312 us -> none  [swapped(): lax.ppermute(x, axis, [(i, i ^ 1 << apart) for i in range(lax.axis_size(a...]
    pallas_call x0 -> x5, Pallas kernels: none -> 111 us  [the longest x1 64.6 us: body(): pl.pallas_call(partial(backward_kernel, shards, groups), out_shape=(f32(s...]
    ppermute x32 -> x0, starting transfers between devices: 48.4 us -> none  [swapped(): lax.ppermute(x, axis, [(i, i ^ 1 << apart) for i in range(lax.axis_size(a...]
    dot_general x36 -> x0, matrix products: 46.3 us -> none  [the longest x24 28.6 us: inter_output(): jnp.einsum('tn,hnp->thp', out_low, level_states[bit_no].astype(jnp.bfloat...]
    reduce_sum x9 -> x0, other arithmetic: 20.4 us -> none  [the longest x7 15.6 us: level_merge(): own_decay[..., None, None] * far_agg + own_agg]
    add x8 -> x0, other arithmetic: 17.8 us -> none  [the longest x7 16.9 us: level_merge(): upper_state * (own_decay[..., None, None] * far_agg + own_agg)]
    add_any x20 -> x0, other arithmetic: 17.5 us -> none  [the longest x8 8.72 us: level_merge(): held_state = upper_state * own_prefix[..., None, None] * far_agg]
    dynamic_update_slice x6 -> x0, other arithmetic: 6.26 us -> none  [intra_output(): mixed = lax.map(head_group, (value_groups, cum_groups))]
  transfers between devices with their start and end apart: 32 -> 0, of which waited for: 16 -> 0; matrix products, arithmetic and copies ran while one was open for 18% -> 0% of each run, Pallas kernels for 0% -> 0%
where the time goes in v1:
time: 128 us
  Pallas kernels  111 us (87%)
  local copies, waits for them, and re-layouts  15.8 us (12%)
    pallas_call x1, Pallas kernels, body(): pl.pallas_call(partial(backward_kernel, shards, groups), out_shape=(f32(s...  64.6 us
    pallas_call x1, Pallas kernels, body(): pl.pallas_call(partial(forward_kernel, shards, groups), out_shape=(f32(nb...  31.8 us
    unnamed x36, local copies, waits for them, and re-layouts  14.4 us
    pallas_call x1, Pallas kernels, body(): pl.pallas_call(partial(middle_kernel, nb, nz), out_shape=(f32(TOK, heads...  10.2 us
    pallas_call x1, Pallas kernels, body(): pl.pallas_call(end_kernel, out_shape=(jax.ShapeDtypeStruct((TOK, heads *...  3.66 us

profile of v1, /device:TPU:1, one launch (start us, length us, event | category | flops | bytes accessed | tf_op | source)
XLA Modules:
  0.0 127.6 jit_solution(5555670917219300943)
XLA Ops:
  0.6 0.0 copy-start
  0.6 0.9 copy.18.k_ref
  1.6 0.8 copy.14.ld_ref
  2.4 0.0 copy-start.1
  2.4 1.0 copy-done.1
  3.5 0.7 state.1
  4.2 0.8 copy.16.q_ref
  5.0 31.8 %forward.1 = (f32[7,16,2,4,8,128]{5,4,3,2,1,0:T(8,128)}, f32[32,5,8,128]{3,2,1,0:T(8,128)S(1)}, f32[32,5,8,128]{3,2,1,0:T(8,128)S(1)}, f32[32,5,8,128]{3,2,1,0:T...) custom-call(f32[32,5,8,128]{3,2,1,0:T(8,128)S(1)} %get-tuple-element.27.blk), custom_call_target="tpu_custom_call" | custom-call | tf_op jit(solution)/shard_map/forward/pallas_call | solution.py:766
  36.8 0.0 copy-start.4
  36.8 0.9 copy-done.4
  37.7 0.0 copy-start.7
  37.7 0.7 copy-done.7
  38.4 0.6 copy-done.10
  39.0 1.0 copy-done.2
  40.1 1.0 copy-done.6
  41.1 0.9 copy-done.9
  42.0 0.7 copy-done.14
  42.7 10.2 %middle.1 = (f32[128,2048]{1,0:T(8,128)S(1)}, f32[128,64]{1,0:T(8,128)S(1)}, f32[128,64]{1,0:T(8,128)S(1)}, f32[128,256]{1,0:T(8,128)}, f32[32,128]{1,0:T(8,128)S(1)}, /*index=5*/f32[8,16,2,4,8,128]{5,4,3,2,1,0:T(8,128)}) custom-call(s32[1,8]{1,0:T(1,128)S(1)} %copy-done.14, bf16[128,2048]{1,0:T(8,128)(2,1)S(1)} %copy-done.2, ...), custom_call_target="tpu_custom_call" | custom-call | tf_op jit(solution)/shard_map/middle/pallas_call | solution.py:795
  52.9 0.0 copy-done
  52.9 0.6 copy.23
  53.6 0.0 copy-done.12
  53.6 0.8 reshape.17.fu
  54.4 1.1 copy-done.5
  55.5 0.9 copy-done.8
  56.4 0.8 copy-done.11
  57.2 64.6 %backward.1 = (f32[32,5,8,128]{3,2,1,0:T(8,128)S(1)}, f32[16,2,4,8,128]{4,3,2,1,0:T(8,128)S(1)}) custom-call(f32[8,16,2,4,8,128]{5,4,3,2,1,0:T(8,128)} %get-tuple-element.30.g, f32[32,5,8,128]{3,2,1,0:T(8,128)S(1)} %get-tuple-element.31.r1, f32[32,5,8,128]{3,2,1,0:T(8,128)S(1)} %copy-done.5, f32[8,5,8,128]{3,2,1,0:T(8,128)S(1)} %copy-done.8, ...), custom_call_target="tpu_custom_call" | custom-call | tf_op jit(solution)/shard_map/backward/pallas_call | solution.py:833
  121.9 0.0 copy-done.3
  121.9 0.0 copy-done.13
  121.9 3.7 %end.1 = (bf16[128,2048]{1,0:T(8,128)(2,1)}, f32[128,64]{1,0:T(8,128)S(1)}, f32[128,32]{1,0:T(8,128)S(1)}) custom-call(bf16[128,2048]{1,0:T(8,128)(2,1)S(1)} %copy-done.3, f32[128,64]{1,0:T(8,128)S(1)} %copy.18.k_ref, f32[128,32]{1,0:T(8,128)S(1)} %get-tuple-element.25.ccol_ref, f32[32,5,8,128]{3,2,1,0:T(8,128)S(1)} %get-tuple-element.35.ds_ref, ...), custom_call_target="tpu_custom_call" | custom-call | tf_op jit(solution)/shard_map/end/pallas_call | solution.py:865
  125.5 0.7 copy.19
  126.2 0.7 copy.20
  126.9 0.7 copy.21
  (12 shorter events, 0.0 us)
Async XLA Ops:
  0.6 52.3 %copy-start = (f32[32,64,64]{2,1,0:T(8,128)S(1)}, f32[32,64,64]{2,1,0:T(8,128)}, u32[]{:S(2)}) copy-start(f32[32,64,64]{2,1,0:T(8,128)} %param.15) | copy-start | bytes 1572868
  2.4 1.0 copy-start.1
  36.8 0.9 copy-start.4
  37.7 0.7 copy-start.7
  38.4 0.6 copy-start.10
  39.0 1.0 copy-start.2
  40.1 1.0 copy-start.6
  41.1 0.9 copy-start.9
  42.0 0.7 copy-start.14
  52.9 0.7 copy-start.12
  52.9 69.0 %copy-start.3 = (bf16[128,2048]{1,0:T(8,128)(2,1)S(1)}, bf16[128,2048]{1,0:T(8,128)(2,1)}, u32[]{:S(2)}) copy-start(bf16[128,2048]{1,0:T(8,128)(2,1)} %v_ref.5) | copy-start | bytes 1572868
  54.4 1.1 copy-start.5
  55.5 0.9 copy-start.8
  56.4 0.8 copy-start.11
  57.2 64.6 %copy-start.13 = (f32[32,128]{1,0:T(8,128)S(1)}, f32[32,128]{1,0:T(8,128)}, u32[]{:S(2)}) copy-start(f32[32,128]{1,0:T(8,128)} %copy-done.12) | copy-start | bytes 49156

commit v2 on v0

v2 whole, which is shorter than its diff:
```python
from functools import partial

import jax
import jax.numpy as jnp
from jax import lax
from jax.experimental import pallas as pl
from jax.experimental.pallas import tpu as pltpu
from jax.sharding import PartitionSpec as P

highest = lax.Precision.HIGHEST
MESH = pl.DeviceIdType.MESH
F32 = jnp.float32
BF16 = jnp.bfloat16
TOK = 128
VMEM_CAP = 48 * 1024 * 1024


def log2(n):
    return n.bit_length() - 1


def vmem():
    return pl.BlockSpec(memory_space=pltpu.VMEM)


def f32(*shape):
    return jax.ShapeDtypeStruct(shape, F32)


def iota(shape, dim):
    return lax.broadcasted_iota(jnp.int32, shape, dim)


def dot(a, b, **kw):
    return jnp.dot(a, b, preferred_element_type=F32, **kw)


def place():
    group = lax.axis_index("grp")
    me = lax.axis_index("shard")
    return group, me, me // 2, me % 2


def remote(src, dst, send, recv, device):
    return pltpu.make_async_remote_copy(
        src_ref=src, dst_ref=dst, send_sem=send, recv_sem=recv, device_id=device, device_id_type=MESH
    )


def loop(start, stop, fn):
    def step(i, carry):
        fn(i)
        return carry

    lax.fori_loop(start, stop, step, 0)


def enter(group, me, chip, core, chips, groups):
    barrier = pltpu.get_barrier_semaphore()

    def greet(shard, grp):
        pl.semaphore_signal(barrier, inc=1, device_id=(grp, shard), device_id_type=MESH)

    loop(1, chips, lambda d: greet(2 * ((chip + d) % chips) + core, group))
    loop(1, groups, lambda d: greet(me, (group + d) % groups))
    greet(me + 1 - 2 * core, group)
    return lambda: pl.semaphore_wait(barrier, chips + groups - 1)


def offsets(chips):
    offs, at, n = [], 0, chips
    while n >= 1:
        offs.append(at)
        at += n
        n //= 2
    return offs


def high_level(group, far, bits):
    level = jnp.int32(0)
    for b in range(1, bits):
        level = jnp.where(group // 2**b != far // 2**b, jnp.int32(b), level)
    return level


def bit_of(x, b):
    return (x // 2**b) % 2 == 1


def main_kernel(
    shards,
    groups,
    ids_ref,
    v_any,
    do_any,
    kt_any,
    qt_any,
    ldt_any,
    lam_any,
    fu_any,
    dv_ref,
    dqt_ref,
    dkt_ref,
    dlam_ref,
    dlogt_ref,
    crow_ref,
    low_ref,
    dld_ref,
    v_ref,
    do_ref,
    kt_ref,
    qt_ref,
    ldt_ref,
    lam_ref,
    fu_ref,
    in_sem,
    bd_t,
    bd,
    lam_t,
    glam,
    rint,
    dq_acc,
    dsc,
    g,
    own,
    dec,
    sib,
    sibd,
    blk,
    nd,
    zb,
    hz,
    stage,
    pin,
    coef,
    h,
    x,
    st,
    rb,
    u,
    zu,
    ct,
    cown,
    dn,
    rt,
    out,
    ds,
    g0,
    s_sem,
    a_sem,
    z_send,
    z_recv,
    h_send,
    h_recv,
    f_send,
    f_recv,
    g0_sem,
    x_send,
    x_recv,
    b_send,
    b_recv,
    u_send,
    u_recv,
    c_send,
    c_recv,
    o_sem,
    w_sem,
):
    chips = shards // 2
    pairs = chips
    heads = shards
    nb, nz = log2(chips), log2(groups)
    levels = nb + nz
    columns = lam_t.shape[0]
    ydim = 2 ** ((nb + 1) // 2)
    xdim = chips // ydim
    group, me, chip, core = place()
    mate = me + 1 - 2 * core
    xpos, ypos = chip // ydim, chip % ydim
    offs = offsets(chips)
    top = offs[nb]
    wide = min(128, columns * heads)
    per = wide // heads

    def shifted(i):
        return ((xpos + i // ydim) % xdim) * ydim + (ypos + i % ydim) % ydim

    def mine(lev):
        return bit_of(chip, lev) if lev < nb else bit_of(group, lev - nb)

    def near(src, dst, send, recv):
        return remote(src, dst, send, recv, (group, mate))

    loads = [
        pltpu.make_async_copy(a, b, in_sem.at[i])
        for i, (a, b) in enumerate(
            [
                (ldt_any, ldt_ref),
                (kt_any, kt_ref),
                (v_any, v_ref),
                (do_any, do_ref),
                (qt_any, qt_ref),
                (lam_any, lam_ref),
                (fu_any.at[chip, :, core], fu_ref),
            ]
        )
    ]
    for c in loads:
        c.start()
    wait_entry = enter(group, me, chip, core, chips, groups)

    row = iota((TOK, TOK), 0)
    col = iota((TOK, TOK), 1)
    upto = (row <= col).astype(F32)
    half = (col < 64).astype(F32)
    m0 = half.astype(BF16)
    m1 = (1.0 - half).astype(BF16)
    loads[0].wait()
    crow = dot(ldt_ref[...], upto, precision=highest)
    crow_ref[...] = crow
    last = jnp.broadcast_to(crow[:, TOK - 1 : TOK], (heads, TOK))
    tail = jnp.exp(last - crow)
    full = jnp.exp(last)
    loads[1].wait()
    kt = kt_ref[...]
    loads[2].wait()
    for p in range(pairs):
        k2 = jnp.concatenate(
            [kt * tail[2 * p : 2 * p + 1], kt * tail[2 * p + 1 : 2 * p + 2]], axis=1
        ).astype(BF16)
        vp = v_ref[:, p * 128 : (p + 1) * 128]
        s = dot(k2, jnp.concatenate([vp * m0, vp * m1], axis=0))
        own[p] = s.reshape(2, 4, 8, 128)
        dec[p] = (
            half[0:8] * full[2 * p : 2 * p + 1] + (1.0 - half[0:8]) * full[2 * p + 1 : 2 * p + 2]
        )

    wait_entry()
    swap_half = near(own.at[:, 1 - core], sib.at[:, 1 - core], s_sem.at[0], s_sem.at[1])
    swap_dec = near(dec, sibd, s_sem.at[2], s_sem.at[3])
    rest = near(own.at[:, core], sib.at[:, core], s_sem.at[4], s_sem.at[5])
    swap_half.start()
    swap_dec.start()

    @pl.when(core == 0)
    def _():
        rest.start()

    swap_dec.wait_recv()
    swap_half.wait_recv()

    def merge_cores(p):
        a = own[p, core]
        b = sib[p, core]
        left = jnp.where(core == 0, a, b)
        right = jnp.where(core == 0, b, a)
        drow = jnp.where(core == 0, sibd[p], dec[p])
        blk[p, 0:4] = drow[None] * left + right
        blk[p, 4] = dec[p] * sibd[p]

    loop(0, pairs, merge_cores)

    def scatter(i):
        to = shifted(i)
        remote(
            blk.at[to], nd.at[chip], a_sem.at[0], a_sem.at[1], (group, 2 * to + core)
        ).start()

    loop(1, chips, scatter)
    nd[chip] = blk[chip]

    loads[3].wait()
    loads[4].wait()
    qt = qt_ref[...]
    q = qt.T
    k = kt.T
    ccol = crow.T
    causal = row <= col
    scores = jnp.where(causal, dot(k, qt, precision=highest), 0.0)
    b_col = jnp.exp(ccol[TOK // 2 - 1 : TOK // 2, :] - ccol)
    a_row = jnp.exp(crow - crow[:, TOK // 2 - 1 : TOK // 2])
    suffix = (row >= col).astype(F32).astype(BF16)
    before = row < col
    t0 = (row < 64).astype(F32).astype(BF16)
    t1 = (row >= 64).astype(F32).astype(BF16)
    dsc[...] = jnp.zeros(dsc.shape, F32)

    def inside(p):
        sl = slice(p * 128, (p + 1) * 128)
        dop = do_ref[:, sl]
        dot_t = dop.astype(F32).T.astype(BF16)
        bdt = jnp.concatenate([dot_t * t0, dot_t * t1], axis=1)
        bdo = jnp.concatenate([dop * m0, dop * m1], axis=0)
        bd_t[p] = bdt
        bd[p] = bdo
        dmix = dot(v_ref[:, sl], bdt)
        xs = []
        for j in range(2):
            head = 2 * p + j
            dm = dmix[:, j * 128 : (j + 1) * 128]
            e = jnp.where(causal, b_col[:, head : head + 1] * a_row[head : head + 1, :], 0.0)
            mix = e * scores
            dsc[...] += e * dm
            y = dot((mix * dm).astype(BF16), suffix)
            dlogt_ref[head : head + 1, :] = jnp.sum(
                jnp.where(before, y, 0.0), axis=0, keepdims=True
            )
            xs.append(mix.astype(BF16))
        dv_ref[:, sl] = dot(jnp.concatenate(xs, axis=1), bdo)

    for p in range(pairs // 2):
        inside(p)

    part = nd.at[pl.ds(0, chips - 1)]
    scattered = near(part, part, a_sem.at[0], a_sem.at[1])
    scattered.wait_recv()
    for b in range(1, nb + 1):
        for i in range(chips >> b):
            lo = offs[b - 1] + 2 * i
            right = nd[lo + 1, 4]
            nd[offs[b] + i, 0:4] = right[None] * nd[lo, 0:4] + nd[lo + 1, 0:4]
            nd[offs[b] + i, 4] = right * nd[lo, 4]

    def up(d):
        return remote(
            nd.at[top], zb.at[group], z_send.at[d], z_recv.at[group], (group + d, me)
        )

    def down(d):
        return remote(
            nd.at[top, 4], zb.at[group, 4], z_send.at[d], z_recv.at[group], (group - d, me)
        )

    for d in range(1, groups):

        @pl.when(group + d < groups)
        def _():
            up(d).start()

    for d in range(1, groups):

        @pl.when(group - d >= 0)
        def _():
            remote(
                nd.at[top, 4],
                zb.at[group, 4],
                z_send.at[groups + d],
                z_recv.at[group],
                (group - d, me),
            ).start()

    for c in range(chips):
        pre = None
        for b in range(nb):
            if (c >> b) & 1:
                left = offs[b] + (c >> b) - 1
                far = nd[left, 0:4]
                stage[c, b] = far if pre is None else pre[None] * far
                pre = nd[left, 4] if pre is None else pre * nd[left, 4]
        pin[c] = jnp.ones((8, 128), F32) if pre is None else pre

    def send_level(lev, to):
        remote(
            stage.at[to, lev],
            h.at[lev, chip, core],
            h_send.at[lev],
            h_recv.at[lev],
            (group, 2 * to + core),
        ).start()

    def send_low(i):
        to = shifted(i)
        for b in reversed(range(nb)):

            @pl.when(bit_of(to, b))
            def _():
                send_level(b, to)

    loop(1, chips, send_low)
    for b in range(nb):

        @pl.when(bit_of(chip, b))
        def _():
            h[b, chip, core] = stage[chip, b]

    for p in range(pairs // 2, pairs):
        inside(p)

    coef[...] = jnp.ones((8, 128), F32)
    hz[...] = jnp.zeros(hz.shape, F32)
    for d in range(1, groups):
        far = group - d

        @pl.when(far >= 0)
        def _():
            slot = zb.at[far]
            near(slot, slot, z_send.at[0], z_recv.at[far]).wait_recv()
            level = high_level(group, far, nz)
            hz[level] = hz[level] + coef[...][None] * zb[far, 0:4]
            coef[...] = coef[...] * zb[far, 4]

    for l in range(nz):

        @pl.when(bit_of(group, l))
        def _():
            def fill(c):
                stage[c, nb + l] = pin[c][None] * hz[l]

            loop(0, chips, fill)
            loop(1, chips, lambda i: send_level(nb + l, shifted(i)))
            h[nb + l, chip, core] = stage[chip, nb + l]

    q_low = qt.astype(BF16).astype(F32)
    q2 = jnp.concatenate([q_low, q_low], axis=1)
    loads[5].wait()
    for j in range(columns // per):
        lam_t[pl.ds(j * per, per)] = lam_ref[:, j * wide : (j + 1) * wide].T.reshape(
            per, heads, TOK
        )
    glam[...] = jnp.zeros(glam.shape, F32)
    rint[...] = jnp.zeros(rint.shape, F32)
    dq_acc[...] = jnp.zeros(dq_acc.shape, F32)
    ids = [ids_ref[0, b] for b in range(1 + levels)]

    def levels_step(group_levels, p):
        gr2 = jnp.exp(crow_ref[pl.ds(2 * p, 2), :])
        scale = jnp.where(core == 1, sibd[p, 0:1], jnp.ones((1, 128), F32))
        helds, ws = [], []
        for b in group_levels:
            if b == 0:
                held = sib[p].reshape(64, 128)
            else:
                held = jnp.where(mine(b - 1), h[b - 1, p].reshape(64, 128) * scale, 0.0)
            helds.append(held.astype(BF16))
            ws.append(lam_t[ids[b], pl.ds(2 * p, 2), :] * gr2)
        m = dot(jnp.concatenate(helds, axis=0), bd_t[p])
        wqs = []
        acc = dq_acc[...]
        r2 = rint[pl.ds(2 * p, 2), :]
        for i, b in enumerate(group_levels):
            mi = m[64 * i : 64 * (i + 1)]
            w = jnp.concatenate([ws[i][0:1], ws[i][1:2]], axis=1)
            gsum = jnp.sum(q2 * mi, axis=0, keepdims=True)
            acc = acc + w * mi
            wqs.append((w * q2).astype(BF16))
            g2 = jnp.concatenate([gsum[:, 0:128], gsum[:, 128:256]], axis=0)
            glam[b, pl.ds(2 * p, 2), :] = gr2 * g2
            r2 = r2 + ws[i] * g2
        dq_acc[...] = acc
        rint[pl.ds(2 * p, 2), :] = r2
        grad = dot(jnp.concatenate(wqs, axis=0), bd[p])
        for i, b in enumerate(group_levels):
            gi = grad[64 * i : 64 * (i + 1)]
            g[b, p] = (gi if b == 0 else gi * scale).reshape(2, 4, 8, 128)

    def levels_pass(group_levels):
        def two(i):
            levels_step(group_levels, 2 * i)
            levels_step(group_levels, 2 * i + 1)

        loop(0, pairs // 2, two)

    g0_copy = near(g.at[0], g0, g0_sem.at[0], g0_sem.at[1])

    @pl.when(core == 1)
    def _():
        rest.wait_recv()
        levels_pass([0])
        g0_copy.start()

    def swap(lev):
        return near(g.at[lev + 1, :, 1 - core], x.at[lev], x_send.at[lev], x_recv.at[lev])

    def fetch(levs):
        for lev in levs:

            @pl.when(mine(lev))
            def _():
                part = h.at[lev, pl.ds(0, chips - 1), core]
                near(part, part, h_send.at[lev], h_recv.at[lev]).wait_recv()
                ours = h.at[lev, :, core]
                near(ours, ours, f_send.at[lev], f_recv.at[lev]).start()

        for lev in levs:

            @pl.when(mine(lev))
            def _():
                theirs = h.at[lev, :, 1 - core]
                near(theirs, theirs, f_send.at[lev], f_recv.at[lev]).wait_recv()

    def give_back(levs):
        for lev in levs:

            @pl.when(mine(lev))
            def _():
                swap(lev).start()

        for lev in levs:

            @pl.when(mine(lev))
            def _():
                swap(lev).wait_recv()

                def add(c):
                    st[lev, c] = g[lev + 1, c, core] + x[lev, c]

                loop(0, chips, add)

                def send(i):
                    to = shifted(i)
                    remote(
                        st.at[lev, to],
                        rb.at[lev, chip],
                        b_send.at[lev],
                        b_recv.at[lev],
                        (group, 2 * to + core),
                    ).start()

                loop(1, chips, send)
                rb[lev, chip] = st[lev, chip]

    low = list(range(nb))
    high = list(range(nb, levels))
    fetch(low)
    levels_pass([b + 1 for b in low])
    give_back(low)
    fetch(high)

    @pl.when(group > 0)
    def _():
        levels_pass([b + 1 for b in high])

    give_back(high)

    for p in range(columns):
        total = jnp.zeros((heads, TOK), F32)
        for b in range(1 + levels):
            total = total + jnp.where(ids[b] == p, glam[b], 0.0)
        dlam_ref[p] = total
    r = rint[...]
    even = jnp.where(core == 0, 1.0, 0.0)
    dlogt_ref[...] += dot(r, (row >= col).astype(F32), precision=highest) - even * jnp.sum(
        r, axis=1, keepdims=True
    )
    dqi = (dq_acc[:, 0:128] + dq_acc[:, 128:256]).astype(BF16).astype(F32)
    dst = dsc[...]
    dqt_ref[...] = dqi + dot(kt, dst, precision=highest)
    dkt_ref[...] = dot(dst, q, precision=highest).T

    def arrived(lev, count):
        part = rb.at[lev, pl.ds(0, count)]
        near(part, part, b_send.at[lev], b_recv.at[lev]).wait_recv()

    lefts = [
        [(b, offs[b] + (c >> b) - 1) for b in range(nb) if (c >> b) & 1] for c in range(chips)
    ]
    rt[...] = jnp.zeros(rt.shape, F32)
    for l in range(nz):

        @pl.when(bit_of(group, l))
        def _():
            arrived(nb + l, chips - 1)
            total = jnp.zeros((4, 8, 128), F32)
            for c in range(chips):
                w = pin[c][None] * rb[nb + l, c]
                total = total + w
                rt[c] = rt[c] + jnp.sum(w * hz[l], axis=0)
            u[l] = total

    for d in range(1, groups):

        @pl.when(group - d >= 0)
        def _():
            level = high_level(group, group - d, nz)
            remote(
                u.at[level], zu.at[group], u_send.at[d], u_recv.at[group], (group - d, me)
            ).start()

    for b in range(nb):

        @pl.when(bit_of(chip, b))
        def _():
            if chips // 2 > 1:
                arrived(b, chips // 2 - 1)

        @pl.when(jnp.logical_not(bit_of(chip, b)))
        def _():
            arrived(b, chips // 2)

    for b in range(nb):
        for i in range(0, chips >> b, 2):
            left = offs[b] + i
            total = None
            for c in range((i + 1) << b, (i + 2) << b):
                w = rb[b, c]
                for bb, node in lefts[c]:
                    if bb < b:
                        w = nd[node, 4][None] * w
                rt[c] = rt[c] + jnp.sum(w * nd[left, 0:4], axis=0)
                total = w if total is None else total + w
            dn[left] = total

    coef[...] = jnp.ones((8, 128), F32)
    dn[top] = jnp.zeros((4, 8, 128), F32)
    for d in range(1, groups):

        @pl.when(group + d < groups)
        def _():
            far = zb.at[group + d, 4]
            near(far, far, z_send.at[0], z_recv.at[group + d]).wait_recv()
            slot = zu.at[group + d]
            near(slot, slot, u_send.at[d], u_recv.at[group + d]).wait_recv()
            dn[top] = dn[top] + coef[...][None] * zu[group + d]
            coef[...] = coef[...] * zb[group + d, 4]

    loads[6].wait()
    fu = jnp.concatenate([fu_ref[0], fu_ref[1]], axis=1).reshape(4, 8, 128)
    dn[top] = dn[top] + coef[...][None] * fu
    cown[...] = jnp.sum(nd[top, 0:4] * dn[top], axis=0)
    for l in range(nz):

        @pl.when(bit_of(group, l))
        def _():
            cown[...] = cown[...] - jnp.sum(u[l] * hz[l], axis=0)

    for d in range(1, groups):

        @pl.when(group + d < groups)
        def _():
            remote(cown, ct.at[group], c_send.at[d], c_recv.at[group], (group + d, me)).start()

    for b in reversed(range(nb)):
        for i in range(0, chips >> b, 2):
            left = offs[b] + i
            parent = dn[offs[b + 1] + i // 2]
            dn[left] = dn[left] + nd[left + 1, 4][None] * parent
            dn[left + 1] = parent

    carry = jnp.zeros((8, 128), F32)
    for c in range(chips):
        out[c, 0:4] = dn[c]
        out[c, 4] = carry
        carry = carry + jnp.sum(nd[c, 0:4] * dn[c], axis=0) - rt[c]
        out[c, 5] = carry

    coef[...] = jnp.zeros((8, 128), F32)
    for d in range(1, groups):

        @pl.when(group - d >= 0)
        def _():
            slot = ct.at[group - d]
            near(slot, slot, c_send.at[d], c_recv.at[group - d]).wait_recv()
            coef[...] = coef[...] + ct[group - d]

    def carry_in(c):
        out[c, 4:6] = out[c, 4:6] + coef[...][None]

    loop(0, chips, carry_in)

    def give(i):
        to = shifted(i)
        remote(
            out.at[to], ds.at[chip, core], o_sem.at[0], o_sem.at[1], (group, 2 * to + core)
        ).start()

    loop(1, chips, give)
    ds[chip, core] = out[chip]
    part = ds.at[pl.ds(0, chips - 1), core]
    given = near(part, part, o_sem.at[0], o_sem.at[1])
    given.wait_recv()
    ours = ds.at[:, core]
    near(ours, ours, w_sem.at[0], w_sem.at[1]).start()

    def sent(lev, count):
        left = stage.at[pl.ds(0, count), lev]
        near(left, left, h_send.at[lev], h_recv.at[lev]).wait_send()

    for lev in range(levels):

        @pl.when(mine(lev))
        def _():
            ours = h.at[lev, :, core]
            near(ours, ours, f_send.at[lev], f_recv.at[lev]).wait_send()
            swap(lev).wait_send()
            part = st.at[lev, pl.ds(0, chips - 1)]
            near(part, part, b_send.at[lev], b_recv.at[lev]).wait_send()
            if lev >= nb:
                sent(lev, chips - 1)
            elif chips // 2 > 1:
                sent(lev, chips // 2 - 1)

        if lev < nb:

            @pl.when(jnp.logical_not(mine(lev)))
            def _():
                sent(lev, chips // 2)

    for d in range(1, groups):

        @pl.when(group + d < groups)
        def _():
            up(d).wait_send()
            near(cown, cown, c_send.at[d], c_recv.at[0]).wait_send()

        @pl.when(group - d >= 0)
        def _():
            line = nd.at[top, 4]
            near(line, line, z_send.at[groups + d], z_recv.at[0]).wait_send()
            near(u.at[0], u.at[0], u_send.at[d], u_recv.at[0]).wait_send()

    swap_half.wait_send()
    swap_dec.wait_send()
    scattered.wait_send()

    @pl.when(core == 1)
    def _():
        g0_copy.wait_send()

    @pl.when(core == 0)
    def _():
        rest.wait_send()
        g0_copy.wait_recv()

    given.wait_send()
    theirs = ds.at[:, 1 - core]
    both = near(theirs, theirs, w_sem.at[0], w_sem.at[1])
    both.wait_recv()
    both.wait_send()

    def finish(p):
        grad = ds[p, :, 0:4]
        dot_own = jnp.sum(own[p] * grad, axis=1)
        dld = jnp.where(core == 0, ds[p, :, 4], ds[p, :, 5] - dot_own)
        dld_ref[p] = dld[0] + dld[1]
        scale = jnp.where(core == 0, sibd[p], jnp.ones((8, 128), F32))
        extra = jnp.where(core == 0, g0[p], 0.0)
        low_ref[p] = (grad * scale[None, None] + extra).reshape(64, 128).astype(BF16)

    loop(0, pairs, finish)


def end_kernel(
    v_ref,
    kt_ref,
    crow_ref,
    low_ref,
    dld_ref,
    dvp_ref,
    dkp_ref,
    dlogp_ref,
    dqp_ref,
    dlamp_ref,
    dv_ref,
    dk_ref,
    dq_ref,
    dlog_ref,
    dlam_ref,
):
    heads = crow_ref.shape[0]
    pairs = heads // 2
    columns = dlamp_ref.shape[0]
    row = iota((TOK, TOK), 0)
    col = iota((TOK, TOK), 1)
    left = col < 64
    ccol = crow_ref[...].T
    tail = jnp.exp(ccol[TOK - 1 : TOK, :] - ccol)
    k_low = kt_ref[...].T.astype(BF16)
    dk = jnp.zeros((64, TOK), F32)
    ls = jnp.zeros((TOK, heads), F32)
    dd = jnp.zeros((8, heads), F32)
    lane_row = iota((TOK, heads), 0)
    lane_col = iota((TOK, heads), 1)
    for p in range(pairs):
        sl = slice(p * 128, (p + 1) * 128)
        pick = (lane_col == 2 * p + lane_row // 64).astype(F32)
        low = low_ref[p]
        scale = jnp.where(left, tail[:, 2 * p : 2 * p + 1], tail[:, 2 * p + 1 : 2 * p + 2])
        vp = v_ref[:, sl].astype(F32)
        dvs = scale * dot(k_low, low)
        decayed = (scale * vp).astype(BF16)
        dk += lax.dot_general(
            low, decayed, (((1,), (1,)), ((), ())), preferred_element_type=F32
        )
        dv_ref[:, sl] = (dvp_ref[:, sl] + dvs).astype(BF16)
        ls += dot((vp * dvs).astype(BF16), pick.astype(BF16))
        dd += dot(dld_ref[p], pick, precision=highest)
    dk_ref[...] = dkp_ref[...] + dk
    dq_ref[...] = dqp_ref[...]
    strict = (row > col).astype(F32)
    dlog_ref[...] = dlogp_ref[...] + (
        dot(strict, ls, precision=highest) + jnp.sum(dd, axis=0, keepdims=True)
    ).T
    wide = min(128, columns * heads)
    per = wide // heads
    for j in range(columns // per):
        dlam_ref[:, j * wide : (j + 1) * wide] = (
            dlamp_ref[pl.ds(j * per, per)].reshape(wide, TOK).T
        )


def body(
    values, state_input, state_output, log_decay, level_lam, level_ids, upstream, final_upstream
):
    shards, groups = lax.axis_size("shard"), lax.axis_size("grp")
    chips = shards // 2
    nb, nz = log2(chips), log2(groups)
    levels = nb + nz
    heads = log_decay.shape[1]
    columns = level_lam.shape[1] // heads
    params = partial(pltpu.CompilerParams, vmem_limit_bytes=VMEM_CAP)
    dma = pltpu.SemaphoreType.DMA
    tile = (4, 8, 128)
    kt = state_input.T

    dv, dqt, dkt, dlam, dlogt, crow, low, dld = pl.pallas_call(
        partial(main_kernel, shards, groups),
        out_shape=(
            f32(TOK, heads * 64),
            f32(64, TOK),
            f32(64, TOK),
            f32(columns, heads, TOK),
            f32(heads, TOK),
            f32(heads, TOK),
            jax.ShapeDtypeStruct((chips, 64, 128), BF16),
            f32(chips, 8, 128),
        ),
        in_specs=[pl.BlockSpec(memory_space=pltpu.SMEM)]
        + [pl.BlockSpec(memory_space=pl.ANY)] * 7,
        out_specs=(vmem(),) * 8,
        scratch_shapes=[
            pltpu.VMEM((TOK, heads * 64), BF16),
            pltpu.VMEM((TOK, heads * 64), BF16),
            pltpu.VMEM((64, TOK), F32),
            pltpu.VMEM((64, TOK), F32),
            pltpu.VMEM((heads, TOK), F32),
            pltpu.VMEM((TOK, columns * heads), F32),
            pltpu.VMEM((2, 32, 64), F32),
            dma((7,)),
            pltpu.VMEM((chips, 128, 256), BF16),
            pltpu.VMEM((chips, 256, 128), BF16),
            pltpu.VMEM((columns, heads, TOK), F32),
            pltpu.VMEM((1 + levels, heads, TOK), F32),
            pltpu.VMEM((heads, TOK), F32),
            pltpu.VMEM((64, 256), F32),
            pltpu.VMEM((TOK, TOK), F32),
            pltpu.VMEM((1 + levels, chips, 2) + tile, F32),
            pltpu.VMEM((chips, 2) + tile, F32),
            pltpu.VMEM((chips, 8, 128), F32),
            pltpu.VMEM((chips, 2) + tile, F32),
            pltpu.VMEM((chips, 8, 128), F32),
            pltpu.VMEM((chips, 5, 8, 128), F32),
            pltpu.VMEM((2 * chips, 5, 8, 128), F32),
            pltpu.VMEM((groups, 5, 8, 128), F32),
            pltpu.VMEM((nz,) + tile, F32),
            pltpu.VMEM((chips, levels) + tile, F32),
            pltpu.VMEM((chips, 8, 128), F32),
            pltpu.VMEM((8, 128), F32),
            pltpu.VMEM((levels, chips, 2) + tile, F32),
            pltpu.VMEM((levels, chips) + tile, F32),
            pltpu.VMEM((levels, chips) + tile, F32),
            pltpu.VMEM((levels, chips) + tile, F32),
            pltpu.VMEM((nz,) + tile, F32),
            pltpu.VMEM((groups,) + tile, F32),
            pltpu.VMEM((groups, 8, 128), F32),
            pltpu.VMEM((8, 128), F32),
            pltpu.VMEM((2 * chips,) + tile, F32),
            pltpu.VMEM((chips, 8, 128), F32),
            pltpu.VMEM((chips, 6, 8, 128), F32),
            pltpu.VMEM((chips, 2, 6, 8, 128), F32),
            pltpu.VMEM((chips, 2) + tile, F32),
            dma((6,)),
            dma((2,)),
            dma((2 * groups,)),
            dma((groups,)),
            dma((levels,)),
            dma((levels,)),
            dma((levels,)),
            dma((levels,)),
            dma((2,)),
            dma((levels,)),
            dma((levels,)),
            dma((levels,)),
            dma((levels,)),
            dma((groups,)),
            dma((groups,)),
            dma((groups,)),
            dma((groups,)),
            dma((2,)),
            dma((2,)),
        ],
        compiler_params=params(collective_id=0, has_side_effects=True),
        name="main",
    )(
        level_ids,
        values,
        upstream,
        kt,
        state_output.T,
        log_decay.T,
        level_lam,
        final_upstream.reshape(chips, 2, 2, 32, 64),
    )

    dv, dk, dq, dlog, dlam = pl.pallas_call(
        end_kernel,
        out_shape=(
            jax.ShapeDtypeStruct((TOK, heads * 64), BF16),
            f32(64, TOK),
            f32(64, TOK),
            f32(heads, TOK),
            f32(TOK, columns * heads),
        ),
        in_specs=[vmem()] * 10,
        out_specs=(vmem(),) * 5,
        compiler_params=params(),
        name="end",
    )(values, kt, crow, low, dld, dv, dkt, dlogt, dqt, dlam)
    return (dv, dk.T, dq.T, dlog.T, dlam)


def solution(mesh):
    spec = P(("grp", "shard"), None)
    return jax.shard_map(
        body,
        mesh=mesh,
        in_specs=(spec,) * 7 + (P(),),
        out_specs=(spec,) * 5,
        check_vma=False,
    )
```

time: 514 us -> 99 us (0.19); the launches traced: 504 us -> 97.7 us
  waiting for transfers between devices: 312 us -> 0 us
  Pallas kernels: 0 us -> 90 us
  other arithmetic: 72.8 us -> 0 us
  starting transfers between devices: 48.4 us -> 0 us
  matrix products: 46.3 us -> 0 us
  local copies, waits for them, and re-layouts: 22.5 us -> 7.09 us
    ppermute x32 -> x0, waiting for transfers between devices: 312 us -> none  [swapped(): lax.ppermute(x, axis, [(i, i ^ 1 << apart) for i in range(lax.axis_size(a...]
    pallas_call x0 -> x2, Pallas kernels: none -> 90 us  [the longest x1 86.2 us: body(): pl.pallas_call(partial(main_kernel, shards, groups), out_shape=(f32(TOK,...]
    ppermute x32 -> x0, starting transfers between devices: 48.4 us -> none  [swapped(): lax.ppermute(x, axis, [(i, i ^ 1 << apart) for i in range(lax.axis_size(a...]
    dot_general x36 -> x0, matrix products: 46.3 us -> none  [the longest x24 28.6 us: inter_output(): jnp.einsum('tn,hnp->thp', out_low, level_states[bit_no].astype(jnp.bfloat...]
    reduce_sum x9 -> x0, other arithmetic: 20.4 us -> none  [the longest x7 15.6 us: level_merge(): own_decay[..., None, None] * far_agg + own_agg]
    add x8 -> x0, other arithmetic: 17.8 us -> none  [the longest x7 16.9 us: level_merge(): upper_state * (own_decay[..., None, None] * far_agg + own_agg)]
    add_any x20 -> x0, other arithmetic: 17.5 us -> none  [the longest x8 8.72 us: level_merge(): held_state = upper_state * own_prefix[..., None, None] * far_agg]
    dynamic_update_slice x6 -> x0, other arithmetic: 6.26 us -> none  [intra_output(): mixed = lax.map(head_group, (value_groups, cum_groups))]
  transfers between devices with their start and end apart: 32 -> 0, of which waited for: 16 -> 0; matrix products, arithmetic and copies ran while one was open for 18% -> 0% of each run, Pallas kernels for 0% -> 0%
where the time goes in v2:
time: 99 us; the launch traced here: 97.7 us
  Pallas kernels  90 us (91%)
  local copies, waits for them, and re-layouts  7.09 us (7%)
    pallas_call x1, Pallas kernels, body(): pl.pallas_call(partial(main_kernel, shards, groups), out_shape=(f32(TOK,...  86.2 us
    unnamed x18, local copies, waits for them, and re-layouts  7.09 us
    pallas_call x1, Pallas kernels, body(): pl.pallas_call(end_kernel, out_shape=(jax.ShapeDtypeStruct((TOK, heads *...  3.77 us

profile of v2, /device:TPU:1, one launch (start us, length us, event | category | flops | bytes accessed | tf_op | source)
XLA Modules:
  0.0 97.7 jit_solution(14502271954015209525)
XLA Ops:
  0.6 0.0 copy-start.8
  0.6 0.6 copy-done.8
  1.3 0.0 copy-start
  1.3 1.0 %copy-done = bf16[128,2048]{1,0:T(8,128)(2,1)S(1)} copy-done((bf16[128,2048]{1,0:T(8,128)(2,1)S(1)}, bf16[128,2048]{1,0:T(8,128)(2,1)}, u32[]{:S(2)}) %copy-start) | copy-done | bytes 524312
  2.3 0.0 copy-start.2
  2.3 1.2 %copy-done.2 = f32[32,64,64]{2,1,0:T(8,128)S(1)} copy-done((f32[32,64,64]{2,1,0:T(8,128)S(1)}, f32[32,64,64]{2,1,0:T(8,128)}, u32[]{:S(2)}) %copy-start.2) | copy-done | bytes 524312
  3.6 0.0 copy-start.3
  3.6 1.0 %copy-done.3 = bf16[128,2048]{1,0:T(8,128)(2,1)S(1)} copy-done((bf16[128,2048]{1,0:T(8,128)(2,1)S(1)}, bf16[128,2048]{1,0:T(8,128)(2,1)}, u32[]{:S(2)}) %copy-start.3) | copy-done | bytes 524312
  4.6 0.0 copy-start.4
  4.6 0.8 copy-done.4
  5.4 0.0 copy-start.5
  5.4 0.9 copy-done.5
  6.3 0.0 copy-start.6
  6.3 0.8 copy-done.6
  7.0 0.0 copy-start.7
  7.0 0.7 copy-done.7
  7.7 0.0 copy-start.1
  7.7 86.2 %main.1 = (f32[128,2048]{1,0:T(8,128)S(1)}, f32[64,128]{1,0:T(8,128)S(1)}, f32[64,128]{1,0:T(8,128)S(1)}, f32[8,32,128]{2,1,0:T(8,128)S(1)}, f32[32,128]{1,0:T(8...) custom-call(s32[1,8]{1,0:T(1,128)S(1)} %copy-done.8, ...), custom_call_target="tpu_custom_call" | custom-call | tf_op jit(solution)/shard_map/main/pallas_call | solution.py:815
  94.0 0.0 copy-done.1
  94.0 3.8 %end.1 = (bf16[128,2048]{1,0:T(8,128)(2,1)}, f32[64,128]{1,0:T(8,128)}, f32[64,128]{1,0:T(8,128)}, f32[32,128]{1,0:T(8,128)}, f32[128,256]{1,0:T(8,128)}) custom-call(bf16[128,2048]{1,0:T(8,128)(2,1)S(1)} %copy-done.1, f32[64,128]{1,0:T(8,128)S(1)} %bitcast.9, f32[32,128]{1,0:T(8,128)S(1)} %get-tuple-element.18.crow_ref, ...), custom_call_target="tpu_custom_call" | custom-call | tf_op jit(solution)/shard_map/end/pallas_call | solution.py:904
Async XLA Ops:
  0.6 0.7 copy-start.8
  1.3 1.0 %copy-start = (bf16[128,2048]{1,0:T(8,128)(2,1)S(1)}, bf16[128,2048]{1,0:T(8,128)(2,1)}, u32[]{:S(2)}) copy-start(bf16[128,2048]{1,0:T(8,128)(2,1)} %v_ref.1) | copy-start | bytes 1572868
  2.3 1.2 %copy-start.2 = (f32[32,64,64]{2,1,0:T(8,128)S(1)}, f32[32,64,64]{2,1,0:T(8,128)}, u32[]{:S(2)}) copy-start(f32[32,64,64]{2,1,0:T(8,128)} %param.15) | copy-start | bytes 1572868
  3.6 1.0 %copy-start.3 = (bf16[128,2048]{1,0:T(8,128)(2,1)S(1)}, bf16[128,2048]{1,0:T(8,128)(2,1)}, u32[]{:S(2)}) copy-start(bf16[128,2048]{1,0:T(8,128)(2,1)} %do_any.1) | copy-start | bytes 1572868
  4.6 0.8 copy-start.4
  5.4 0.9 copy-start.5
  6.3 0.8 copy-start.6
  7.0 0.7 copy-start.7
  7.7 86.2 %copy-start.1 = (bf16[128,2048]{1,0:T(8,128)(2,1)S(1)}, bf16[128,2048]{1,0:T(8,128)(2,1)}, u32[]{:S(2)}) copy-start(bf16[128,2048]{1,0:T(8,128)(2,1)} %v_ref.1) | copy-start | bytes 1572868

commit v3 on v2

--- a/solution.py
+++ b/solution.py
@@ -85,6 +85,24 @@
 
 def bit_of(x, b):
     return (x // 2**b) % 2 == 1
+
+
+def routes_of(nb, nz, xdim, ydim):
+    routes, slot = [], 0
+    for lev in range(nb + nz):
+        ybits = log2(ydim)
+        rows_first = lev < ybits or lev == nb
+        first, second = (xdim, ydim) if rows_first else (ydim, xdim)
+        if lev < nb:
+            bit = lev if rows_first else lev - ybits
+            users = [s for s in range(second) if (s >> bit) & 1]
+            arrays = [[s for s in users if s >> (bit + 1) == a] for a in range(second >> (bit + 1))]
+        else:
+            users = list(range(second))
+            arrays = [users]
+        routes.append((rows_first, first, second, users, arrays, slot))
+        slot += len(arrays)
+    return routes
 
 
 def main_kernel(
@@ -119,9 +137,11 @@
     lam_t,
     glam,
     rint,
+    rnear,
     dq_acc,
     dsc,
     g,
+    gn,
     own,
     dec,
     sib,
@@ -130,26 +150,34 @@
     nd,
     zb,
     hz,
-    stage,
-    pin,
+    pks,
+    pk,
     coef,
+    ring,
     h,
     x,
     st,
-    rb,
+    back,
+    q_sum,
+    parts,
+    rs,
+    rr,
     u,
     zu,
     ct,
     cown,
     dn,
-    rt,
-    out,
+    carry_out,
+    carry_in,
     ds,
     g0,
     s_sem,
     a_sem,
     z_send,
     z_recv,
+    k_sem,
+    r_send,
+    r_recv,
     h_send,
     h_recv,
     f_send,
@@ -159,6 +187,9 @@
     x_recv,
     b_send,
     b_recv,
+    q_send,
+    q_recv,
+    t_sem,
     u_send,
     u_recv,
     c_send,
@@ -182,11 +213,10 @@
     wide = min(128, columns * heads)
     per = wide // heads
 
+    routes = routes_of(nb, nz, xdim, ydim)
+
     def shifted(i):
         return ((xpos + i // ydim) % xdim) * ydim + (ypos + i % ydim) % ydim
-
-    def mine(lev):
-        return bit_of(chip, lev) if lev < nb else bit_of(group, lev - nb)
 
     def near(src, dst, send, recv):
         return remote(src, dst, send, recv, (group, mate))
@@ -349,41 +379,108 @@
                 (group - d, me),
             ).start()
 
+    sub = iota((8, 128), 0)
     for c in range(chips):
-        pre = None
+        pre = jnp.ones((8, 128), F32)
+        rows = pre
         for b in range(nb):
+            rows = jnp.where(sub >= b, pre, rows)
             if (c >> b) & 1:
-                left = offs[b] + (c >> b) - 1
-                far = nd[left, 0:4]
-                stage[c, b] = far if pre is None else pre[None] * far
-                pre = nd[left, 4] if pre is None else pre * nd[left, 4]
-        pin[c] = jnp.ones((8, 128), F32) if pre is None else pre
-
-    def send_level(lev, to):
+                pre = pre * nd[offs[b] + (c >> b) - 1, 4]
+        pks[c] = jnp.where(sub >= nb, pre, rows)
+
+    def send_scales(i):
+        to = shifted(i)
         remote(
-            stage.at[to, lev],
-            h.at[lev, chip, core],
-            h_send.at[lev],
-            h_recv.at[lev],
-            (group, 2 * to + core),
+            pks.at[to], pk.at[chip], k_sem.at[0], k_sem.at[1], (group, 2 * to + core)
         ).start()
 
-    def send_low(i):
-        to = shifted(i)
-        for b in reversed(range(nb)):
-
-            @pl.when(bit_of(to, b))
-            def _():
-                send_level(b, to)
-
-    loop(1, chips, send_low)
-    for b in range(nb):
-
-        @pl.when(bit_of(chip, b))
-        def _():
-            h[b, chip, core] = stage[chip, b]
-
-    for p in range(pairs // 2, pairs):
+    loop(1, chips, send_scales)
+    pk[chip] = pks[chip]
+
+    def where_on(lev):
+        rows_first, first, second, users, arrays, slot = routes[lev]
+        if rows_first:
+            return xpos, ypos, lambda f, s: f * ydim + s
+        return ypos, xpos, lambda f, s: s * ydim + f
+
+    def reads(lev):
+        if lev >= nb:
+            return bit_of(group, lev - nb)
+        return bit_of(chip, lev)
+
+    def when_level(lev, fn):
+        if lev >= nb:
+            pl.when(bit_of(group, lev - nb))(fn)
+        else:
+            fn()
+
+    def first_phase(lev):
+        rows_first, first, second, users, arrays, slot = routes[lev]
+        fpos, spos, at = where_on(lev)
+
+        def source(a, f):
+            if lev >= nb:
+                return hz.at[lev - nb]
+            if rows_first:
+                return nd.at[offs[lev] + f * (ydim >> lev) + 2 * a, 0:4]
+            return nd.at[offs[lev] + 2 * a, 0:4]
+
+        def go():
+            for d in range(1, first):
+                f = (fpos + d) % first
+                for a in range(len(arrays)):
+                    remote(
+                        source(a, f),
+                        ring.at[slot + a, fpos],
+                        r_send.at[slot + a],
+                        r_recv.at[slot + a],
+                        (group, 2 * at(f, spos) + core),
+                    ).start()
+            for a in range(len(arrays)):
+                ring[slot + a, fpos] = source(a, fpos)[...]
+
+        when_level(lev, go)
+
+    def second_phase(lev):
+        rows_first, first, second, users, arrays, slot = routes[lev]
+        fpos, spos, at = where_on(lev)
+
+        def go():
+            if first > 1:
+                for a in range(len(arrays)):
+                    part = ring.at[slot + a, pl.ds(0, first - 1)]
+                    near(part, part, r_send.at[slot + a], r_recv.at[slot + a]).wait_recv()
+            for a, readers in enumerate(arrays):
+                for s in readers:
+                    there = h.at[lev, core, pl.ds(spos * first, first)]
+
+                    @pl.when(spos != s)
+                    def _():
+                        remote(
+                            ring.at[slot + a, pl.ds(0, first)],
+                            there,
+                            h_send.at[lev],
+                            h_recv.at[lev],
+                            (group, 2 * at(fpos, s) + core),
+                        ).start()
+
+                    @pl.when(spos == s)
+                    def _():
+                        there[...] = ring[slot + a, 0:first]
+
+        when_level(lev, go)
+
+    low = list(range(nb))
+    high = list(range(nb, levels))
+    for lev in low:
+        first_phase(lev)
+
+    for p in range(pairs // 2, 3 * pairs // 4):
+        inside(p)
+    for lev in low:
+        second_phase(lev)
+    for p in range(3 * pairs // 4, pairs):
         inside(p)
 
     coef[...] = jnp.ones((8, 128), F32)
@@ -399,16 +496,8 @@
             hz[level] = hz[level] + coef[...][None] * zb[far, 0:4]
             coef[...] = coef[...] * zb[far, 4]
 
-    for l in range(nz):
-
-        @pl.when(bit_of(group, l))
-        def _():
-            def fill(c):
-                stage[c, nb + l] = pin[c][None] * hz[l]
-
-            loop(0, chips, fill)
-            loop(1, chips, lambda i: send_level(nb + l, shifted(i)))
-            h[nb + l, chip, core] = stage[chip, nb + l]
+    for lev in high:
+        first_phase(lev)
 
     q_low = qt.astype(BF16).astype(F32)
     q2 = jnp.concatenate([q_low, q_low], axis=1)
@@ -419,24 +508,34 @@
         )
     glam[...] = jnp.zeros(glam.shape, F32)
     rint[...] = jnp.zeros(rint.shape, F32)
+    rnear[...] = jnp.zeros(rnear.shape, F32)
     dq_acc[...] = jnp.zeros(dq_acc.shape, F32)
     ids = [ids_ref[0, b] for b in range(1 + levels)]
 
+    def spot(lev, p):
+        if routes[lev][0]:
+            return (p % ydim) * xdim + p // ydim
+        return p
+
     def levels_step(group_levels, p):
         gr2 = jnp.exp(crow_ref[pl.ds(2 * p, 2), :])
-        scale = jnp.where(core == 1, sibd[p, 0:1], jnp.ones((1, 128), F32))
-        helds, ws = [], []
+        mate_scale = jnp.where(core == 1, sibd[p, 0:1], jnp.ones((1, 128), F32))
+        helds, ws, scales = [], [], []
         for b in group_levels:
             if b == 0:
                 held = sib[p].reshape(64, 128)
+                scales.append(None)
             else:
-                held = jnp.where(mine(b - 1), h[b - 1, p].reshape(64, 128) * scale, 0.0)
+                scales.append(mate_scale * pk[p, b - 1 : b])
+                at = spot(b - 1, p)
+                held = jnp.concatenate([h[b - 1, 0, at], h[b - 1, 1, at]], axis=0)
+                held = jnp.where(reads(b - 1), held.reshape(64, 128) * scales[-1], 0.0)
             helds.append(held.astype(BF16))
             ws.append(lam_t[ids[b], pl.ds(2 * p, 2), :] * gr2)
         m = dot(jnp.concatenate(helds, axis=0), bd_t[p])
         wqs = []
         acc = dq_acc[...]
-        r2 = rint[pl.ds(2 * p, 2), :]
+        r2 = jnp.zeros((2, TOK), F32)
         for i, b in enumerate(group_levels):
             mi = m[64 * i : 64 * (i + 1)]
             w = jnp.concatenate([ws[i][0:1], ws[i][1:2]], axis=1)
@@ -447,11 +546,20 @@
             glam[b, pl.ds(2 * p, 2), :] = gr2 * g2
             r2 = r2 + ws[i] * g2
         dq_acc[...] = acc
-        rint[pl.ds(2 * p, 2), :] = r2
+        if group_levels == [0]:
+            rnear[pl.ds(2 * p, 2), :] = r2
+        else:
+            rint[pl.ds(2 * p, 2), :] += r2
         grad = dot(jnp.concatenate(wqs, axis=0), bd[p])
         for i, b in enumerate(group_levels):
             gi = grad[64 * i : 64 * (i + 1)]
-            g[b, p] = (gi if b == 0 else gi * scale).reshape(2, 4, 8, 128)
+            if b == 0:
+                gn[p] = gi.reshape(2, 4, 8, 128)
+            else:
+                gi = (gi * scales[i]).reshape(2, 4, 8, 128)
+                at = spot(b - 1, p)
+                g[b - 1, 0, at] = gi[0]
+                g[b - 1, 1, at] = gi[1]
 
     def levels_pass(group_levels):
         def two(i):
@@ -460,7 +568,7 @@
 
         loop(0, pairs // 2, two)
 
-    g0_copy = near(g.at[0], g0, g0_sem.at[0], g0_sem.at[1])
+    g0_copy = near(gn, g0, g0_sem.at[0], g0_sem.at[1])
 
     @pl.when(core == 1)
     def _():
@@ -468,59 +576,112 @@
         levels_pass([0])
         g0_copy.start()
 
+    for lev in high:
+        second_phase(lev)
+
     def swap(lev):
-        return near(g.at[lev + 1, :, 1 - core], x.at[lev], x_send.at[lev], x_recv.at[lev])
+        return near(g.at[lev, 1 - core], x.at[lev], x_send.at[lev], x_recv.at[lev])
 
     def fetch(levs):
         for lev in levs:
-
-            @pl.when(mine(lev))
+            rows_first, first, second, users, arrays, slot = routes[lev]
+
+            @pl.when(reads(lev))
             def _():
-                part = h.at[lev, pl.ds(0, chips - 1), core]
-                near(part, part, h_send.at[lev], h_recv.at[lev]).wait_recv()
-                ours = h.at[lev, :, core]
+                if second > 1:
+                    part = h.at[lev, core, pl.ds(0, (second - 1) * first)]
+                    near(part, part, h_send.at[lev], h_recv.at[lev]).wait_recv()
+                ours = h.at[lev, core]
                 near(ours, ours, f_send.at[lev], f_recv.at[lev]).start()
 
         for lev in levs:
 
-            @pl.when(mine(lev))
+            @pl.when(reads(lev))
             def _():
-                theirs = h.at[lev, :, 1 - core]
+                theirs = h.at[lev, 1 - core]
                 near(theirs, theirs, f_send.at[lev], f_recv.at[lev]).wait_recv()
 
     def give_back(levs):
         for lev in levs:
 
-            @pl.when(mine(lev))
+            @pl.when(reads(lev))
             def _():
                 swap(lev).start()
 
         for lev in levs:
-
-            @pl.when(mine(lev))
+            rows_first, first, second, users, arrays, slot = routes[lev]
+            fpos, spos, at = where_on(lev)
+
+            @pl.when(reads(lev))
             def _():
                 swap(lev).wait_recv()
 
                 def add(c):
-                    st[lev, c] = g[lev + 1, c, core] + x[lev, c]
+                    st[lev, c] = g[lev, core, c] + x[lev, c]
 
                 loop(0, chips, add)
-
-                def send(i):
-                    to = shifted(i)
+                for d in range(1, second):
+                    s = (spos + d) % second
                     remote(
-                        st.at[lev, to],
-                        rb.at[lev, chip],
+                        st.at[lev, pl.ds(s * first, first)],
+                        back.at[lev, spos, pl.ds(0, first)],
                         b_send.at[lev],
                         b_recv.at[lev],
-                        (group, 2 * to + core),
+                        (group, 2 * at(fpos, s) + core),
                     ).start()
-
-                loop(1, chips, send)
-                rb[lev, chip] = st[lev, chip]
-
-    low = list(range(nb))
-    high = list(range(nb, levels))
+                back[lev, spos, 0:first] = st[lev, pl.ds(spos * first, first)]
+
+    def gather_back(lev):
+        rows_first, first, second, users, arrays, slot = routes[lev]
+        fpos, spos, at = where_on(lev)
+
+        def arrived(count):
+            if count:
+                part = back.at[lev, pl.ds(0, count), pl.ds(0, first)]
+                near(part, part, b_send.at[lev], b_recv.at[lev]).wait_recv()
+
+        def go():
+            if lev >= nb:
+                arrived(second - 1)
+            else:
+
+                @pl.when(reads(lev))
+                def _():
+                    arrived(len(users) - 1)
+
+                @pl.when(jnp.logical_not(reads(lev)))
+                def _():
+                    arrived(len(users))
+
+            for a, readers in enumerate(arrays):
+                for f in range(first):
+                    total = back[lev, readers[0], f]
+                    for s in readers[1:]:
+                        total = total + back[lev, s, f]
+                    q_sum[slot + a, f] = total
+                for d in range(1, first):
+                    f = (fpos + d) % first
+                    remote(
+                        q_sum.at[slot + a, f],
+                        parts.at[slot + a, fpos],
+                        q_send.at[slot + a],
+                        q_recv.at[slot + a],
+                        (group, 2 * at(f, spos) + core),
+                    ).start()
+                parts[slot + a, fpos] = q_sum[slot + a, fpos]
+
+        when_level(lev, go)
+
+    def parts_in(lev):
+        rows_first, first, second, users, arrays, slot = routes[lev]
+        if first > 1:
+            for a in range(len(arrays)):
+                part = parts.at[slot + a, pl.ds(0, first - 1)]
+                near(part, part, q_send.at[slot + a], q_recv.at[slot + a]).wait_recv()
+
+    k_part = pk.at[pl.ds(0, chips - 1)]
+    scales_in = near(k_part, k_part, k_sem.at[0], k_sem.at[1])
+    scales_in.wait_recv()
     fetch(low)
     levels_pass([b + 1 for b in low])
     give_back(low)
@@ -531,41 +692,53 @@
         levels_pass([b + 1 for b in high])
 
     give_back(high)
+
+    r = rint[...]
+    rsum = jnp.broadcast_to(jnp.sum(r, axis=1, keepdims=True), (heads, TOK))
+    lane = iota((8, 128), 1)
+    first_lane = jnp.where((sub == 0) & (lane == 0), 1.0, 0.0)
+    mid_lane = jnp.where((sub == 0) & (lane == 64), 1.0, 0.0)
+    for p in range(pairs):
+        rs[p] = first_lane * rsum[2 * p : 2 * p + 1] + mid_lane * rsum[2 * p + 1 : 2 * p + 2]
+
+    def send_sums(i):
+        to = shifted(i)
+        remote(
+            rs.at[to], rr.at[chip], t_sem.at[0], t_sem.at[1], (group, 2 * to + core)
+        ).start()
+
+    loop(1, chips, send_sums)
+    rr[chip] = rs[chip]
+    for lev in low:
+        gather_back(lev)
 
     for p in range(columns):
         total = jnp.zeros((heads, TOK), F32)
         for b in range(1 + levels):
             total = total + jnp.where(ids[b] == p, glam[b], 0.0)
         dlam_ref[p] = total
-    r = rint[...]
     even = jnp.where(core == 0, 1.0, 0.0)
-    dlogt_ref[...] += dot(r, (row >= col).astype(F32), precision=highest) - even * jnp.sum(
-        r, axis=1, keepdims=True
+    dlogt_ref[...] += (
+        dot(r + rnear[...], (row >= col).astype(F32), precision=highest) - even * rsum
     )
     dqi = (dq_acc[:, 0:128] + dq_acc[:, 128:256]).astype(BF16).astype(F32)
     dst = dsc[...]
     dqt_ref[...] = dqi + dot(kt, dst, precision=highest)
     dkt_ref[...] = dot(dst, q, precision=highest).T
 
-    def arrived(lev, count):
-        part = rb.at[lev, pl.ds(0, count)]
-        near(part, part, b_send.at[lev], b_recv.at[lev]).wait_recv()
-
-    lefts = [
-        [(b, offs[b] + (c >> b) - 1) for b in range(nb) if (c >> b) & 1] for c in range(chips)
-    ]
-    rt[...] = jnp.zeros(rt.shape, F32)
-    for l in range(nz):
-
-        @pl.when(bit_of(group, l))
+    for lev in high:
+        gather_back(lev)
+
+    for lev in high:
+        first, slot = routes[lev][1], routes[lev][5]
+
+        @pl.when(reads(lev))
         def _():
-            arrived(nb + l, chips - 1)
-            total = jnp.zeros((4, 8, 128), F32)
-            for c in range(chips):
-                w = pin[c][None] * rb[nb + l, c]
-                total = total + w
-                rt[c] = rt[c] + jnp.sum(w * hz[l], axis=0)
-            u[l] = total
+            parts_in(lev)
+            total = parts[slot, 0]
+            for f in range(1, first):
+                total = total + parts[slot, f]
+            u[lev - nb] = total
 
     for d in range(1, groups):
 
@@ -576,29 +749,18 @@
                 u.at[level], zu.at[group], u_send.at[d], u_recv.at[group], (group - d, me)
             ).start()
 
-    for b in range(nb):
-
-        @pl.when(bit_of(chip, b))
-        def _():
-            if chips // 2 > 1:
-                arrived(b, chips // 2 - 1)
-
-        @pl.when(jnp.logical_not(bit_of(chip, b)))
-        def _():
-            arrived(b, chips // 2)
-
-    for b in range(nb):
-        for i in range(0, chips >> b, 2):
-            left = offs[b] + i
-            total = None
-            for c in range((i + 1) << b, (i + 2) << b):
-                w = rb[b, c]
-                for bb, node in lefts[c]:
-                    if bb < b:
-                        w = nd[node, 4][None] * w
-                rt[c] = rt[c] + jnp.sum(w * nd[left, 0:4], axis=0)
-                total = w if total is None else total + w
-            dn[left] = total
+    for lev in low:
+        rows_first, first, second, users, arrays, slot = routes[lev]
+        parts_in(lev)
+        for a in range(len(arrays)):
+            if rows_first:
+                for f in range(first):
+                    dn[offs[lev] + f * (ydim >> lev) + 2 * a] = parts[slot + a, f]
+            else:
+                total = parts[slot + a, 0]
+                for f in range(1, first):
+                    total = total + parts[slot + a, f]
+                dn[offs[lev] + 2 * a] = total
 
     coef[...] = jnp.ones((8, 128), F32)
     dn[top] = jnp.zeros((4, 8, 128), F32)
@@ -636,13 +798,18 @@
             dn[left] = dn[left] + nd[left + 1, 4][None] * parent
             dn[left + 1] = parent
 
-    carry = jnp.zeros((8, 128), F32)
-    for c in range(chips):
-        out[c, 0:4] = dn[c]
-        out[c, 4] = carry
-        carry = carry + jnp.sum(nd[c, 0:4] * dn[c], axis=0) - rt[c]
-        out[c, 5] = carry
-
+    def give(i):
+        to = shifted(i)
+        remote(
+            dn.at[to], ds.at[core, chip], o_sem.at[0], o_sem.at[1], (group, 2 * to + core)
+        ).start()
+
+    loop(1, chips, give)
+    ds[core, chip] = dn[chip]
+
+    t_part = rr.at[pl.ds(0, chips - 1)]
+    sums_in = near(t_part, t_part, t_sem.at[0], t_sem.at[1])
+    sums_in.wait_recv()
     coef[...] = jnp.zeros((8, 128), F32)
     for d in range(1, groups):
 
@@ -652,48 +819,64 @@
             near(slot, slot, c_send.at[d], c_recv.at[group - d]).wait_recv()
             coef[...] = coef[...] + ct[group - d]
 
-    def carry_in(c):
-        out[c, 4:6] = out[c, 4:6] + coef[...][None]
-
-    loop(0, chips, carry_in)
-
-    def give(i):
+    carry = coef[...]
+    for c in range(chips):
+        carry_out[c, 0] = carry
+        carry = carry + jnp.sum(nd[c, 0:4] * dn[c], axis=0) - rr[c]
+        carry_out[c, 1] = carry
+
+    def give_carry(i):
         to = shifted(i)
         remote(
-            out.at[to], ds.at[chip, core], o_sem.at[0], o_sem.at[1], (group, 2 * to + core)
+            carry_out.at[to], carry_in.at[core, chip], o_sem.at[2], o_sem.at[3], (group, 2 * to + core)
         ).start()
 
-    loop(1, chips, give)
-    ds[chip, core] = out[chip]
-    part = ds.at[pl.ds(0, chips - 1), core]
+    loop(1, chips, give_carry)
+    carry_in[core, chip] = carry_out[chip]
+    part = ds.at[core, pl.ds(0, chips - 1)]
     given = near(part, part, o_sem.at[0], o_sem.at[1])
     given.wait_recv()
-    ours = ds.at[:, core]
-    near(ours, ours, w_sem.at[0], w_sem.at[1]).start()
-
-    def sent(lev, count):
-        left = stage.at[pl.ds(0, count), lev]
-        near(left, left, h_send.at[lev], h_recv.at[lev]).wait_send()
+    near(ds.at[core], ds.at[core], w_sem.at[0], w_sem.at[1]).start()
+    c_part = carry_in.at[core, pl.ds(0, chips - 1)]
+    carried = near(c_part, c_part, o_sem.at[2], o_sem.at[3])
+    carried.wait_recv()
+    near(carry_in.at[core], carry_in.at[core], w_sem.at[2], w_sem.at[3]).start()
 
     for lev in range(levels):
-
-        @pl.when(mine(lev))
+        rows_first, first, second, users, arrays, slot = routes[lev]
+
+        def out_of_ring(count):
+            if count:
+                part = h.at[lev, core, pl.ds(0, count * first)]
+                near(part, part, h_send.at[lev], h_recv.at[lev]).wait_send()
+
+        def sends():
+            if first > 1:
+                for a in range(len(arrays)):
+                    part = ring.at[slot + a, pl.ds(0, first - 1)]
+                    near(part, part, r_send.at[slot + a], r_recv.at[slot + a]).wait_send()
+                    near(part, part, q_send.at[slot + a], q_recv.at[slot + a]).wait_send()
+            if lev >= nb:
+                out_of_ring(second - 1)
+
+        when_level(lev, sends)
+
+        if lev < nb:
+
+            @pl.when(jnp.logical_not(reads(lev)))
+            def _():
+                out_of_ring(len(users))
+
+        @pl.when(reads(lev))
         def _():
-            ours = h.at[lev, :, core]
+            if lev < nb:
+                out_of_ring(len(users) - 1)
+            ours = h.at[lev, core]
             near(ours, ours, f_send.at[lev], f_recv.at[lev]).wait_send()
             swap(lev).wait_send()
-            part = st.at[lev, pl.ds(0, chips - 1)]
-            near(part, part, b_send.at[lev], b_recv.at[lev]).wait_send()
-            if lev >= nb:
-                sent(lev, chips - 1)
-            elif chips // 2 > 1:
-                sent(lev, chips // 2 - 1)
-
-        if lev < nb:
-
-            @pl.when(jnp.logical_not(mine(lev)))
-            def _():
-                sent(lev, chips // 2)
+            if second > 1:
+                part = st.at[lev, pl.ds(0, (second - 1) * first)]
+                near(part, part, b_send.at[lev], b_recv.at[lev]).wait_send()
 
     for d in range(1, groups):
 
@@ -711,6 +894,9 @@
     swap_half.wait_send()
     swap_dec.wait_send()
     scattered.wait_send()
+    scales_in.wait_send()
+    sums_in.wait_send()
+    carried.wait_send()
 
     @pl.when(core == 1)
     def _():
@@ -722,19 +908,27 @@
         g0_copy.wait_recv()
 
     given.wait_send()
-    theirs = ds.at[:, 1 - core]
+    theirs = ds.at[1 - core]
     both = near(theirs, theirs, w_sem.at[0], w_sem.at[1])
     both.wait_recv()
     both.wait_send()
+    theirs = carry_in.at[1 - core]
+    both = near(theirs, theirs, w_sem.at[2], w_sem.at[3])
+    both.wait_recv()
+    both.wait_send()
 
     def finish(p):
-        grad = ds[p, :, 0:4]
-        dot_own = jnp.sum(own[p] * grad, axis=1)
-        dld = jnp.where(core == 0, ds[p, :, 4], ds[p, :, 5] - dot_own)
-        dld_ref[p] = dld[0] + dld[1]
         scale = jnp.where(core == 0, sibd[p], jnp.ones((8, 128), F32))
-        extra = jnp.where(core == 0, g0[p], 0.0)
-        low_ref[p] = (grad * scale[None, None] + extra).reshape(64, 128).astype(BF16)
+        dld = jnp.zeros((8, 128), F32)
+        for j in range(2):
+            grad = ds[j, p]
+            dot_own = jnp.sum(own[p, j] * grad, axis=0)
+            dld = dld + jnp.where(core == 0, carry_in[j, p, 0], carry_in[j, p, 1] - dot_own)
+            extra = jnp.where(core == 0, g0[p, j], 0.0)
+            low_ref[p, 32 * j : 32 * (j + 1)] = (
+                (grad * scale[None] + extra).reshape(32, 128).astype(BF16)
+            )
+        dld_ref[pl.ds(p, 1), :] = jnp.sum(dld, axis=0, keepdims=True)
 
     loop(0, pairs, finish)
 
@@ -767,7 +961,6 @@
     k_low = kt_ref[...].T.astype(BF16)
     dk = jnp.zeros((64, TOK), F32)
     ls = jnp.zeros((TOK, heads), F32)
-    dd = jnp.zeros((8, heads), F32)
     lane_row = iota((TOK, heads), 0)
     lane_col = iota((TOK, heads), 1)
     for p in range(pairs):
@@ -783,13 +976,14 @@
         )
         dv_ref[:, sl] = (dvp_ref[:, sl] + dvs).astype(BF16)
         ls += dot((vp * dvs).astype(BF16), pick.astype(BF16))
-        dd += dot(dld_ref[p], pick, precision=highest)
     dk_ref[...] = dkp_ref[...] + dk
     dq_ref[...] = dqp_ref[...]
     strict = (row > col).astype(F32)
-    dlog_ref[...] = dlogp_ref[...] + (
-        dot(strict, ls, precision=highest) + jnp.sum(dd, axis=0, keepdims=True)
-    ).T
+    head = iota((heads, pairs), 0)
+    rows = dot((iota((heads, pairs), 1) == head // 2).astype(F32), dld_ref[...], precision=highest)
+    side = iota((heads, TOK), 1) // 64 == iota((heads, TOK), 0) % 2
+    dd = jnp.sum(jnp.where(side, rows, 0.0), axis=1, keepdims=True)
+    dlog_ref[...] = dlogp_ref[...] + dot(strict, ls, precision=highest).T + dd
     wide = min(128, columns * heads)
     per = wide // heads
     for j in range(columns // per):
@@ -811,6 +1005,9 @@
     dma = pltpu.SemaphoreType.DMA
     tile = (4, 8, 128)
     kt = state_input.T
+    ydim = 2 ** ((nb + 1) // 2)
+    routes = routes_of(nb, nz, chips // ydim, ydim)
+    slots = sum(len(route[4]) for route in routes)
 
     dv, dqt, dkt, dlam, dlogt, crow, low, dld = pl.pallas_call(
         partial(main_kernel, shards, groups),
@@ -822,10 +1019,10 @@
             f32(heads, TOK),
             f32(heads, TOK),
             jax.ShapeDtypeStruct((chips, 64, 128), BF16),
-            f32(chips, 8, 128),
+            f32(chips, 128),
         ),
         in_specs=[pl.BlockSpec(memory_space=pltpu.SMEM)]
-        + [pl.BlockSpec(memory_space=pl.ANY)] * 7,
+        + [pl.BlockSpec(memory_space=pltpu.HBM)] * 7,
         out_specs=(vmem(),) * 8,
         scratch_shapes=[
             pltpu.VMEM((TOK, heads * 64), BF16),
@@ -841,9 +1038,11 @@
             pltpu.VMEM((columns, heads, TOK), F32),
             pltpu.VMEM((1 + levels, heads, TOK), F32),
             pltpu.VMEM((heads, TOK), F32),
+            pltpu.VMEM((heads, TOK), F32),
             pltpu.VMEM((64, 256), F32),
             pltpu.VMEM((TOK, TOK), F32),
-            pltpu.VMEM((1 + levels, chips, 2) + tile, F32),
+            pltpu.VMEM((levels, 2, chips) + tile, F32),
+            pltpu.VMEM((chips, 2) + tile, F32),
             pltpu.VMEM((chips, 2) + tile, F32),
             pltpu.VMEM((chips, 8, 128), F32),
             pltpu.VMEM((chips, 2) + tile, F32),
@@ -852,26 +1051,34 @@
             pltpu.VMEM((2 * chips, 5, 8, 128), F32),
             pltpu.VMEM((groups, 5, 8, 128), F32),
             pltpu.VMEM((nz,) + tile, F32),
-            pltpu.VMEM((chips, levels) + tile, F32),
+            pltpu.VMEM((chips, 8, 128), F32),
             pltpu.VMEM((chips, 8, 128), F32),
             pltpu.VMEM((8, 128), F32),
-            pltpu.VMEM((levels, chips, 2) + tile, F32),
+            pltpu.VMEM((slots, ydim) + tile, F32),
+            pltpu.VMEM((levels, 2, chips) + tile, F32),
             pltpu.VMEM((levels, chips) + tile, F32),
             pltpu.VMEM((levels, chips) + tile, F32),
-            pltpu.VMEM((levels, chips) + tile, F32),
+            pltpu.VMEM((levels, ydim, ydim) + tile, F32),
+            pltpu.VMEM((slots, ydim) + tile, F32),
+            pltpu.VMEM((slots, ydim) + tile, F32),
+            pltpu.VMEM((chips, 8, 128), F32),
+            pltpu.VMEM((chips, 8, 128), F32),
             pltpu.VMEM((nz,) + tile, F32),
             pltpu.VMEM((groups,) + tile, F32),
             pltpu.VMEM((groups, 8, 128), F32),
             pltpu.VMEM((8, 128), F32),
             pltpu.VMEM((2 * chips,) + tile, F32),
-            pltpu.VMEM((chips, 8, 128), F32),
-            pltpu.VMEM((chips, 6, 8, 128), F32),
-            pltpu.VMEM((chips, 2, 6, 8, 128), F32),
+            pltpu.VMEM((chips, 2, 8, 128), F32),
+            pltpu.VMEM((2, chips, 2, 8, 128), F32),
+            pltpu.VMEM((2, chips) + tile, F32),
             pltpu.VMEM((chips, 2) + tile, F32),
             dma((6,)),
             dma((2,)),
             dma((2 * groups,)),
             dma((groups,)),
+            dma((2,)),
+            dma((slots,)),
+            dma((slots,)),
             dma((levels,)),
             dma((levels,)),
             dma((levels,)),
@@ -881,12 +1088,15 @@
             dma((levels,)),
             dma((levels,)),
             dma((levels,)),
+            dma((slots,)),
+            dma((slots,)),
+            dma((2,)),
             dma((groups,)),
             dma((groups,)),
             dma((groups,)),
             dma((groups,)),
-            dma((2,)),
-            dma((2,)),
+            dma((4,)),
+            dma((4,)),
         ],
         compiler_params=params(collective_id=0, has_side_effects=True),
         name="main",

time: 99 us -> 84.9 us (0.86)
  Pallas kernels: 90 us -> 76.7 us
    pallas_call x1, Pallas kernels: 86.2 us -> 73.4 us  [body(): pl.pallas_call(partial(main_kernel, shards, groups), out_shape=(f32(TOK,...]
where the time goes in v3:
time: 84.9 us; the launch traced here: 84.5 us
  Pallas kernels  76.7 us (90%)
  local copies, waits for them, and re-layouts  7.09 us (8%)
    pallas_call x1, Pallas kernels, body(): pl.pallas_call(partial(main_kernel, shards, groups), out_shape=(f32(TOK,...  73.4 us
    unnamed x18, local copies, waits for them, and re-layouts  7.09 us
    pallas_call x1, Pallas kernels, body(): pl.pallas_call(end_kernel, out_shape=(jax.ShapeDtypeStruct((TOK, heads *...  3.34 us

profile of v3, /device:TPU:1, one launch (start us, length us, event | category | flops | bytes accessed | tf_op | source)
XLA Modules:
  0.0 84.5 jit_solution(16404473267245537915)
XLA Ops:
  0.6 0.0 copy-start.8
  0.6 0.6 copy-done.8
  1.3 0.0 copy-start
  1.3 1.0 %copy-done = bf16[128,2048]{1,0:T(8,128)(2,1)S(1)} copy-done((bf16[128,2048]{1,0:T(8,128)(2,1)S(1)}, bf16[128,2048]{1,0:T(8,128)(2,1)}, u32[]{:S(2)}) %copy-start) | copy-done | bytes 524312
  2.3 0.0 copy-start.2
  2.3 1.2 %copy-done.2 = f32[32,64,64]{2,1,0:T(8,128)S(1)} copy-done((f32[32,64,64]{2,1,0:T(8,128)S(1)}, f32[32,64,64]{2,1,0:T(8,128)}, u32[]{:S(2)}) %copy-start.2) | copy-done | bytes 524312
  3.6 0.0 copy-start.3
  3.6 1.0 %copy-done.3 = bf16[128,2048]{1,0:T(8,128)(2,1)S(1)} copy-done((bf16[128,2048]{1,0:T(8,128)(2,1)S(1)}, bf16[128,2048]{1,0:T(8,128)(2,1)}, u32[]{:S(2)}) %copy-start.3) | copy-done | bytes 524312
  4.6 0.0 copy-start.4
  4.6 0.8 copy-done.4
  5.4 0.0 copy-start.5
  5.4 0.9 %copy-done.5 = f32[128,256]{1,0:T(8,128)S(1)} copy-done((f32[128,256]{1,0:T(8,128)S(1)}, f32[128,256]{1,0:T(8,128)}, u32[]{:S(2)}) %copy-start.5) | copy-done | bytes 131096
  6.3 0.0 copy-start.6
  6.3 0.8 copy-done.6
  7.0 0.0 copy-start.7
  7.0 0.7 copy-done.7
  7.7 0.0 copy-start.1
  7.7 73.4 %main.1 = (f32[128,2048]{1,0:T(8,128)S(1)}, f32[64,128]{1,0:T(8,128)S(1)}, f32[64,128]{1,0:T(8,128)S(1)}, f32[8,32,128]{2,1,0:T(8,128)S(1)}, f32[32,128]{1,0:T(8...) custom-call(s32[1,8]{1,0:T(1,128)S(1)} %copy-done.8, ...), custom_call_target="tpu_custom_call" | custom-call | tf_op jit(solution)/shard_map/main/pallas_call | solution.py:1012
  81.1 0.0 copy-done.1
  81.2 3.3 %end.1 = (bf16[128,2048]{1,0:T(8,128)(2,1)}, f32[64,128]{1,0:T(8,128)}, f32[64,128]{1,0:T(8,128)}, f32[32,128]{1,0:T(8,128)}, f32[128,256]{1,0:T(8,128)}) custom-call(bf16[128,2048]{1,0:T(8,128)(2,1)S(1)} %copy-done.1, f32[64,128]{1,0:T(8,128)S(1)} %bitcast.9, f32[32,128]{1,0:T(8,128)S(1)} %get-tuple-element.18.crow_ref, ...), custom_call_target="tpu_custom_call" | custom-call | tf_op jit(solution)/shard_map/end/pallas_call | solution.py:1114
Async XLA Ops:
  0.6 0.7 copy-start.8
  1.3 1.0 %copy-start = (bf16[128,2048]{1,0:T(8,128)(2,1)S(1)}, bf16[128,2048]{1,0:T(8,128)(2,1)}, u32[]{:S(2)}) copy-start(bf16[128,2048]{1,0:T(8,128)(2,1)} %v_ref.1) | copy-start | bytes 1572868
  2.3 1.2 %copy-start.2 = (f32[32,64,64]{2,1,0:T(8,128)S(1)}, f32[32,64,64]{2,1,0:T(8,128)}, u32[]{:S(2)}) copy-start(f32[32,64,64]{2,1,0:T(8,128)} %param.15) | copy-start | bytes 1572868
  3.6 1.0 %copy-start.3 = (bf16[128,2048]{1,0:T(8,128)(2,1)S(1)}, bf16[128,2048]{1,0:T(8,128)(2,1)}, u32[]{:S(2)}) copy-start(bf16[128,2048]{1,0:T(8,128)(2,1)} %do_any.1) | copy-start | bytes 1572868
  4.6 0.8 copy-start.4
  5.4 0.9 %copy-start.5 = (f32[128,256]{1,0:T(8,128)S(1)}, f32[128,256]{1,0:T(8,128)}, u32[]{:S(2)}) copy-start(f32[128,256]{1,0:T(8,128)} %lam_any.1) | copy-start | bytes 393220
  6.3 0.8 copy-start.6
  7.0 0.7 copy-start.7
  7.7 73.4 %copy-start.1 = (bf16[128,2048]{1,0:T(8,128)(2,1)S(1)}, bf16[128,2048]{1,0:T(8,128)(2,1)}, u32[]{:S(2)}) copy-start(bf16[128,2048]{1,0:T(8,128)(2,1)} %v_ref.1) | copy-start | bytes 1572868

commit v4 on v3

--- a/solution.py
+++ b/solution.py
@@ -12,15 +12,11 @@
 F32 = jnp.float32
 BF16 = jnp.bfloat16
 TOK = 128
-VMEM_CAP = 48 * 1024 * 1024
+VMEM_CAP = 62 * 1024 * 1024
 
 
 def log2(n):
     return n.bit_length() - 1
-
-
-def vmem():
-    return pl.BlockSpec(memory_space=pltpu.VMEM)
 
 
 def f32(*shape):
@@ -116,6 +112,14 @@
     ldt_any,
     lam_any,
     fu_any,
+    dv_any,
+    dqt_any,
+    dkt_any,
+    dlam_any,
+    dlogt_any,
+    crow_any,
+    low_any,
+    dld_any,
     dv_ref,
     dqt_ref,
     dkt_ref,
@@ -124,6 +128,7 @@
     crow_ref,
     low_ref,
     dld_ref,
+    out_sem,
     v_ref,
     do_ref,
     kt_ref,
@@ -153,6 +158,7 @@
     pks,
     pk,
     coef,
+    before_far,
     ring,
     h,
     x,
@@ -164,11 +170,9 @@
     rr,
     u,
     zu,
-    ct,
+    z_out,
     cown,
     dn,
-    carry_out,
-    carry_in,
     ds,
     g0,
     s_sem,
@@ -192,8 +196,6 @@
     t_sem,
     u_send,
     u_recv,
-    c_send,
-    c_recv,
     o_sem,
     w_sem,
 ):
@@ -237,6 +239,21 @@
     ]
     for c in loads:
         c.start()
+    results = [
+        pltpu.make_async_copy(a, b, out_sem.at[i])
+        for i, (a, b) in enumerate(
+            [
+                (dv_ref, dv_any),
+                (dqt_ref, dqt_any),
+                (dkt_ref, dkt_any),
+                (dlam_ref, dlam_any),
+                (dlogt_ref, dlogt_any),
+                (crow_ref, crow_any),
+                (low_ref, low_any),
+                (dld_ref, dld_any),
+            ]
+        )
+    ]
     wait_entry = enter(group, me, chip, core, chips, groups)
 
     row = iota((TOK, TOK), 0)
@@ -248,6 +265,7 @@
     loads[0].wait()
     crow = dot(ldt_ref[...], upto, precision=highest)
     crow_ref[...] = crow
+    results[5].start()
     last = jnp.broadcast_to(crow[:, TOK - 1 : TOK], (heads, TOK))
     tail = jnp.exp(last - crow)
     full = jnp.exp(last)
@@ -440,7 +458,10 @@
             for a in range(len(arrays)):
                 ring[slot + a, fpos] = source(a, fpos)[...]
 
-        when_level(lev, go)
+        if lev >= nb:
+            go()
+        else:
+            when_level(lev, go)
 
     def second_phase(lev):
         rows_first, first, second, users, arrays, slot = routes[lev]
@@ -482,6 +503,7 @@
         second_phase(lev)
     for p in range(3 * pairs // 4, pairs):
         inside(p)
+    results[0].start()
 
     coef[...] = jnp.ones((8, 128), F32)
     hz[...] = jnp.zeros(hz.shape, F32)
@@ -494,10 +516,14 @@
             near(slot, slot, z_send.at[0], z_recv.at[far]).wait_recv()
             level = high_level(group, far, nz)
             hz[level] = hz[level] + coef[...][None] * zb[far, 0:4]
+            before_far[d] = coef[...]
             coef[...] = coef[...] * zb[far, 4]
 
-    for lev in high:
-        first_phase(lev)
+        l = log2(d)
+
+        @pl.when(bit_of(group, l) & (group % 2**l + 2**l == d))
+        def _():
+            first_phase(nb + l)
 
     q_low = qt.astype(BF16).astype(F32)
     q2 = jnp.concatenate([q_low, q_low], axis=1)
@@ -684,7 +710,6 @@
     scales_in.wait_recv()
     fetch(low)
     levels_pass([b + 1 for b in low])
-    give_back(low)
     fetch(high)
 
     @pl.when(group > 0)
@@ -692,6 +717,7 @@
         levels_pass([b + 1 for b in high])
 
     give_back(high)
+    give_back(low)
 
     r = rint[...]
     rsum = jnp.broadcast_to(jnp.sum(r, axis=1, keepdims=True), (heads, TOK))
@@ -709,6 +735,34 @@
 
     loop(1, chips, send_sums)
     rr[chip] = rs[chip]
+    for lev in high:
+        gather_back(lev)
+
+    for lev in high:
+        first, slot = routes[lev][1], routes[lev][5]
+
+        @pl.when(reads(lev))
+        def _():
+            parts_in(lev)
+            total = parts[slot, 0]
+            for f in range(1, first):
+                total = total + parts[slot, f]
+            u[lev - nb] = total
+
+    coef[...] = jnp.zeros((8, 128), F32)
+    for d in reversed(range(1, groups)):
+
+        @pl.when(group - d >= 0)
+        def _():
+            level = high_level(group, group - d, nz)
+            grad = u[level]
+            z_out[d, 0:4] = grad
+            z_out[d, 4] = coef[...]
+            remote(
+                z_out.at[d], zu.at[group], u_send.at[d], u_recv.at[group], (group - d, me)
+            ).start()
+            coef[...] = coef[...] + before_far[d] * jnp.sum(grad * zb[group - d, 0:4], axis=0)
+
     for lev in low:
         gather_back(lev)
 
@@ -725,29 +779,8 @@
     dst = dsc[...]
     dqt_ref[...] = dqi + dot(kt, dst, precision=highest)
     dkt_ref[...] = dot(dst, q, precision=highest).T
-
-    for lev in high:
-        gather_back(lev)
-
-    for lev in high:
-        first, slot = routes[lev][1], routes[lev][5]
-
-        @pl.when(reads(lev))
-        def _():
-            parts_in(lev)
-            total = parts[slot, 0]
-            for f in range(1, first):
-                total = total + parts[slot, f]
-            u[lev - nb] = total
-
-    for d in range(1, groups):
-
-        @pl.when(group - d >= 0)
-        def _():
-            level = high_level(group, group - d, nz)
-            remote(
-                u.at[level], zu.at[group], u_send.at[d], u_recv.at[group], (group - d, me)
-            ).start()
+    for i in range(1, 5):
+        results[i].start()
 
     for lev in low:
         rows_first, first, second, users, arrays, slot = routes[lev]
@@ -755,15 +788,22 @@
         for a in range(len(arrays)):
             if rows_first:
                 for f in range(first):
-                    dn[offs[lev] + f * (ydim >> lev) + 2 * a] = parts[slot + a, f]
+                    dn[offs[lev] + f * (ydim >> lev) + 2 * a, 0:4] = parts[slot + a, f]
             else:
                 total = parts[slot + a, 0]
                 for f in range(1, first):
                     total = total + parts[slot + a, f]
-                dn[offs[lev] + 2 * a] = total
+                dn[offs[lev] + 2 * a, 0:4] = total
 
     coef[...] = jnp.ones((8, 128), F32)
-    dn[top] = jnp.zeros((4, 8, 128), F32)
+    dn[top, 0:4] = jnp.zeros((4, 8, 128), F32)
+    cown[...] = jnp.zeros((8, 128), F32)
+    for l in range(nz):
+
+        @pl.when(bit_of(group, l))
+        def _():
+            cown[...] = cown[...] + jnp.sum(u[l] * hz[l], axis=0)
+
     for d in range(1, groups):
 
         @pl.when(group + d < groups)
@@ -772,31 +812,33 @@
             near(far, far, z_send.at[0], z_recv.at[group + d]).wait_recv()
             slot = zu.at[group + d]
             near(slot, slot, u_send.at[d], u_recv.at[group + d]).wait_recv()
-            dn[top] = dn[top] + coef[...][None] * zu[group + d]
+            dn[top, 0:4] = dn[top, 0:4] + coef[...][None] * zu[group + d, 0:4]
+            cown[...] = cown[...] + zu[group + d, 4]
             coef[...] = coef[...] * zb[group + d, 4]
 
     loads[6].wait()
     fu = jnp.concatenate([fu_ref[0], fu_ref[1]], axis=1).reshape(4, 8, 128)
-    dn[top] = dn[top] + coef[...][None] * fu
-    cown[...] = jnp.sum(nd[top, 0:4] * dn[top], axis=0)
-    for l in range(nz):
-
-        @pl.when(bit_of(group, l))
-        def _():
-            cown[...] = cown[...] - jnp.sum(u[l] * hz[l], axis=0)
-
-    for d in range(1, groups):
-
-        @pl.when(group + d < groups)
-        def _():
-            remote(cown, ct.at[group], c_send.at[d], c_recv.at[group], (group + d, me)).start()
-
+    dn[top, 0:4] = dn[top, 0:4] + coef[...][None] * fu
+    earlier = hz[0]
+    for l in range(1, nz):
+        earlier = earlier + hz[l]
+    carry = cown[...] + coef[...] * nd[top, 4] * jnp.sum(earlier * fu, axis=0)
     for b in reversed(range(nb)):
         for i in range(0, chips >> b, 2):
             left = offs[b] + i
-            parent = dn[offs[b + 1] + i // 2]
-            dn[left] = dn[left] + nd[left + 1, 4][None] * parent
-            dn[left + 1] = parent
+            parent = dn[offs[b + 1] + i // 2, 0:4]
+            dn[left, 0:4] = dn[left, 0:4] + nd[left + 1, 4][None] * parent
+            dn[left + 1, 0:4] = parent
+
+    t_part = rr.at[pl.ds(0, chips - 1)]
+    sums_in = near(t_part, t_part, t_sem.at[0], t_sem.at[1])
+    sums_in.wait_recv()
+    now = jnp.sum(carry, axis=0, keepdims=True)
+    for c in range(chips):
+        step = jnp.sum(nd[c, 0:4] * dn[c, 0:4], axis=0) - rr[c]
+        then = now + jnp.sum(step, axis=0, keepdims=True)
+        dn[c, 4] = jnp.where(sub == 0, now, jnp.where(sub == 1, then, 0.0))
+        now = then
 
     def give(i):
         to = shifted(i)
@@ -807,40 +849,10 @@
     loop(1, chips, give)
     ds[core, chip] = dn[chip]
 
-    t_part = rr.at[pl.ds(0, chips - 1)]
-    sums_in = near(t_part, t_part, t_sem.at[0], t_sem.at[1])
-    sums_in.wait_recv()
-    coef[...] = jnp.zeros((8, 128), F32)
-    for d in range(1, groups):
-
-        @pl.when(group - d >= 0)
-        def _():
-            slot = ct.at[group - d]
-            near(slot, slot, c_send.at[d], c_recv.at[group - d]).wait_recv()
-            coef[...] = coef[...] + ct[group - d]
-
-    carry = coef[...]
-    for c in range(chips):
-        carry_out[c, 0] = carry
-        carry = carry + jnp.sum(nd[c, 0:4] * dn[c], axis=0) - rr[c]
-        carry_out[c, 1] = carry
-
-    def give_carry(i):
-        to = shifted(i)
-        remote(
-            carry_out.at[to], carry_in.at[core, chip], o_sem.at[2], o_sem.at[3], (group, 2 * to + core)
-        ).start()
-
-    loop(1, chips, give_carry)
-    carry_in[core, chip] = carry_out[chip]
     part = ds.at[core, pl.ds(0, chips - 1)]
     given = near(part, part, o_sem.at[0], o_sem.at[1])
     given.wait_recv()
     near(ds.at[core], ds.at[core], w_sem.at[0], w_sem.at[1]).start()
-    c_part = carry_in.at[core, pl.ds(0, chips - 1)]
-    carried = near(c_part, c_part, o_sem.at[2], o_sem.at[3])
-    carried.wait_recv()
-    near(carry_in.at[core], carry_in.at[core], w_sem.at[2], w_sem.at[3]).start()
 
     for lev in range(levels):
         rows_first, first, second, users, arrays, slot = routes[lev]
@@ -883,20 +895,18 @@
         @pl.when(group + d < groups)
         def _():
             up(d).wait_send()
-            near(cown, cown, c_send.at[d], c_recv.at[0]).wait_send()
 
         @pl.when(group - d >= 0)
         def _():
             line = nd.at[top, 4]
             near(line, line, z_send.at[groups + d], z_recv.at[0]).wait_send()
-            near(u.at[0], u.at[0], u_send.at[d], u_recv.at[0]).wait_send()
+            near(z_out.at[d], z_out.at[d], u_send.at[d], u_recv.at[0]).wait_send()
 
     swap_half.wait_send()
     swap_dec.wait_send()
     scattered.wait_send()
     scales_in.wait_send()
     sums_in.wait_send()
-    carried.wait_send()
 
     @pl.when(core == 1)
     def _():
@@ -912,18 +922,14 @@
     both = near(theirs, theirs, w_sem.at[0], w_sem.at[1])
     both.wait_recv()
     both.wait_send()
-    theirs = carry_in.at[1 - core]
-    both = near(theirs, theirs, w_sem.at[2], w_sem.at[3])
-    both.wait_recv()
-    both.wait_send()
-
     def finish(p):
         scale = jnp.where(core == 0, sibd[p], jnp.ones((8, 128), F32))
         dld = jnp.zeros((8, 128), F32)
         for j in range(2):
-            grad = ds[j, p]
+            grad = ds[j, p, 0:4]
             dot_own = jnp.sum(own[p, j] * grad, axis=0)
-            dld = dld + jnp.where(core == 0, carry_in[j, p, 0], carry_in[j, p, 1] - dot_own)
+            dld = dld + jnp.where(sub == core, ds[j, p, 4], 0.0)
+            dld = dld - jnp.where(core == 0, 0.0, dot_own)
             extra = jnp.where(core == 0, g0[p, j], 0.0)
             low_ref[p, 32 * j : 32 * (j + 1)] = (
                 (grad * scale[None] + extra).reshape(32, 128).astype(BF16)
@@ -931,9 +937,28 @@
         dld_ref[pl.ds(p, 1), :] = jnp.sum(dld, axis=0, keepdims=True)
 
     loop(0, pairs, finish)
+    results[6].start()
+    results[7].start()
+    for c in results:
+        c.wait()
 
 
 def end_kernel(
+    v_any,
+    kt_any,
+    crow_any,
+    low_any,
+    dld_any,
+    dvp_any,
+    dkp_any,
+    dlogp_any,
+    dqp_any,
+    dlamp_any,
+    dv_any,
+    dk_any,
+    dq_any,
+    dlog_any,
+    dlam_any,
     v_ref,
     kt_ref,
     crow_ref,
@@ -942,27 +967,61 @@
     dvp_ref,
     dkp_ref,
     dlogp_ref,
-    dqp_ref,
     dlamp_ref,
     dv_ref,
     dk_ref,
-    dq_ref,
     dlog_ref,
     dlam_ref,
+    in_sem,
+    out_sem,
 ):
     heads = crow_ref.shape[0]
     pairs = heads // 2
     columns = dlamp_ref.shape[0]
+    loads = [
+        pltpu.make_async_copy(a, b, in_sem.at[i])
+        for i, (a, b) in enumerate(
+            [
+                (dlamp_any, dlamp_ref),
+                (crow_any, crow_ref),
+                (kt_any, kt_ref),
+                (low_any, low_ref),
+                (v_any, v_ref),
+                (dvp_any, dvp_ref),
+                (dld_any, dld_ref),
+                (dkp_any, dkp_ref),
+                (dlogp_any, dlogp_ref),
+            ]
+        )
+    ]
+    for c in loads:
+        c.start()
+    through = pltpu.make_async_copy(dqp_any, dq_any, out_sem.at[0])
+    through.start()
     row = iota((TOK, TOK), 0)
     col = iota((TOK, TOK), 1)
     left = col < 64
+    loads[0].wait()
+    wide = min(128, columns * heads)
+    per = wide // heads
+    for j in range(columns // per):
+        dlam_ref[:, j * wide : (j + 1) * wide] = (
+            dlamp_ref[pl.ds(j * per, per)].reshape(wide, TOK).T
+        )
+    lam_out = pltpu.make_async_copy(dlam_ref, dlam_any, out_sem.at[1])
+    lam_out.start()
+    loads[1].wait()
     ccol = crow_ref[...].T
     tail = jnp.exp(ccol[TOK - 1 : TOK, :] - ccol)
+    loads[2].wait()
     k_low = kt_ref[...].T.astype(BF16)
     dk = jnp.zeros((64, TOK), F32)
     ls = jnp.zeros((TOK, heads), F32)
     lane_row = iota((TOK, heads), 0)
     lane_col = iota((TOK, heads), 1)
+    for i in range(3, 9):
+        loads[i].wait()
+    parts = []
     for p in range(pairs):
         sl = slice(p * 128, (p + 1) * 128)
         pick = (lane_col == 2 * p + lane_row // 64).astype(F32)
@@ -976,20 +1035,27 @@
         )
         dv_ref[:, sl] = (dvp_ref[:, sl] + dvs).astype(BF16)
         ls += dot((vp * dvs).astype(BF16), pick.astype(BF16))
+        if (p + 1) % (pairs // 2) == 0:
+            cols = pl.ds((p + 1 - pairs // 2) * 128, pairs // 2 * 128)
+            parts.append(
+                pltpu.make_async_copy(
+                    dv_ref.at[:, cols], dv_any.at[:, cols], out_sem.at[4 + len(parts)]
+                )
+            )
+            parts[-1].start()
     dk_ref[...] = dkp_ref[...] + dk
-    dq_ref[...] = dqp_ref[...]
+    k_out = pltpu.make_async_copy(dk_ref, dk_any, out_sem.at[2])
+    k_out.start()
     strict = (row > col).astype(F32)
     head = iota((heads, pairs), 0)
     rows = dot((iota((heads, pairs), 1) == head // 2).astype(F32), dld_ref[...], precision=highest)
     side = iota((heads, TOK), 1) // 64 == iota((heads, TOK), 0) % 2
     dd = jnp.sum(jnp.where(side, rows, 0.0), axis=1, keepdims=True)
     dlog_ref[...] = dlogp_ref[...] + dot(strict, ls, precision=highest).T + dd
-    wide = min(128, columns * heads)
-    per = wide // heads
-    for j in range(columns // per):
-        dlam_ref[:, j * wide : (j + 1) * wide] = (
-            dlamp_ref[pl.ds(j * per, per)].reshape(wide, TOK).T
-        )
+    log_out = pltpu.make_async_copy(dlog_ref, dlog_any, out_sem.at[3])
+    log_out.start()
+    for c in [through, lam_out, k_out, log_out] + parts:
+        c.wait()
 
 
 def body(
@@ -1022,9 +1088,18 @@
             f32(chips, 128),
         ),
         in_specs=[pl.BlockSpec(memory_space=pltpu.SMEM)]
-        + [pl.BlockSpec(memory_space=pltpu.HBM)] * 7,
-        out_specs=(vmem(),) * 8,
+        + [pl.BlockSpec(memory_space=pl.ANY)] * 7,
+        out_specs=(pl.BlockSpec(memory_space=pl.ANY),) * 8,
         scratch_shapes=[
+            pltpu.VMEM((TOK, heads * 64), F32),
+            pltpu.VMEM((64, TOK), F32),
+            pltpu.VMEM((64, TOK), F32),
+            pltpu.VMEM((columns, heads, TOK), F32),
+            pltpu.VMEM((heads, TOK), F32),
+            pltpu.VMEM((heads, TOK), F32),
+            pltpu.VMEM((chips, 64, 128), BF16),
+            pltpu.VMEM((chips, 128), F32),
+            dma((8,)),
             pltpu.VMEM((TOK, heads * 64), BF16),
             pltpu.VMEM((TOK, heads * 64), BF16),
             pltpu.VMEM((64, TOK), F32),
@@ -1054,6 +1129,7 @@
             pltpu.VMEM((chips, 8, 128), F32),
             pltpu.VMEM((chips, 8, 128), F32),
             pltpu.VMEM((8, 128), F32),
+            pltpu.VMEM((groups, 8, 128), F32),
             pltpu.VMEM((slots, ydim) + tile, F32),
             pltpu.VMEM((levels, 2, chips) + tile, F32),
             pltpu.VMEM((levels, chips) + tile, F32),
@@ -1064,13 +1140,11 @@
             pltpu.VMEM((chips, 8, 128), F32),
             pltpu.VMEM((chips, 8, 128), F32),
             pltpu.VMEM((nz,) + tile, F32),
-            pltpu.VMEM((groups,) + tile, F32),
-            pltpu.VMEM((groups, 8, 128), F32),
+            pltpu.VMEM((groups, 5, 8, 128), F32),
+            pltpu.VMEM((groups, 5, 8, 128), F32),
             pltpu.VMEM((8, 128), F32),
-            pltpu.VMEM((2 * chips,) + tile, F32),
-            pltpu.VMEM((chips, 2, 8, 128), F32),
-            pltpu.VMEM((2, chips, 2, 8, 128), F32),
-            pltpu.VMEM((2, chips) + tile, F32),
+            pltpu.VMEM((2 * chips, 5, 8, 128), F32),
+            pltpu.VMEM((2, chips, 5, 8, 128), F32),
             pltpu.VMEM((chips, 2) + tile, F32),
             dma((6,)),
             dma((2,)),
@@ -1093,10 +1167,8 @@
             dma((2,)),
             dma((groups,)),
             dma((groups,)),
-            dma((groups,)),
-            dma((groups,)),
-            dma((4,)),
-            dma((4,)),
+            dma((2,)),
+            dma((2,)),
         ],
         compiler_params=params(collective_id=0, has_side_effects=True),
         name="main",
@@ -1120,8 +1192,25 @@
             f32(heads, TOK),
             f32(TOK, columns * heads),
         ),
-        in_specs=[vmem()] * 10,
-        out_specs=(vmem(),) * 5,
+        in_specs=[pl.BlockSpec(memory_space=pl.ANY)] * 10,
+        out_specs=(pl.BlockSpec(memory_space=pl.ANY),) * 5,
+        scratch_shapes=[
+            pltpu.VMEM((TOK, heads * 64), BF16),
+            pltpu.VMEM((64, TOK), F32),
+            pltpu.VMEM((heads, TOK), F32),
+            pltpu.VMEM((chips, 64, 128), BF16),
+            pltpu.VMEM((chips, 128), F32),
+            pltpu.VMEM((TOK, heads * 64), F32),
+            pltpu.VMEM((64, TOK), F32),
+            pltpu.VMEM((heads, TOK), F32),
+            pltpu.VMEM((columns, heads, TOK), F32),
+            pltpu.VMEM((TOK, heads * 64), BF16),
+            pltpu.VMEM((64, TOK), F32),
+            pltpu.VMEM((heads, TOK), F32),
+            pltpu.VMEM((TOK, columns * heads), F32),
+            dma((9,)),
+            dma((6,)),
+        ],
         compiler_params=params(),
         name="end",
     )(values, kt, crow, low, dld, dv, dkt, dlogt, dqt, dlam)

time: 84.9 us -> 80.8 us (0.952)
  local copies, waits for them, and re-layouts: 7.09 us -> 0 us
  Pallas kernels: 76.7 us -> 80 us
    unnamed x18 -> x0, local copies, waits for them, and re-layouts: 7.09 us -> none
    pallas_call x1, Pallas kernels: 73.4 us -> 75.1 us  [body(): pl.pallas_call(partial(main_kernel, shards, groups), out_shape=(f32(TOK,...]
    pallas_call x1, Pallas kernels: 3.34 us -> 4.86 us  [body(): pl.pallas_call(end_kernel, out_shape=(jax.ShapeDtypeStruct((TOK, heads *...]
where the time goes in v4:
time: 80.8 us; the launch traced here: 80.6 us
  Pallas kernels  80 us (99%)
    pallas_call x1, Pallas kernels, body(): pl.pallas_call(partial(main_kernel, shards, groups), out_shape=(f32(TOK,...  75.1 us
    pallas_call x1, Pallas kernels, body(): pl.pallas_call(end_kernel, out_shape=(jax.ShapeDtypeStruct((TOK, heads *...  4.86 us

profile of v4, /device:TPU:1, one launch (start us, length us, event | category | flops | bytes accessed | tf_op | source)
XLA Modules:
  0.0 80.6 jit_solution(10480198731152658334)
XLA Ops:
  0.6 75.1 %main.1 = (f32[128,2048]{1,0:T(8,128)}, f32[64,128]{1,0:T(8,128)}, f32[64,128]{1,0:T(8,128)}, f32[8,32,128]{2,1,0:T(8,128)}, f32[32,128]{1,0:T(8,128)}, /*index=...) custom-call(s32[1,8]{1,0:T(1,128)} %ids_ref.1, bf16[128,2048]{1,0:T(8,128)(2,1)} %v_any.3, ...), custom_call_target="tpu_custom_call" | custom-call | tf_op jit(solution)/shard_map/main/pallas_call | solution.py:1078
  75.8 4.9 %end.1 = (bf16[128,2048]{1,0:T(8,128)(2,1)}, f32[64,128]{1,0:T(8,128)}, f32[64,128]{1,0:T(8,128)}, f32[32,128]{1,0:T(8,128)}, f32[128,256]{1,0:T(8,128)}) custom-call(bf16[128,2048]{1,0:T(8,128)(2,1)} %v_any.3, f32[64,128]{1,0:T(8,128)} %bitcast.9, f32[32,128]{1,0:T(8,128)} %get-tuple-element.18.crow_any, bf16[16,64,128]{2,1,0:T(8,128)(2,1)} %get-tuple-element.19.low_any, ...), custom_call_target="tpu_custom_call" | custom-call | tf_op jit(solution)/shard_map/end/pallas_call | solution.py:1186

commit v5 on v4

--- a/solution.py
+++ b/solution.py
@@ -85,19 +85,26 @@
 
 def routes_of(nb, nz, xdim, ydim):
     routes, slot = [], 0
+    ybits = log2(ydim)
+    split = nb + min(1, nz - 1)
     for lev in range(nb + nz):
-        ybits = log2(ydim)
-        rows_first = lev < ybits or lev == nb
-        first, second = (xdim, ydim) if rows_first else (ydim, xdim)
-        if lev < nb:
-            bit = lev if rows_first else lev - ybits
-            users = [s for s in range(second) if (s >> bit) & 1]
-            arrays = [[s for s in users if s >> (bit + 1) == a] for a in range(second >> (bit + 1))]
+        if lev == split:
+            ways = [(0, 2, True), (2, 4, False)]
         else:
-            users = list(range(second))
-            arrays = [users]
-        routes.append((rows_first, first, second, users, arrays, slot))
-        slot += len(arrays)
+            ways = [(0, 4, lev < ybits or nb <= lev < split)]
+        for t0, t1, rows_first in ways:
+            first, second = (xdim, ydim) if rows_first else (ydim, xdim)
+            if lev < nb:
+                bit = lev if rows_first else lev - ybits
+                users = [s for s in range(second) if (s >> bit) & 1]
+                arrays = [
+                    [s for s in users if s >> (bit + 1) == a] for a in range(second >> (bit + 1))
+                ]
+            else:
+                users = list(range(second))
+                arrays = [users]
+            routes.append((lev, slice(t0, t1), rows_first, first, second, users, arrays, slot))
+            slot += len(arrays)
     return routes
 
 
@@ -216,6 +223,7 @@
     per = wide // heads
 
     routes = routes_of(nb, nz, xdim, ydim)
+    ways = [[r for r in range(len(routes)) if routes[r][0] == lev] for lev in range(levels)]
 
     def shifted(i):
         return ((xpos + i // ydim) % xdim) * ydim + (ypos + i % ydim) % ydim
@@ -416,9 +424,8 @@
     loop(1, chips, send_scales)
     pk[chip] = pks[chip]
 
-    def where_on(lev):
-        rows_first, first, second, users, arrays, slot = routes[lev]
-        if rows_first:
+    def where_on(r):
+        if routes[r][2]:
             return xpos, ypos, lambda f, s: f * ydim + s
         return ypos, xpos, lambda f, s: s * ydim + f
 
@@ -433,13 +440,13 @@
         else:
             fn()
 
-    def first_phase(lev):
-        rows_first, first, second, users, arrays, slot = routes[lev]
-        fpos, spos, at = where_on(lev)
+    def first_phase(r):
+        lev, tiles, rows_first, first, second, users, arrays, slot = routes[r]
+        fpos, spos, at = where_on(r)
 
         def source(a, f):
             if lev >= nb:
-                return hz.at[lev - nb]
+                return hz.at[lev - nb, tiles]
             if rows_first:
                 return nd.at[offs[lev] + f * (ydim >> lev) + 2 * a, 0:4]
             return nd.at[offs[lev] + 2 * a, 0:4]
@@ -450,57 +457,59 @@
                 for a in range(len(arrays)):
                     remote(
                         source(a, f),
-                        ring.at[slot + a, fpos],
+                        ring.at[slot + a, fpos, tiles],
                         r_send.at[slot + a],
                         r_recv.at[slot + a],
                         (group, 2 * at(f, spos) + core),
                     ).start()
             for a in range(len(arrays)):
-                ring[slot + a, fpos] = source(a, fpos)[...]
+                ring[slot + a, fpos, tiles] = source(a, fpos)[...]
 
         if lev >= nb:
             go()
         else:
             when_level(lev, go)
 
-    def second_phase(lev):
-        rows_first, first, second, users, arrays, slot = routes[lev]
-        fpos, spos, at = where_on(lev)
+    def second_phase(r):
+        lev, tiles, rows_first, first, second, users, arrays, slot = routes[r]
+        fpos, spos, at = where_on(r)
 
         def go():
             if first > 1:
                 for a in range(len(arrays)):
-                    part = ring.at[slot + a, pl.ds(0, first - 1)]
+                    part = ring.at[slot + a, pl.ds(0, first - 1), tiles]
                     near(part, part, r_send.at[slot + a], r_recv.at[slot + a]).wait_recv()
             for a, readers in enumerate(arrays):
                 for s in readers:
-                    there = h.at[lev, core, pl.ds(spos * first, first)]
+                    there = h.at[lev, core, pl.ds(spos * first, first), tiles]
 
                     @pl.when(spos != s)
                     def _():
                         remote(
-                            ring.at[slot + a, pl.ds(0, first)],
+                            ring.at[slot + a, pl.ds(0, first), tiles],
                             there,
-                            h_send.at[lev],
-                            h_recv.at[lev],
+                            h_send.at[r],
+                            h_recv.at[r],
                             (group, 2 * at(fpos, s) + core),
                         ).start()
 
                     @pl.when(spos == s)
                     def _():
-                        there[...] = ring[slot + a, 0:first]
+                        there[...] = ring[slot + a, 0:first, tiles]
 
         when_level(lev, go)
 
     low = list(range(nb))
     high = list(range(nb, levels))
-    for lev in low:
-        first_phase(lev)
+    low_ways = [r for lev in low for r in ways[lev]]
+    high_ways = [r for lev in high for r in ways[lev]]
+    for r in low_ways:
+        first_phase(r)
 
     for p in range(pairs // 2, 3 * pairs // 4):
         inside(p)
-    for lev in low:
-        second_phase(lev)
+    for r in low_ways:
+        second_phase(r)
     for p in range(3 * pairs // 4, pairs):
         inside(p)
     results[0].start()
@@ -523,7 +532,8 @@
 
         @pl.when(bit_of(group, l) & (group % 2**l + 2**l == d))
         def _():
-            first_phase(nb + l)
+            for r in ways[nb + l]:
+                first_phase(r)
 
     q_low = qt.astype(BF16).astype(F32)
     q2 = jnp.concatenate([q_low, q_low], axis=1)
@@ -538,8 +548,8 @@
     dq_acc[...] = jnp.zeros(dq_acc.shape, F32)
     ids = [ids_ref[0, b] for b in range(1 + levels)]
 
-    def spot(lev, p):
-        if routes[lev][0]:
+    def spot(r, p):
+        if routes[r][2]:
             return (p % ydim) * xdim + p // ydim
         return p
 
@@ -553,8 +563,10 @@
                 scales.append(None)
             else:
                 scales.append(mate_scale * pk[p, b - 1 : b])
-                at = spot(b - 1, p)
-                held = jnp.concatenate([h[b - 1, 0, at], h[b - 1, 1, at]], axis=0)
+                held = jnp.concatenate(
+                    [h[b - 1, j, spot(r, p), routes[r][1]] for j in range(2) for r in ways[b - 1]],
+                    axis=0,
+                )
                 held = jnp.where(reads(b - 1), held.reshape(64, 128) * scales[-1], 0.0)
             helds.append(held.astype(BF16))
             ws.append(lam_t[ids[b], pl.ds(2 * p, 2), :] * gr2)
@@ -583,9 +595,10 @@
                 gn[p] = gi.reshape(2, 4, 8, 128)
             else:
                 gi = (gi * scales[i]).reshape(2, 4, 8, 128)
-                at = spot(b - 1, p)
-                g[b - 1, 0, at] = gi[0]
-                g[b - 1, 1, at] = gi[1]
+                for r in ways[b - 1]:
+                    tiles = routes[r][1]
+                    for j in range(2):
+                        g[b - 1, j, spot(r, p), tiles] = gi[j, tiles]
 
     def levels_pass(group_levels):
         def two(i):
@@ -602,21 +615,22 @@
         levels_pass([0])
         g0_copy.start()
 
-    for lev in high:
-        second_phase(lev)
+    for r in high_ways:
+        second_phase(r)
 
     def swap(lev):
         return near(g.at[lev, 1 - core], x.at[lev], x_send.at[lev], x_recv.at[lev])
 
     def fetch(levs):
         for lev in levs:
-            rows_first, first, second, users, arrays, slot = routes[lev]
 
             @pl.when(reads(lev))
             def _():
-                if second > 1:
-                    part = h.at[lev, core, pl.ds(0, (second - 1) * first)]
-                    near(part, part, h_send.at[lev], h_recv.at[lev]).wait_recv()
+                for r in ways[lev]:
+                    _, tiles, _, first, second, _, _, _ = routes[r]
+                    if second > 1:
+                        part = h.at[lev, core, pl.ds(0, (second - 1) * first), tiles]
+                        near(part, part, h_send.at[r], h_recv.at[r]).wait_recv()
                 ours = h.at[lev, core]
                 near(ours, ours, f_send.at[lev], f_recv.at[lev]).start()
 
@@ -634,9 +648,21 @@
             def _():
                 swap(lev).start()
 
+        def send_back(r):
+            lev, tiles, _, first, second, _, _, _ = routes[r]
+            fpos, spos, at = where_on(r)
+            for d in range(1, second):
+                s = (spos + d) % second
+                remote(
+                    st.at[lev, pl.ds(s * first, first), tiles],
+                    back.at[lev, spos, pl.ds(0, first), tiles],
+                    b_send.at[r],
+                    b_recv.at[r],
+                    (group, 2 * at(fpos, s) + core),
+                ).start()
+            back[lev, spos, 0:first, tiles] = st[lev, pl.ds(spos * first, first), tiles]
+
         for lev in levs:
-            rows_first, first, second, users, arrays, slot = routes[lev]
-            fpos, spos, at = where_on(lev)
 
             @pl.when(reads(lev))
             def _():
@@ -646,25 +672,17 @@
                     st[lev, c] = g[lev, core, c] + x[lev, c]
 
                 loop(0, chips, add)
-                for d in range(1, second):
-                    s = (spos + d) % second
-                    remote(
-                        st.at[lev, pl.ds(s * first, first)],
-                        back.at[lev, spos, pl.ds(0, first)],
-                        b_send.at[lev],
-                        b_recv.at[lev],
-                        (group, 2 * at(fpos, s) + core),
-                    ).start()
-                back[lev, spos, 0:first] = st[lev, pl.ds(spos * first, first)]
-
-    def gather_back(lev):
-        rows_first, first, second, users, arrays, slot = routes[lev]
-        fpos, spos, at = where_on(lev)
+                for r in ways[lev]:
+                    send_back(r)
+
+    def gather_back(r):
+        lev, tiles, rows_first, first, second, users, arrays, slot = routes[r]
+        fpos, spos, at = where_on(r)
 
         def arrived(count):
             if count:
-                part = back.at[lev, pl.ds(0, count), pl.ds(0, first)]
-                near(part, part, b_send.at[lev], b_recv.at[lev]).wait_recv()
+                part = back.at[lev, pl.ds(0, count), pl.ds(0, first), tiles]
+                near(part, part, b_send.at[r], b_recv.at[r]).wait_recv()
 
         def go():
             if lev >= nb:
@@ -681,28 +699,28 @@
 
             for a, readers in enumerate(arrays):
                 for f in range(first):
-                    total = back[lev, readers[0], f]
+                    total = back[lev, readers[0], f, tiles]
                     for s in readers[1:]:
-                        total = total + back[lev, s, f]
-                    q_sum[slot + a, f] = total
+                        total = total + back[lev, s, f, tiles]
+                    q_sum[slot + a, f, tiles] = total
                 for d in range(1, first):
                     f = (fpos + d) % first
                     remote(
-                        q_sum.at[slot + a, f],
-                        parts.at[slot + a, fpos],
+                        q_sum.at[slot + a, f, tiles],
+                        parts.at[slot + a, fpos, tiles],
                         q_send.at[slot + a],
                         q_recv.at[slot + a],
                         (group, 2 * at(f, spos) + core),
                     ).start()
-                parts[slot + a, fpos] = q_sum[slot + a, fpos]
+                parts[slot + a, fpos, tiles] = q_sum[slot + a, fpos, tiles]
 
         when_level(lev, go)
 
-    def parts_in(lev):
-        rows_first, first, second, users, arrays, slot = routes[lev]
+    def parts_in(r):
+        lev, tiles, rows_first, first, second, users, arrays, slot = routes[r]
         if first > 1:
             for a in range(len(arrays)):
-                part = parts.at[slot + a, pl.ds(0, first - 1)]
+                part = parts.at[slot + a, pl.ds(0, first - 1), tiles]
                 near(part, part, q_send.at[slot + a], q_recv.at[slot + a]).wait_recv()
 
     k_part = pk.at[pl.ds(0, chips - 1)]
@@ -719,8 +737,8 @@
     give_back(high)
     give_back(low)
 
-    r = rint[...]
-    rsum = jnp.broadcast_to(jnp.sum(r, axis=1, keepdims=True), (heads, TOK))
+    pulls = rint[...]
+    rsum = jnp.broadcast_to(jnp.sum(pulls, axis=1, keepdims=True), (heads, TOK))
     lane = iota((8, 128), 1)
     first_lane = jnp.where((sub == 0) & (lane == 0), 1.0, 0.0)
     mid_lane = jnp.where((sub == 0) & (lane == 64), 1.0, 0.0)
@@ -735,19 +753,22 @@
 
     loop(1, chips, send_sums)
     rr[chip] = rs[chip]
-    for lev in high:
-        gather_back(lev)
-
-    for lev in high:
-        first, slot = routes[lev][1], routes[lev][5]
+    for r in high_ways:
+        gather_back(r)
+
+    def sum_high(r):
+        lev, tiles, _, first, _, _, _, slot = routes[r]
 
         @pl.when(reads(lev))
         def _():
-            parts_in(lev)
-            total = parts[slot, 0]
+            parts_in(r)
+            total = parts[slot, 0, tiles]
             for f in range(1, first):
-                total = total + parts[slot, f]
-            u[lev - nb] = total
+                total = total + parts[slot, f, tiles]
+            u[lev - nb, tiles] = total
+
+    for r in high_ways:
+        sum_high(r)
 
     coef[...] = jnp.zeros((8, 128), F32)
     for d in reversed(range(1, groups)):
@@ -763,8 +784,8 @@
             ).start()
             coef[...] = coef[...] + before_far[d] * jnp.sum(grad * zb[group - d, 0:4], axis=0)
 
-    for lev in low:
-        gather_back(lev)
+    for r in low_ways:
+        gather_back(r)
 
     for p in range(columns):
         total = jnp.zeros((heads, TOK), F32)
@@ -773,7 +794,7 @@
         dlam_ref[p] = total
     even = jnp.where(core == 0, 1.0, 0.0)
     dlogt_ref[...] += (
-        dot(r + rnear[...], (row >= col).astype(F32), precision=highest) - even * rsum
+        dot(pulls + rnear[...], (row >= col).astype(F32), precision=highest) - even * rsum
     )
     dqi = (dq_acc[:, 0:128] + dq_acc[:, 128:256]).astype(BF16).astype(F32)
     dst = dsc[...]
@@ -782,9 +803,9 @@
     for i in range(1, 5):
         results[i].start()
 
-    for lev in low:
-        rows_first, first, second, users, arrays, slot = routes[lev]
-        parts_in(lev)
+    for r in low_ways:
+        lev, tiles, rows_first, first, second, users, arrays, slot = routes[r]
+        parts_in(r)
         for a in range(len(arrays)):
             if rows_first:
                 for f in range(first):
@@ -840,32 +861,40 @@
         dn[c, 4] = jnp.where(sub == 0, now, jnp.where(sub == 1, then, 0.0))
         now = then
 
-    def give(i):
+    def give(i, half):
         to = shifted(i)
         remote(
-            dn.at[to], ds.at[core, chip], o_sem.at[0], o_sem.at[1], (group, 2 * to + core)
+            dn.at[to],
+            ds.at[core, half, i % split_at],
+            o_sem.at[0],
+            o_sem.at[1 + half],
+            (group, 2 * to + core),
         ).start()
 
-    loop(1, chips, give)
-    ds[core, chip] = dn[chip]
-
-    part = ds.at[core, pl.ds(0, chips - 1)]
-    given = near(part, part, o_sem.at[0], o_sem.at[1])
-    given.wait_recv()
-    near(ds.at[core], ds.at[core], w_sem.at[0], w_sem.at[1]).start()
-
-    for lev in range(levels):
-        rows_first, first, second, users, arrays, slot = routes[lev]
+    split_at = chips // 2
+    loop(1, split_at, lambda i: give(i, 0))
+    loop(split_at, chips, lambda i: give(i, 1))
+    ds[core, 0, 0] = dn[chip, 0:5]
+    if split_at > 1:
+        part = ds.at[core, 0, pl.ds(0, split_at - 1)]
+        near(part, part, o_sem.at[0], o_sem.at[1]).wait_recv()
+    near(ds.at[core, 0], ds.at[core, 0], w_sem.at[0], w_sem.at[1]).start()
+    part = ds.at[core, 1]
+    near(part, part, o_sem.at[0], o_sem.at[2]).wait_recv()
+    near(part, part, w_sem.at[2], w_sem.at[3]).start()
+
+    def all_sent(r):
+        lev, tiles, rows_first, first, second, users, arrays, slot = routes[r]
 
         def out_of_ring(count):
             if count:
-                part = h.at[lev, core, pl.ds(0, count * first)]
-                near(part, part, h_send.at[lev], h_recv.at[lev]).wait_send()
+                part = h.at[lev, core, pl.ds(0, count * first), tiles]
+                near(part, part, h_send.at[r], h_recv.at[r]).wait_send()
 
         def sends():
             if first > 1:
                 for a in range(len(arrays)):
-                    part = ring.at[slot + a, pl.ds(0, first - 1)]
+                    part = ring.at[slot + a, pl.ds(0, first - 1), tiles]
                     near(part, part, r_send.at[slot + a], r_recv.at[slot + a]).wait_send()
                     near(part, part, q_send.at[slot + a], q_recv.at[slot + a]).wait_send()
             if lev >= nb:
@@ -883,12 +912,19 @@
         def _():
             if lev < nb:
                 out_of_ring(len(users) - 1)
+            if second > 1:
+                part = st.at[lev, pl.ds(0, (second - 1) * first), tiles]
+                near(part, part, b_send.at[r], b_recv.at[r]).wait_send()
+
+    for r in range(len(routes)):
+        all_sent(r)
+    for lev in range(levels):
+
+        @pl.when(reads(lev))
+        def _():
             ours = h.at[lev, core]
             near(ours, ours, f_send.at[lev], f_recv.at[lev]).wait_send()
             swap(lev).wait_send()
-            if second > 1:
-                part = st.at[lev, pl.ds(0, (second - 1) * first)]
-                near(part, part, b_send.at[lev], b_recv.at[lev]).wait_send()
 
     for d in range(1, groups):
 
@@ -917,26 +953,31 @@
         rest.wait_send()
         g0_copy.wait_recv()
 
-    given.wait_send()
-    theirs = ds.at[1 - core]
-    both = near(theirs, theirs, w_sem.at[0], w_sem.at[1])
-    both.wait_recv()
-    both.wait_send()
-    def finish(p):
+    part = dn.at[pl.ds(0, chips - 1)]
+    near(part, part, o_sem.at[0], o_sem.at[1]).wait_send()
+
+    def finish(half, i):
+        at = i + half * split_at
+        p = ((xpos + xdim - at // ydim) % xdim) * ydim + (ypos + ydim - at % ydim) % ydim
         scale = jnp.where(core == 0, sibd[p], jnp.ones((8, 128), F32))
         dld = jnp.zeros((8, 128), F32)
+        lows = []
         for j in range(2):
-            grad = ds[j, p, 0:4]
+            grad = ds[j, half, i, 0:4]
             dot_own = jnp.sum(own[p, j] * grad, axis=0)
-            dld = dld + jnp.where(sub == core, ds[j, p, 4], 0.0)
+            dld = dld + jnp.where(sub == core, ds[j, half, i, 4], 0.0)
             dld = dld - jnp.where(core == 0, 0.0, dot_own)
             extra = jnp.where(core == 0, g0[p, j], 0.0)
-            low_ref[p, 32 * j : 32 * (j + 1)] = (
-                (grad * scale[None] + extra).reshape(32, 128).astype(BF16)
-            )
+            lows.append(grad * scale[None] + extra)
+        low_ref[p] = jnp.concatenate(lows, axis=0).reshape(64, 128).astype(BF16)
         dld_ref[pl.ds(p, 1), :] = jnp.sum(dld, axis=0, keepdims=True)
 
-    loop(0, pairs, finish)
+    for half in range(2):
+        theirs = ds.at[1 - core, half]
+        both = near(theirs, theirs, w_sem.at[2 * half], w_sem.at[2 * half + 1])
+        both.wait_recv()
+        both.wait_send()
+        loop(0, split_at, partial(finish, half))
     results[6].start()
     results[7].start()
     for c in results:
@@ -1073,7 +1114,8 @@
     kt = state_input.T
     ydim = 2 ** ((nb + 1) // 2)
     routes = routes_of(nb, nz, chips // ydim, ydim)
-    slots = sum(len(route[4]) for route in routes)
+    slots = sum(len(route[6]) for route in routes)
+    count = len(routes)
 
     dv, dqt, dkt, dlam, dlogt, crow, low, dld = pl.pallas_call(
         partial(main_kernel, shards, groups),
@@ -1144,7 +1186,7 @@
             pltpu.VMEM((groups, 5, 8, 128), F32),
             pltpu.VMEM((8, 128), F32),
             pltpu.VMEM((2 * chips, 5, 8, 128), F32),
-            pltpu.VMEM((2, chips, 5, 8, 128), F32),
+            pltpu.VMEM((2, 2, chips // 2, 5, 8, 128), F32),
             pltpu.VMEM((chips, 2) + tile, F32),
             dma((6,)),
             dma((2,)),
@@ -1153,22 +1195,22 @@
             dma((2,)),
             dma((slots,)),
             dma((slots,)),
-            dma((levels,)),
-            dma((levels,)),
+            dma((count,)),
+            dma((count,)),
             dma((levels,)),
             dma((levels,)),
             dma((2,)),
             dma((levels,)),
             dma((levels,)),
-            dma((levels,)),
-            dma((levels,)),
+            dma((count,)),
+            dma((count,)),
             dma((slots,)),
             dma((slots,)),
             dma((2,)),
             dma((groups,)),
             dma((groups,)),
-            dma((2,)),
-            dma((2,)),
+            dma((3,)),
+            dma((4,)),
         ],
         compiler_params=params(collective_id=0, has_side_effects=True),
         name="main",

time: 80.8 us -> 79.7 us (0.986)
  Pallas kernels: 80 us -> 78.9 us
    pallas_call x1, Pallas kernels: 75.1 us -> 74 us  [body(): pl.pallas_call(partial(main_kernel, shards, groups), out_shape=(f32(TOK,...]
where the time goes in v5:
time: 79.7 us; the launch traced here: 79.5 us
  Pallas kernels  78.9 us (99%)
    pallas_call x1, Pallas kernels, body(): pl.pallas_call(partial(main_kernel, shards, groups), out_shape=(f32(TOK,...  74 us
    pallas_call x1, Pallas kernels, body(): pl.pallas_call(end_kernel, out_shape=(jax.ShapeDtypeStruct((TOK, heads *...  4.86 us

profile of v5, /device:TPU:1, one launch (start us, length us, event | category | flops | bytes accessed | tf_op | source)
XLA Modules:
  0.0 79.5 jit_solution(13137440470111120194)
XLA Ops:
  0.6 74.0 %main.1 = (f32[128,2048]{1,0:T(8,128)}, f32[64,128]{1,0:T(8,128)}, f32[64,128]{1,0:T(8,128)}, f32[8,32,128]{2,1,0:T(8,128)}, f32[32,128]{1,0:T(8,128)}, /*index=...) custom-call(s32[1,8]{1,0:T(1,128)} %ids_ref.1, bf16[128,2048]{1,0:T(8,128)(2,1)} %v_any.3, ...), custom_call_target="tpu_custom_call" | custom-call | tf_op jit(solution)/shard_map/main/pallas_call | solution.py:1120
  74.7 4.9 %end.1 = (bf16[128,2048]{1,0:T(8,128)(2,1)}, f32[64,128]{1,0:T(8,128)}, f32[64,128]{1,0:T(8,128)}, f32[32,128]{1,0:T(8,128)}, f32[128,256]{1,0:T(8,128)}) custom-call(bf16[128,2048]{1,0:T(8,128)(2,1)} %v_any.3, f32[64,128]{1,0:T(8,128)} %bitcast.9, f32[32,128]{1,0:T(8,128)} %get-tuple-element.18.crow_any, bf16[16,64,128]{2,1,0:T(8,128)(2,1)} %get-tuple-element.19.low_any, ...), custom_call_target="tpu_custom_call" | custom-call | tf_op jit(solution)/shard_map/end/pallas_call | solution.py:1228

commit v6 on v5

--- a/solution.py
+++ b/solution.py
@@ -120,22 +120,22 @@
     lam_any,
     fu_any,
     dv_any,
+    dkt_any,
     dqt_any,
-    dkt_any,
+    dlogt_any,
     dlam_any,
-    dlogt_any,
-    crow_any,
-    low_any,
-    dld_any,
+    dv_out,
+    dkt_ref,
+    dqt_ref,
+    dlogt_ref,
+    dlam_ref,
+    out_sem,
     dv_ref,
-    dqt_ref,
-    dkt_ref,
-    dlam_ref,
-    dlogt_ref,
     crow_ref,
-    low_ref,
     dld_ref,
-    out_sem,
+    tails,
+    decayed,
+    lrow,
     v_ref,
     do_ref,
     kt_ref,
@@ -251,14 +251,10 @@
         pltpu.make_async_copy(a, b, out_sem.at[i])
         for i, (a, b) in enumerate(
             [
-                (dv_ref, dv_any),
+                (dkt_ref, dkt_any),
                 (dqt_ref, dqt_any),
-                (dkt_ref, dkt_any),
+                (dlogt_ref, dlogt_any),
                 (dlam_ref, dlam_any),
-                (dlogt_ref, dlogt_any),
-                (crow_ref, crow_any),
-                (low_ref, low_any),
-                (dld_ref, dld_any),
             ]
         )
     ]
@@ -273,7 +269,6 @@
     loads[0].wait()
     crow = dot(ldt_ref[...], upto, precision=highest)
     crow_ref[...] = crow
-    results[5].start()
     last = jnp.broadcast_to(crow[:, TOK - 1 : TOK], (heads, TOK))
     tail = jnp.exp(last - crow)
     full = jnp.exp(last)
@@ -512,7 +507,6 @@
         second_phase(r)
     for p in range(3 * pairs // 4, pairs):
         inside(p)
-    results[0].start()
 
     coef[...] = jnp.ones((8, 128), F32)
     hz[...] = jnp.zeros(hz.shape, F32)
@@ -723,6 +717,16 @@
                 part = parts.at[slot + a, pl.ds(0, first - 1), tiles]
                 near(part, part, q_send.at[slot + a], q_recv.at[slot + a]).wait_recv()
 
+    tail_col = jnp.exp(ccol[TOK - 1 : TOK, :] - ccol)
+    for p in range(pairs):
+        tails[p] = jnp.where(
+            col < 64, tail_col[:, 2 * p : 2 * p + 1], tail_col[:, 2 * p + 1 : 2 * p + 2]
+        )
+        vp = v_ref[:, p * 128 : (p + 1) * 128].astype(F32)
+        decayed[p] = (tails[p] * vp).astype(BF16)
+    k_low = k.astype(BF16)
+    kt_low = kt.astype(BF16).astype(F32)
+
     k_part = pk.at[pl.ds(0, chips - 1)]
     scales_in = near(k_part, k_part, k_sem.at[0], k_sem.at[1])
     scales_in.wait_recv()
@@ -735,7 +739,6 @@
         levels_pass([b + 1 for b in high])
 
     give_back(high)
-    give_back(low)
 
     pulls = rint[...]
     rsum = jnp.broadcast_to(jnp.sum(pulls, axis=1, keepdims=True), (heads, TOK))
@@ -755,6 +758,7 @@
     rr[chip] = rs[chip]
     for r in high_ways:
         gather_back(r)
+    give_back(low)
 
     def sum_high(r):
         lev, tiles, _, first, _, _, _, slot = routes[r]
@@ -787,11 +791,15 @@
     for r in low_ways:
         gather_back(r)
 
-    for p in range(columns):
-        total = jnp.zeros((heads, TOK), F32)
-        for b in range(1 + levels):
-            total = total + jnp.where(ids[b] == p, glam[b], 0.0)
-        dlam_ref[p] = total
+    for j in range(columns // per):
+        slabs = []
+        for p in range(j * per, (j + 1) * per):
+            total = jnp.zeros((heads, TOK), F32)
+            for b in range(1 + levels):
+                total = total + jnp.where(ids[b] == p, glam[b], 0.0)
+            slabs.append(total)
+        dlam_ref[:, j * wide : (j + 1) * wide] = jnp.concatenate(slabs, axis=0).T
+    results[3].start()
     even = jnp.where(core == 0, 1.0, 0.0)
     dlogt_ref[...] += (
         dot(pulls + rnear[...], (row >= col).astype(F32), precision=highest) - even * rsum
@@ -800,8 +808,7 @@
     dst = dsc[...]
     dqt_ref[...] = dqi + dot(kt, dst, precision=highest)
     dkt_ref[...] = dot(dst, q, precision=highest).T
-    for i in range(1, 5):
-        results[i].start()
+    results[1].start()
 
     for r in low_ways:
         lev, tiles, rows_first, first, second, users, arrays, slot = routes[r]
@@ -956,146 +963,77 @@
     part = dn.at[pl.ds(0, chips - 1)]
     near(part, part, o_sem.at[0], o_sem.at[1]).wait_send()
 
-    def finish(half, i):
-        at = i + half * split_at
-        p = ((xpos + xdim - at // ydim) % xdim) * ydim + (ypos + ydim - at % ydim) % ydim
+    def finish(a, i):
+        at = a * ydim + i
+        half, slot = at // split_at, at % split_at
+        p = ((xpos + xdim - a) % xdim) * ydim + (ypos + ydim - i) % ydim
         scale = jnp.where(core == 0, sibd[p], jnp.ones((8, 128), F32))
         dld = jnp.zeros((8, 128), F32)
         lows = []
         for j in range(2):
-            grad = ds[j, half, i, 0:4]
+            grad = ds[j, half, slot, 0:4]
             dot_own = jnp.sum(own[p, j] * grad, axis=0)
-            dld = dld + jnp.where(sub == core, ds[j, half, i, 4], 0.0)
+            dld = dld + jnp.where(sub == core, ds[j, half, slot, 4], 0.0)
             dld = dld - jnp.where(core == 0, 0.0, dot_own)
             extra = jnp.where(core == 0, g0[p, j], 0.0)
             lows.append(grad * scale[None] + extra)
-        low_ref[p] = jnp.concatenate(lows, axis=0).reshape(64, 128).astype(BF16)
+        low = jnp.concatenate(lows, axis=0).reshape(64, 128).astype(BF16)
         dld_ref[pl.ds(p, 1), :] = jnp.sum(dld, axis=0, keepdims=True)
-
-    for half in range(2):
+        cols = pl.ds(pl.multiple_of(p * 128, 128), 128)
+        dv_out[:, cols] = (dv_ref[:, cols] + tails[p] * dot(k_low, low)).astype(BF16)
+        both_heads = jnp.concatenate([low * m0[0:64], low * m1[0:64]], axis=0)
+        dk = lax.dot_general(
+            both_heads, decayed[p], (((1,), (1,)), ((), ())), preferred_element_type=F32
+        )
+        dkt_ref[...] += dk[0:64] + dk[64:128]
+        lrow[pl.ds(2 * p, 1), :] = jnp.sum(kt_low * dk[0:64], axis=0, keepdims=True)
+        lrow[pl.ds(2 * p + 1, 1), :] = jnp.sum(kt_low * dk[64:128], axis=0, keepdims=True)
+
+    def half_in(half):
         theirs = ds.at[1 - core, half]
         both = near(theirs, theirs, w_sem.at[2 * half], w_sem.at[2 * half + 1])
         both.wait_recv()
         both.wait_send()
-        loop(0, split_at, partial(finish, half))
-    results[6].start()
-    results[7].start()
-    for c in results:
-        c.wait()
-
-
-def end_kernel(
-    v_any,
-    kt_any,
-    crow_any,
-    low_any,
-    dld_any,
-    dvp_any,
-    dkp_any,
-    dlogp_any,
-    dqp_any,
-    dlamp_any,
-    dv_any,
-    dk_any,
-    dq_any,
-    dlog_any,
-    dlam_any,
-    v_ref,
-    kt_ref,
-    crow_ref,
-    low_ref,
-    dld_ref,
-    dvp_ref,
-    dkp_ref,
-    dlogp_ref,
-    dlamp_ref,
-    dv_ref,
-    dk_ref,
-    dlog_ref,
-    dlam_ref,
-    in_sem,
-    out_sem,
-):
-    heads = crow_ref.shape[0]
-    pairs = heads // 2
-    columns = dlamp_ref.shape[0]
-    loads = [
-        pltpu.make_async_copy(a, b, in_sem.at[i])
-        for i, (a, b) in enumerate(
-            [
-                (dlamp_any, dlamp_ref),
-                (crow_any, crow_ref),
-                (kt_any, kt_ref),
-                (low_any, low_ref),
-                (v_any, v_ref),
-                (dvp_any, dvp_ref),
-                (dld_any, dld_ref),
-                (dkp_any, dkp_ref),
-                (dlogp_any, dlogp_ref),
-            ]
+
+    for a in range(xdim):
+        if a == 0:
+            half_in(0)
+        if a == xdim // 2:
+            half_in(1)
+        for i in range(ydim):
+            finish(a, i)
+        cols = pl.ds(pl.multiple_of(((xpos + xdim - a) % xdim) * ydim * 128, 128), ydim * 128)
+        results.append(
+            pltpu.make_async_copy(dv_out.at[:, cols], dv_any.at[:, cols], out_sem.at[4 + a])
         )
-    ]
-    for c in loads:
-        c.start()
-    through = pltpu.make_async_copy(dqp_any, dq_any, out_sem.at[0])
-    through.start()
-    row = iota((TOK, TOK), 0)
-    col = iota((TOK, TOK), 1)
-    left = col < 64
-    loads[0].wait()
-    wide = min(128, columns * heads)
-    per = wide // heads
-    for j in range(columns // per):
-        dlam_ref[:, j * wide : (j + 1) * wide] = (
-            dlamp_ref[pl.ds(j * per, per)].reshape(wide, TOK).T
-        )
-    lam_out = pltpu.make_async_copy(dlam_ref, dlam_any, out_sem.at[1])
-    lam_out.start()
-    loads[1].wait()
-    ccol = crow_ref[...].T
-    tail = jnp.exp(ccol[TOK - 1 : TOK, :] - ccol)
-    loads[2].wait()
-    k_low = kt_ref[...].T.astype(BF16)
-    dk = jnp.zeros((64, TOK), F32)
-    ls = jnp.zeros((TOK, heads), F32)
-    lane_row = iota((TOK, heads), 0)
-    lane_col = iota((TOK, heads), 1)
-    for i in range(3, 9):
-        loads[i].wait()
-    parts = []
-    for p in range(pairs):
-        sl = slice(p * 128, (p + 1) * 128)
-        pick = (lane_col == 2 * p + lane_row // 64).astype(F32)
-        low = low_ref[p]
-        scale = jnp.where(left, tail[:, 2 * p : 2 * p + 1], tail[:, 2 * p + 1 : 2 * p + 2])
-        vp = v_ref[:, sl].astype(F32)
-        dvs = scale * dot(k_low, low)
-        decayed = (scale * vp).astype(BF16)
-        dk += lax.dot_general(
-            low, decayed, (((1,), (1,)), ((), ())), preferred_element_type=F32
-        )
-        dv_ref[:, sl] = (dvp_ref[:, sl] + dvs).astype(BF16)
-        ls += dot((vp * dvs).astype(BF16), pick.astype(BF16))
-        if (p + 1) % (pairs // 2) == 0:
-            cols = pl.ds((p + 1 - pairs // 2) * 128, pairs // 2 * 128)
-            parts.append(
-                pltpu.make_async_copy(
-                    dv_ref.at[:, cols], dv_any.at[:, cols], out_sem.at[4 + len(parts)]
-                )
-            )
-            parts[-1].start()
-    dk_ref[...] = dkp_ref[...] + dk
-    k_out = pltpu.make_async_copy(dk_ref, dk_any, out_sem.at[2])
-    k_out.start()
-    strict = (row > col).astype(F32)
+        results[-1].start()
+    results[0].start()
     head = iota((heads, pairs), 0)
     rows = dot((iota((heads, pairs), 1) == head // 2).astype(F32), dld_ref[...], precision=highest)
     side = iota((heads, TOK), 1) // 64 == iota((heads, TOK), 0) % 2
     dd = jnp.sum(jnp.where(side, rows, 0.0), axis=1, keepdims=True)
-    dlog_ref[...] = dlogp_ref[...] + dot(strict, ls, precision=highest).T + dd
-    log_out = pltpu.make_async_copy(dlog_ref, dlog_any, out_sem.at[3])
-    log_out.start()
-    for c in [through, lam_out, k_out, log_out] + parts:
+    dlogt_ref[...] += dot(lrow[...], (row < col).astype(F32), precision=highest) + dd
+    results[2].start()
+    for c in results:
+        c.wait()
+
+
+def end_kernel(*refs):
+    n = (len(refs) - 1) // 2
+    sem = refs[-1]
+    copies = []
+    for i in range(n):
+        src, dst = refs[i], refs[n + i]
+        cuts = 4 if i == 0 else 1
+        step = src.shape[0] // cuts
+        for j in range(cuts):
+            part = pl.ds(j * step, step)
+            copies.append(
+                pltpu.make_async_copy(src.at[part], dst.at[part], sem.at[len(copies)])
+            )
+    for c in copies:
+        c.start()
+    for c in copies:
         c.wait()
 
 
@@ -1117,31 +1055,33 @@
     slots = sum(len(route[6]) for route in routes)
     count = len(routes)
 
-    dv, dqt, dkt, dlam, dlogt, crow, low, dld = pl.pallas_call(
+    shapes = (
+        jax.ShapeDtypeStruct((TOK, heads * 64), BF16),
+        f32(64, TOK),
+        f32(64, TOK),
+        f32(heads, TOK),
+        f32(TOK, columns * heads),
+    )
+    anywhere = pl.BlockSpec(memory_space=pl.ANY)
+    parts = pl.pallas_call(
         partial(main_kernel, shards, groups),
-        out_shape=(
-            f32(TOK, heads * 64),
-            f32(64, TOK),
-            f32(64, TOK),
-            f32(columns, heads, TOK),
-            f32(heads, TOK),
-            f32(heads, TOK),
-            jax.ShapeDtypeStruct((chips, 64, 128), BF16),
-            f32(chips, 128),
-        ),
+        out_shape=shapes,
         in_specs=[pl.BlockSpec(memory_space=pltpu.SMEM)]
-        + [pl.BlockSpec(memory_space=pl.ANY)] * 7,
-        out_specs=(pl.BlockSpec(memory_space=pl.ANY),) * 8,
+        + [anywhere] * 7,
+        out_specs=(anywhere,) * 5,
         scratch_shapes=[
-            pltpu.VMEM((TOK, heads * 64), F32),
+            pltpu.VMEM((TOK, heads * 64), BF16),
             pltpu.VMEM((64, TOK), F32),
             pltpu.VMEM((64, TOK), F32),
-            pltpu.VMEM((columns, heads, TOK), F32),
             pltpu.VMEM((heads, TOK), F32),
+            pltpu.VMEM((TOK, columns * heads), F32),
+            dma((4 + chips // ydim,)),
+            pltpu.VMEM((TOK, heads * 64), F32),
             pltpu.VMEM((heads, TOK), F32),
-            pltpu.VMEM((chips, 64, 128), BF16),
             pltpu.VMEM((chips, 128), F32),
-            dma((8,)),
+            pltpu.VMEM((chips, TOK, 128), F32),
+            pltpu.VMEM((chips, TOK, 128), BF16),
+            pltpu.VMEM((heads, TOK), F32),
             pltpu.VMEM((TOK, heads * 64), BF16),
             pltpu.VMEM((TOK, heads * 64), BF16),
             pltpu.VMEM((64, TOK), F32),
@@ -1227,35 +1167,13 @@
 
     dv, dk, dq, dlog, dlam = pl.pallas_call(
         end_kernel,
-        out_shape=(
-            jax.ShapeDtypeStruct((TOK, heads * 64), BF16),
-            f32(64, TOK),
-            f32(64, TOK),
-            f32(heads, TOK),
-            f32(TOK, columns * heads),
-        ),
-        in_specs=[pl.BlockSpec(memory_space=pl.ANY)] * 10,
-        out_specs=(pl.BlockSpec(memory_space=pl.ANY),) * 5,
-        scratch_shapes=[
-            pltpu.VMEM((TOK, heads * 64), BF16),
-            pltpu.VMEM((64, TOK), F32),
-            pltpu.VMEM((heads, TOK), F32),
-            pltpu.VMEM((chips, 64, 128), BF16),
-            pltpu.VMEM((chips, 128), F32),
-            pltpu.VMEM((TOK, heads * 64), F32),
-            pltpu.VMEM((64, TOK), F32),
-            pltpu.VMEM((heads, TOK), F32),
-            pltpu.VMEM((columns, heads, TOK), F32),
-            pltpu.VMEM((TOK, heads * 64), BF16),
-            pltpu.VMEM((64, TOK), F32),
-            pltpu.VMEM((heads, TOK), F32),
-            pltpu.VMEM((TOK, columns * heads), F32),
-            dma((9,)),
-            dma((6,)),
-        ],
+        out_shape=shapes,
+        in_specs=[anywhere] * 5,
+        out_specs=(anywhere,) * 5,
+        scratch_shapes=[dma((8,))],
         compiler_params=params(),
         name="end",
-    )(values, kt, crow, low, dld, dv, dkt, dlogt, dqt, dlam)
+    )(*parts)
     return (dv, dk.T, dq.T, dlog.T, dlam)
 
 

time: 79.7 us -> 98.1 us (1.23); the launches traced: 79.5 us -> 96.4 us
  Pallas kernels: 78.9 us -> 95.7 us
    pallas_call x2, Pallas kernels: 78.9 us -> 95.7 us  [the longest x1 72.2 us: body(): pl.pallas_call(partial(main_kernel, shards, groups), out_shape=shapes, in...]
where the time goes in v6:
time: 98.1 us; the launch traced here: 96.4 us
  Pallas kernels  95.7 us (98%)
    pallas_call x1, Pallas kernels, body(): pl.pallas_call(partial(main_kernel, shards, groups), out_shape=shapes, in...  72.2 us
    pallas_call x1, Pallas kernels, body(): pl.pallas_call(end_kernel, out_shape=shapes, in_specs=[anywhere] * 5, out...  23.5 us

profile of v6, /device:TPU:1, one launch (start us, length us, event | category | flops | bytes accessed | tf_op | source)
XLA Modules:
  0.0 96.4 jit_solution(14610608235614053324)
XLA Ops:
  0.6 72.2 %main.1 = (bf16[128,2048]{1,0:T(8,128)(2,1)}, f32[64,128]{1,0:T(8,128)}, f32[64,128]{1,0:T(8,128)}, f32[32,128]{1,0:T(8,128)}, f32[128,256]{1,0:T(8,128)}) custom-call(s32[1,8]{1,0:T(1,128)} %ids_ref.1, bf16[128,2048]{1,0:T(8,128)(2,1)} %v_any.1, bf16[128,2048]{1,0:T(8,128)(2,1)} %do_any.1, f32[64,128]{1,0:T(8,128)} %bitcast.8, f32[64,128]{1,0:T(8,128)} %bitcast.9, ...), custom_call_target="tpu_custom_call" | custom-call | tf_op jit(solution)/shard_map/main/pallas_call | solution.py:1066
  72.9 23.5 %end.1 = (bf16[128,2048]{1,0:T(8,128)(2,1)}, f32[64,128]{1,0:T(8,128)}, f32[64,128]{1,0:T(8,128)}, f32[32,128]{1,0:T(8,128)}, f32[128,256]{1,0:T(8,128)}) custom-call(bf16[128,2048]{1,0:T(8,128)(2,1)} %get-tuple-element.15.refs_0_, f32[64,128]{1,0:T(8,128)} %get-tuple-element.16.refs_1_, f32[64,128]{1,0:T(8,128)} %get-tuple-element.17.refs_2_, ...), custom_call_target="tpu_custom_call" | custom-call | tf_op jit(solution)/shard_map/end/pallas_call | solution.py:1168

commit v7 on v6

--- a/solution.py
+++ b/solution.py
@@ -1019,21 +1019,24 @@
 
 
 def end_kernel(*refs):
-    n = (len(refs) - 1) // 2
-    sem = refs[-1]
-    copies = []
+    n = (len(refs) - 2) // 3
+    in_sem, out_sem = refs[-2:]
+    loads, stores = [], []
     for i in range(n):
-        src, dst = refs[i], refs[n + i]
+        src, dst, held = refs[i], refs[n + i], refs[2 * n + i]
         cuts = 4 if i == 0 else 1
         step = src.shape[0] // cuts
         for j in range(cuts):
             part = pl.ds(j * step, step)
-            copies.append(
-                pltpu.make_async_copy(src.at[part], dst.at[part], sem.at[len(copies)])
-            )
-    for c in copies:
+            k = len(loads)
+            loads.append(pltpu.make_async_copy(src.at[part], held.at[part], in_sem.at[k]))
+            stores.append(pltpu.make_async_copy(held.at[part], dst.at[part], out_sem.at[k]))
+    for c in loads:
         c.start()
-    for c in copies:
+    for load, store in zip(loads, stores):
+        load.wait()
+        store.start()
+    for c in stores:
         c.wait()
 
 
@@ -1170,7 +1173,7 @@
         out_shape=shapes,
         in_specs=[anywhere] * 5,
         out_specs=(anywhere,) * 5,
-        scratch_shapes=[dma((8,))],
+        scratch_shapes=[pltpu.VMEM(x.shape, x.dtype) for x in shapes] + [dma((8,)), dma((8,))],
         compiler_params=params(),
         name="end",
     )(*parts)

time: 98.1 us -> 76.6 us (0.78)
  the two profiles are of different devices: /device:TPU:1 before, /device:TPU:225 now
where the time goes in v7:
time: 76.6 us; the launch traced here: 76.4 us
  Pallas kernels  75.7 us (99%)
    pallas_call x1, Pallas kernels, body(): pl.pallas_call(partial(main_kernel, shards, groups), out_shape=shapes, in...  73.7 us
    pallas_call x1, Pallas kernels, body(): pl.pallas_call(end_kernel, out_shape=shapes, in_specs=[anywhere] * 5, out...  2.01 us

profile of v7, /device:TPU:225, one launch (start us, length us, event | category | flops | bytes accessed | tf_op | source)
XLA Modules:
  0.0 76.4 jit_solution(5326429273237901506)
XLA Ops:
  0.6 73.7 %main.1 = (bf16[128,2048]{1,0:T(8,128)(2,1)}, f32[64,128]{1,0:T(8,128)}, f32[64,128]{1,0:T(8,128)}, f32[32,128]{1,0:T(8,128)}, f32[128,256]{1,0:T(8,128)}) custom-call(s32[1,8]{1,0:T(1,128)} %ids_ref.1, bf16[128,2048]{1,0:T(8,128)(2,1)} %v_any.1, bf16[128,2048]{1,0:T(8,128)(2,1)} %do_any.1, f32[64,128]{1,0:T(8,128)} %bitcast.8, f32[64,128]{1,0:T(8,128)} %bitcast.9, ...), custom_call_target="tpu_custom_call" | custom-call | tf_op jit(solution)/shard_map/main/pallas_call | solution.py:1069
  74.4 2.0 %end.1 = (bf16[128,2048]{1,0:T(8,128)(2,1)}, f32[64,128]{1,0:T(8,128)}, f32[64,128]{1,0:T(8,128)}, f32[32,128]{1,0:T(8,128)}, f32[128,256]{1,0:T(8,128)}) custom-call(bf16[128,2048]{1,0:T(8,128)(2,1)} %get-tuple-element.15.refs_0_, f32[64,128]{1,0:T(8,128)} %get-tuple-element.16.refs_1_, f32[64,128]{1,0:T(8,128)} %get-tuple-element.17.refs_2_, ...), custom_call_target="tpu_custom_call" | custom-call | tf_op jit(solution)/shard_map/end/pallas_call | solution.py:1171

commit v8 on v7

--- a/solution.py
+++ b/solution.py
@@ -186,6 +186,8 @@
     a_sem,
     z_send,
     z_recv,
+    zd_recv,
+    d_sem,
     k_sem,
     r_send,
     r_recv,
@@ -290,14 +292,28 @@
     swap_half = near(own.at[:, 1 - core], sib.at[:, 1 - core], s_sem.at[0], s_sem.at[1])
     swap_dec = near(dec, sibd, s_sem.at[2], s_sem.at[3])
     rest = near(own.at[:, core], sib.at[:, core], s_sem.at[4], s_sem.at[5])
+    swap_dec.start()
     swap_half.start()
-    swap_dec.start()
 
     @pl.when(core == 0)
     def _():
         rest.start()
 
     swap_dec.wait_recv()
+
+    def merge_decays(p):
+        blk[p, 4] = dec[p] * sibd[p]
+
+    loop(0, pairs, merge_decays)
+
+    def scatter_decays(i):
+        to = shifted(i)
+        remote(
+            blk.at[to, 4], nd.at[chip, 4], d_sem.at[0], d_sem.at[1], (group, 2 * to + core)
+        ).start()
+
+    loop(1, chips, scatter_decays)
+    nd[chip, 4] = blk[chip, 4]
     swap_half.wait_recv()
 
     def merge_cores(p):
@@ -307,18 +323,21 @@
         right = jnp.where(core == 0, b, a)
         drow = jnp.where(core == 0, sibd[p], dec[p])
         blk[p, 0:4] = drow[None] * left + right
-        blk[p, 4] = dec[p] * sibd[p]
 
     loop(0, pairs, merge_cores)
 
     def scatter(i):
         to = shifted(i)
         remote(
-            blk.at[to], nd.at[chip], a_sem.at[0], a_sem.at[1], (group, 2 * to + core)
+            blk.at[to, 0:4],
+            nd.at[chip, 0:4],
+            a_sem.at[0],
+            a_sem.at[1],
+            (group, 2 * to + core),
         ).start()
 
     loop(1, chips, scatter)
-    nd[chip] = blk[chip]
+    nd[chip, 0:4] = blk[chip, 0:4]
 
     loads[3].wait()
     loads[4].wait()
@@ -362,44 +381,21 @@
     for p in range(pairs // 2):
         inside(p)
 
-    part = nd.at[pl.ds(0, chips - 1)]
-    scattered = near(part, part, a_sem.at[0], a_sem.at[1])
-    scattered.wait_recv()
+    part = nd.at[pl.ds(0, chips - 1), 4]
+    decays_in = near(part, part, d_sem.at[0], d_sem.at[1])
+    decays_in.wait_recv()
     for b in range(1, nb + 1):
         for i in range(chips >> b):
             lo = offs[b - 1] + 2 * i
-            right = nd[lo + 1, 4]
-            nd[offs[b] + i, 0:4] = right[None] * nd[lo, 0:4] + nd[lo + 1, 0:4]
-            nd[offs[b] + i, 4] = right * nd[lo, 4]
-
-    def up(d):
-        return remote(
-            nd.at[top], zb.at[group], z_send.at[d], z_recv.at[group], (group + d, me)
-        )
-
-    def down(d):
-        return remote(
-            nd.at[top, 4], zb.at[group, 4], z_send.at[d], z_recv.at[group], (group - d, me)
-        )
-
-    for d in range(1, groups):
-
-        @pl.when(group + d < groups)
-        def _():
-            up(d).start()
-
-    for d in range(1, groups):
-
-        @pl.when(group - d >= 0)
-        def _():
-            remote(
-                nd.at[top, 4],
-                zb.at[group, 4],
-                z_send.at[groups + d],
-                z_recv.at[group],
-                (group - d, me),
-            ).start()
-
+            nd[offs[b] + i, 4] = nd[lo + 1, 4] * nd[lo, 4]
+
+    def spread_decay(d):
+        to = (group + d) % groups
+        remote(
+            nd.at[top, 4], zb.at[group, 4], z_send.at[groups], zd_recv.at[group], (to, me)
+        ).start()
+
+    loop(1, groups, spread_decay)
     sub = iota((8, 128), 0)
     for c in range(chips):
         pre = jnp.ones((8, 128), F32)
@@ -418,6 +414,26 @@
 
     loop(1, chips, send_scales)
     pk[chip] = pks[chip]
+
+    part = nd.at[pl.ds(0, chips - 1), 0:4]
+    scattered = near(part, part, a_sem.at[0], a_sem.at[1])
+    scattered.wait_recv()
+    for b in range(1, nb + 1):
+        for i in range(chips >> b):
+            lo = offs[b - 1] + 2 * i
+            right = nd[lo + 1, 4]
+            nd[offs[b] + i, 0:4] = right[None] * nd[lo, 0:4] + nd[lo + 1, 0:4]
+
+    def up(d):
+        return remote(
+            nd.at[top, 0:4], zb.at[group, 0:4], z_send.at[d], z_recv.at[group], (group + d, me)
+        )
+
+    for d in range(1, groups):
+
+        @pl.when(group + d < groups)
+        def _():
+            up(d).start()
 
     def where_on(r):
         if routes[r][2]:
@@ -515,7 +531,9 @@
 
         @pl.when(far >= 0)
         def _():
-            slot = zb.at[far]
+            slot = zb.at[far, 4]
+            near(slot, slot, z_send.at[0], zd_recv.at[far]).wait_recv()
+            slot = zb.at[far, 0:4]
             near(slot, slot, z_send.at[0], z_recv.at[far]).wait_recv()
             level = high_level(group, far, nz)
             hz[level] = hz[level] + coef[...][None] * zb[far, 0:4]
@@ -603,12 +621,6 @@
 
     g0_copy = near(gn, g0, g0_sem.at[0], g0_sem.at[1])
 
-    @pl.when(core == 1)
-    def _():
-        rest.wait_recv()
-        levels_pass([0])
-        g0_copy.start()
-
     for r in high_ways:
         second_phase(r)
 
@@ -716,6 +728,12 @@
             for a in range(len(arrays)):
                 part = parts.at[slot + a, pl.ds(0, first - 1), tiles]
                 near(part, part, q_send.at[slot + a], q_recv.at[slot + a]).wait_recv()
+
+    @pl.when(core == 1)
+    def _():
+        rest.wait_recv()
+        levels_pass([0])
+        g0_copy.start()
 
     tail_col = jnp.exp(ccol[TOK - 1 : TOK, :] - ccol)
     for p in range(pairs):
@@ -837,7 +855,7 @@
         @pl.when(group + d < groups)
         def _():
             far = zb.at[group + d, 4]
-            near(far, far, z_send.at[0], z_recv.at[group + d]).wait_recv()
+            near(far, far, z_send.at[0], zd_recv.at[group + d]).wait_recv()
             slot = zu.at[group + d]
             near(slot, slot, u_send.at[d], u_recv.at[group + d]).wait_recv()
             dn[top, 0:4] = dn[top, 0:4] + coef[...][None] * zu[group + d, 0:4]
@@ -868,27 +886,20 @@
         dn[c, 4] = jnp.where(sub == 0, now, jnp.where(sub == 1, then, 0.0))
         now = then
 
-    def give(i, half):
-        to = shifted(i)
+    def give(a, i):
+        to = shifted(a * ydim + i)
         remote(
-            dn.at[to],
-            ds.at[core, half, i % split_at],
-            o_sem.at[0],
-            o_sem.at[1 + half],
-            (group, 2 * to + core),
+            dn.at[to], ds.at[core, a, i], o_sem.at[0], o_sem.at[1 + a], (group, 2 * to + core)
         ).start()
 
-    split_at = chips // 2
-    loop(1, split_at, lambda i: give(i, 0))
-    loop(split_at, chips, lambda i: give(i, 1))
+    for a in range(xdim):
+        loop(0 if a else 1, ydim, partial(give, a))
     ds[core, 0, 0] = dn[chip, 0:5]
-    if split_at > 1:
-        part = ds.at[core, 0, pl.ds(0, split_at - 1)]
-        near(part, part, o_sem.at[0], o_sem.at[1]).wait_recv()
-    near(ds.at[core, 0], ds.at[core, 0], w_sem.at[0], w_sem.at[1]).start()
-    part = ds.at[core, 1]
-    near(part, part, o_sem.at[0], o_sem.at[2]).wait_recv()
-    near(part, part, w_sem.at[2], w_sem.at[3]).start()
+    for a in range(xdim):
+        part = ds.at[core, a] if a else ds.at[core, a, pl.ds(0, ydim - 1)]
+        near(part, part, o_sem.at[0], o_sem.at[1 + a]).wait_recv()
+        row_in = ds.at[core, a]
+        near(row_in, row_in, w_sem.at[0, a], w_sem.at[1, a]).start()
 
     def all_sent(r):
         lev, tiles, rows_first, first, second, users, arrays, slot = routes[r]
@@ -941,13 +952,14 @@
 
         @pl.when(group - d >= 0)
         def _():
-            line = nd.at[top, 4]
-            near(line, line, z_send.at[groups + d], z_recv.at[0]).wait_send()
             near(z_out.at[d], z_out.at[d], u_send.at[d], u_recv.at[0]).wait_send()
 
     swap_half.wait_send()
     swap_dec.wait_send()
     scattered.wait_send()
+    decays_in.wait_send()
+    lines = zb.at[pl.ds(0, groups - 1), 4]
+    near(lines, lines, z_send.at[groups], zd_recv.at[0]).wait_send()
     scales_in.wait_send()
     sums_in.wait_send()
 
@@ -964,16 +976,14 @@
     near(part, part, o_sem.at[0], o_sem.at[1]).wait_send()
 
     def finish(a, i):
-        at = a * ydim + i
-        half, slot = at // split_at, at % split_at
         p = ((xpos + xdim - a) % xdim) * ydim + (ypos + ydim - i) % ydim
         scale = jnp.where(core == 0, sibd[p], jnp.ones((8, 128), F32))
         dld = jnp.zeros((8, 128), F32)
         lows = []
         for j in range(2):
-            grad = ds[j, half, slot, 0:4]
+            grad = ds[j, a, i, 0:4]
             dot_own = jnp.sum(own[p, j] * grad, axis=0)
-            dld = dld + jnp.where(sub == core, ds[j, half, slot, 4], 0.0)
+            dld = dld + jnp.where(sub == core, ds[j, a, i, 4], 0.0)
             dld = dld - jnp.where(core == 0, 0.0, dot_own)
             extra = jnp.where(core == 0, g0[p, j], 0.0)
             lows.append(grad * scale[None] + extra)
@@ -989,17 +999,14 @@
         lrow[pl.ds(2 * p, 1), :] = jnp.sum(kt_low * dk[0:64], axis=0, keepdims=True)
         lrow[pl.ds(2 * p + 1, 1), :] = jnp.sum(kt_low * dk[64:128], axis=0, keepdims=True)
 
-    def half_in(half):
-        theirs = ds.at[1 - core, half]
-        both = near(theirs, theirs, w_sem.at[2 * half], w_sem.at[2 * half + 1])
+    def row_there(a):
+        theirs = ds.at[1 - core, a]
+        both = near(theirs, theirs, w_sem.at[0, a], w_sem.at[1, a])
         both.wait_recv()
         both.wait_send()
 
     for a in range(xdim):
-        if a == 0:
-            half_in(0)
-        if a == xdim // 2:
-            half_in(1)
+        row_there(a)
         for i in range(ydim):
             finish(a, i)
         cols = pl.ds(pl.multiple_of(((xpos + xdim - a) % xdim) * ydim * 128, 128), ydim * 128)
@@ -1129,12 +1136,14 @@
             pltpu.VMEM((groups, 5, 8, 128), F32),
             pltpu.VMEM((8, 128), F32),
             pltpu.VMEM((2 * chips, 5, 8, 128), F32),
-            pltpu.VMEM((2, 2, chips // 2, 5, 8, 128), F32),
+            pltpu.VMEM((2, chips // ydim, ydim, 5, 8, 128), F32),
             pltpu.VMEM((chips, 2) + tile, F32),
             dma((6,)),
             dma((2,)),
-            dma((2 * groups,)),
+            dma((groups + 1,)),
             dma((groups,)),
+            dma((groups,)),
+            dma((2,)),
             dma((2,)),
             dma((slots,)),
             dma((slots,)),
@@ -1152,8 +1161,8 @@
             dma((2,)),
             dma((groups,)),
             dma((groups,)),
-            dma((3,)),
-            dma((4,)),
+            dma((1 + chips // ydim,)),
+            dma((2, chips // ydim)),
         ],
         compiler_params=params(collective_id=0, has_side_effects=True),
         name="main",

time: 76.6 us -> 74.4 us (0.971)
  Pallas kernels: 75.7 us -> 73.6 us
    pallas_call x1, Pallas kernels: 73.7 us -> 71.6 us  [body(): pl.pallas_call(partial(main_kernel, shards, groups), out_shape=shapes, in...]
where the time goes in v8:
time: 74.4 us; the launch traced here: 74.2 us
  Pallas kernels  73.6 us (99%)
    pallas_call x1, Pallas kernels, body(): pl.pallas_call(partial(main_kernel, shards, groups), out_shape=shapes, in...  71.6 us
    pallas_call x1, Pallas kernels, body(): pl.pallas_call(end_kernel, out_shape=shapes, in_specs=[anywhere] * 5, out...  2.01 us

profile of v8, /device:TPU:225, one launch (start us, length us, event | category | flops | bytes accessed | tf_op | source)
XLA Modules:
  0.0 74.2 jit_solution(17970535479516542987)
XLA Ops:
  0.6 71.6 %main.1 = (bf16[128,2048]{1,0:T(8,128)(2,1)}, f32[64,128]{1,0:T(8,128)}, f32[64,128]{1,0:T(8,128)}, f32[32,128]{1,0:T(8,128)}, f32[128,256]{1,0:T(8,128)}) custom-call(s32[1,8]{1,0:T(1,128)} %ids_ref.1, bf16[128,2048]{1,0:T(8,128)(2,1)} %v_any.1, bf16[128,2048]{1,0:T(8,128)(2,1)} %do_any.1, f32[64,128]{1,0:T(8,128)} %bitcast.8, f32[64,128]{1,0:T(8,128)} %bitcast.9, ...), custom_call_target="tpu_custom_call" | custom-call | tf_op jit(solution)/shard_map/main/pallas_call | solution.py:1076
  72.2 2.0 %end.1 = (bf16[128,2048]{1,0:T(8,128)(2,1)}, f32[64,128]{1,0:T(8,128)}, f32[64,128]{1,0:T(8,128)}, f32[32,128]{1,0:T(8,128)}, f32[128,256]{1,0:T(8,128)}) custom-call(bf16[128,2048]{1,0:T(8,128)(2,1)} %get-tuple-element.15.refs_0_, f32[64,128]{1,0:T(8,128)} %get-tuple-element.16.refs_1_, f32[64,128]{1,0:T(8,128)} %get-tuple-element.17.refs_2_, ...), custom_call_target="tpu_custom_call" | custom-call | tf_op jit(solution)/shard_map/end/pallas_call | solution.py:1180

commit v9 on v8

--- a/solution.py
+++ b/solution.py
@@ -876,6 +876,18 @@
             dn[left, 0:4] = dn[left, 0:4] + nd[left + 1, 4][None] * parent
             dn[left + 1, 0:4] = parent
 
+    def give(tiles, a, i):
+        to = shifted(a * ydim + i)
+        remote(
+            dn.at[to, tiles],
+            ds.at[core, a, i, tiles],
+            o_sem.at[0],
+            o_sem.at[1 + a],
+            (group, 2 * to + core),
+        ).start()
+
+    for a in range(xdim):
+        loop(0 if a else 1, ydim, partial(give, slice(0, 4), a))
     t_part = rr.at[pl.ds(0, chips - 1)]
     sums_in = near(t_part, t_part, t_sem.at[0], t_sem.at[1])
     sums_in.wait_recv()
@@ -886,14 +898,8 @@
         dn[c, 4] = jnp.where(sub == 0, now, jnp.where(sub == 1, then, 0.0))
         now = then
 
-    def give(a, i):
-        to = shifted(a * ydim + i)
-        remote(
-            dn.at[to], ds.at[core, a, i], o_sem.at[0], o_sem.at[1 + a], (group, 2 * to + core)
-        ).start()
-
     for a in range(xdim):
-        loop(0 if a else 1, ydim, partial(give, a))
+        loop(0 if a else 1, ydim, partial(give, slice(4, 5), a))
     ds[core, 0, 0] = dn[chip, 0:5]
     for a in range(xdim):
         part = ds.at[core, a] if a else ds.at[core, a, pl.ds(0, ydim - 1)]

time: 74.4 us -> 74.5 us (level)
  the two profiles are of different devices: /device:TPU:225 before, /device:TPU:1 now
where the time goes in v9:
time: 74.5 us; the launch traced here: 73.4 us
  Pallas kernels  72.7 us (98%)
    pallas_call x1, Pallas kernels, body(): pl.pallas_call(partial(main_kernel, shards, groups), out_shape=shapes, in...  70.7 us
    pallas_call x1, Pallas kernels, body(): pl.pallas_call(end_kernel, out_shape=shapes, in_specs=[anywhere] * 5, out...  2.01 us

profile of v9, /device:TPU:1, one launch (start us, length us, event | category | flops | bytes accessed | tf_op | source)
XLA Modules:
  0.0 73.4 jit_solution(1108796435159001199)
XLA Ops:
  0.6 70.7 %main.1 = (bf16[128,2048]{1,0:T(8,128)(2,1)}, f32[64,128]{1,0:T(8,128)}, f32[64,128]{1,0:T(8,128)}, f32[32,128]{1,0:T(8,128)}, f32[128,256]{1,0:T(8,128)}) custom-call(s32[1,8]{1,0:T(1,128)} %ids_ref.1, bf16[128,2048]{1,0:T(8,128)(2,1)} %v_any.1, bf16[128,2048]{1,0:T(8,128)(2,1)} %do_any.1, f32[64,128]{1,0:T(8,128)} %bitcast.8, f32[64,128]{1,0:T(8,128)} %bitcast.9, ...), custom_call_target="tpu_custom_call" | custom-call | tf_op jit(solution)/shard_map/main/pallas_call | solution.py:1082
  71.4 2.0 %end.1 = (bf16[128,2048]{1,0:T(8,128)(2,1)}, f32[64,128]{1,0:T(8,128)}, f32[64,128]{1,0:T(8,128)}, f32[32,128]{1,0:T(8,128)}, f32[128,256]{1,0:T(8,128)}) custom-call(bf16[128,2048]{1,0:T(8,128)(2,1)} %get-tuple-element.15.refs_0_, f32[64,128]{1,0:T(8,128)} %get-tuple-element.16.refs_1_, f32[64,128]{1,0:T(8,128)} %get-tuple-element.17.refs_2_, ...), custom_call_target="tpu_custom_call" | custom-call | tf_op jit(solution)/shard_map/end/pallas_call | solution.py:1186
